TPU v7x, 32 devices: a whole 2x2x4 slice. The times are simulated.
32 devices in a mesh: ctx: 8 (over y, x, core), tp: 4 (over z).
Axes of the slice: x: 2, y: 2, z: 4, core: 2. Of those that a mesh axis runs over, the one named last changes fastest.
Arguments:
- tokens: bfloat16 [4096, 2304], P(('ctx', 'tp')), may hold values from -8 to 8
- cotangent: bfloat16 [4096, 2304], P(('ctx', 'tp')), may hold values from -6 to 6
- w_query: bfloat16 [2304, 2048], P('ctx', 'tp'), may hold values from -0.125 to 0.125
- key_projection: bfloat16 [2304, 1024], P('ctx', 'tp'), may hold values from -0.125 to 0.125
- value_projection: bfloat16 [2304, 1024], P('ctx', 'tp'), may hold values from -0.125 to 0.125
- w_out: bfloat16 [2048, 2304], P('tp', 'ctx'), may hold values from -0.125 to 0.125
- w_gate: bfloat16 [2304, 9216], P('ctx', 'tp'), may hold values from -0.125 to 0.125
- w_up: bfloat16 [2304, 9216], P('ctx', 'tp'), may hold values from -0.125 to 0.125
- w_down: bfloat16 [9216, 2304], P('tp', 'ctx'), may hold values from -0.0625 to 0.0625
- norm_gains: bfloat16 [4, 2304], P(None, 'ctx'), may hold values from -0.5 to 0.5
- block_mask: int32 [32, 32], replicated, may hold values from 0 to 1, as said below
- block_seq: int32 [32], replicated, may hold values from 0 to 0, as said below
- block_place: int32 [32], replicated, may hold values from 0 to 31, as said below
Outputs:
- mixed_out: bfloat16 [4096, 2304], P(('ctx', 'tp'))
- grad_tokens: float32 [4096, 2304], P(('ctx', 'tp'))
- grad_query: float32 [2304, 2048], P('ctx', 'tp')
- grad_key: float32 [2304, 1024], P('ctx', 'tp')
- grad_value: float32 [2304, 1024], P('ctx', 'tp')
- grad_out: float32 [2048, 2304], P('tp', 'ctx')
- grad_gate: float32 [2304, 9216], P('ctx', 'tp')
- grad_up: float32 [2304, 9216], P('ctx', 'tp')
- grad_down: float32 [9216, 2304], P('tp', 'ctx')
- grad_gains: float32 [4, 2304], P('tp', 'ctx')
Inputs may be any that keep to these rules, and one draw needn't show every extreme that they name: block_mask[i, i] = 1 and block_mask[i, j] = 0 for j > i. `block_seq`: blocks 2m and 2m + 1 belong to one sequence; each sequence owns 32 blocks. `block_place`: blocks 2m and 2m + 1 hold places p and 31 - p; within a sequence each place occurs once.
All inputs are finite; a program needn't handle non-finite values.
Results may differ from a plain program's by a relative error of at most 0.015.
Values may be sent and summed in bfloat16 or wider, within the bound.
No kernel may reach another device: no remote copies, remote signals or barrier semaphores. Data moves between devices by JAX's collectives and lax.ppermute only.
A program may use at most 192 MiB of HBM per device.

v0:
```python
import jax
import jax.numpy as jnp
from jax import lax
from jax.sharding import PartitionSpec as P

QUERY_HEADS = 8
KEY_VALUE_HEADS = 4
HEAD_SIZE = 256
SCORE_SOFT_LIMIT = 50
BLOCK_TOKENS = 128


EPSILON = 1e-06


def rms_norm(inputs, gain_row):
    inv_rms = lax.rsqrt(jnp.mean(inputs * inputs, axis=-1, keepdims=True) + EPSILON)
    return inputs * inv_rms * (1.0 + gain_row)


def matmul_fwd(first_op, second_op):
    return jnp.dot(first_op, second_op, preferred_element_type=jnp.float32)


def matmul_back(first_op, second_op):
    return jnp.einsum("ra,ba->rb", first_op, second_op, preferred_element_type=jnp.float32)


def contract_rows(first_op, second_op):
    return jnp.einsum("ra,rb->ab", first_op, second_op, preferred_element_type=jnp.float32)


def gelu_gate(gate_pre, up_pre):
    return jax.nn.gelu(gate_pre, approximate=True) * up_pre


def on_device(
    tokens,
    cotangent,
    w_query,
    key_projection,
    value_projection,
    w_out,
    w_gate,
    w_up,
    w_down,
    norm_gains,
    block_mask,
    block_seq,
    block_place,
):
    weight_set = (
        w_query,
        key_projection,
        value_projection,
        w_out,
        w_gate,
        w_up,
        w_down,
        norm_gains,
    )
    full_set = (
        lax.all_gather(weight_set[0], "ctx", axis=0, tiled=True),
        lax.all_gather(weight_set[1], "ctx", axis=0, tiled=True),
        lax.all_gather(weight_set[2], "ctx", axis=0, tiled=True),
        lax.all_gather(weight_set[3], "ctx", axis=1, tiled=True),
        lax.all_gather(weight_set[4], "ctx", axis=0, tiled=True),
        lax.all_gather(weight_set[5], "ctx", axis=0, tiled=True),
        lax.all_gather(weight_set[6], "ctx", axis=1, tiled=True),
        lax.all_gather(weight_set[7], "ctx", axis=1, tiled=True),
    )
    gain_set = full_set[7].astype(jnp.float32)
    group_rows = lax.all_gather(tokens, "tp", axis=0, tiled=True)
    count_of_rows = group_rows.shape[0]
    query_block_rows = count_of_rows // BLOCK_TOKENS
    heads_kv = full_set[1].shape[1] // HEAD_SIZE
    heads_per_group = QUERY_HEADS // KEY_VALUE_HEADS
    scale_query = HEAD_SIZE ** (-0.5)
    group_float = group_rows.astype(jnp.float32)
    normed = rms_norm(group_float, gain_set[0]).astype(jnp.bfloat16)
    query_matrix = (matmul_fwd(normed, full_set[0]) * scale_query).astype(jnp.bfloat16)
    query_matrix = query_matrix.reshape(count_of_rows, heads_kv, heads_per_group, HEAD_SIZE)
    projected_keys = matmul_fwd(normed, full_set[1]).astype(jnp.bfloat16)
    projected_values = matmul_fwd(normed, full_set[2]).astype(jnp.bfloat16)
    first_block = lax.axis_index("ctx") * query_block_rows
    query_seq = lax.dynamic_slice_in_dim(block_seq, first_block, query_block_rows)
    query_place = lax.dynamic_slice_in_dim(block_place, first_block, query_block_rows)
    place_ids = jnp.arange(block_mask.shape[0], dtype=jnp.int32)
    query_pick = (query_place[:, None] == place_ids[None, :]).astype(jnp.float32)
    mask_rows = jnp.dot(query_pick, block_mask.astype(jnp.float32))

    def tile(key_block, offset):
        key_count = key_block.shape[0]
        key_blocks = key_count // BLOCK_TOKENS
        key_seq = lax.dynamic_slice_in_dim(block_seq, offset // BLOCK_TOKENS, key_blocks)
        key_place = lax.dynamic_slice_in_dim(block_place, offset // BLOCK_TOKENS, key_blocks)
        picked = (key_place[:, None] == place_ids[None, :]).astype(jnp.float32)
        hits = jnp.einsum("qp,kp->qk", mask_rows, picked)
        permitted_pairs = (hits > 0.5) & (query_seq[:, None] == key_seq[None, :])
        scores = jnp.einsum(
            "qcgd,kcd->cgqk",
            query_matrix,
            key_block.reshape(key_count, heads_kv, HEAD_SIZE),
            preferred_element_type=jnp.float32,
        )
        incoming_gradient = jnp.tanh(scores / SCORE_SOFT_LIMIT)
        widened_heads = jnp.exp(SCORE_SOFT_LIMIT * incoming_gradient).reshape(
            heads_kv, heads_per_group, query_block_rows, BLOCK_TOKENS, key_blocks, BLOCK_TOKENS
        )
        widened_heads = jnp.where(permitted_pairs[:, None, :, None], widened_heads, 0.0).reshape(
            heads_kv, heads_per_group, count_of_rows, key_count
        )
        return (incoming_gradient, widened_heads)

    def over_blocks(step_fn, running, shard_pair):
        block_total = shard_pair[0].shape[0] // count_of_rows
        key_split = shard_pair[0].reshape(block_total, count_of_rows, shard_pair[0].shape[1])
        value_split = shard_pair[1].reshape(block_total, count_of_rows, shard_pair[1].shape[1])
        offsets = jnp.arange(block_total, dtype=jnp.int32) * count_of_rows

        def advance(state_now, members):
            return (step_fn(state_now, members[0], members[1], members[2]), None)

        running, _ = lax.scan(advance, running, (key_split, value_split, offsets))
        return running

    def forward_step(running, key_block, value_block, offset):
        accum, totals = running
        incoming_gradient, widened_heads = tile(key_block, offset)
        totals = totals + jnp.sum(widened_heads, axis=-1)
        value_heads = value_block.reshape(value_block.shape[0], heads_kv, HEAD_SIZE)
        accum = accum + jnp.einsum(
            "cgqk,kcd->cgqd",
            widened_heads.astype(jnp.bfloat16),
            value_heads,
            preferred_element_type=jnp.float32,
        )
        return (accum, totals)

    accum_zero = jnp.zeros((heads_kv, heads_per_group, count_of_rows, HEAD_SIZE), jnp.float32)
    totals_zero = jnp.zeros((heads_kv, heads_per_group, count_of_rows), jnp.float32)
    accum, totals = over_blocks(
        forward_step,
        (accum_zero, totals_zero),
        (
            lax.all_gather(projected_keys, "ctx", axis=0, tiled=True),
            lax.all_gather(projected_values, "ctx", axis=0, tiled=True),
        ),
    )
    outcome = accum / totals[..., None]
    attended = (
        jnp.transpose(outcome, (2, 0, 1, 3))
        .reshape(count_of_rows, heads_kv * heads_per_group * HEAD_SIZE)
        .astype(jnp.bfloat16)
    )
    branch = lax.psum_scatter(
        matmul_fwd(attended, full_set[3]), "tp", scatter_dimension=0, tiled=True
    )
    token_float = tokens.astype(jnp.float32)
    post_attn, pull_attn = jax.vjp(rms_norm, branch, gain_set[1])
    hidden = token_float + post_attn
    pre_ffw, pull_pre = jax.vjp(rms_norm, hidden, gain_set[2])
    inner = pre_ffw.astype(jnp.bfloat16)
    inner_rows = lax.all_gather(inner, "tp", axis=0, tiled=True)
    gate_pre = matmul_fwd(inner_rows, full_set[4])
    up_pre = matmul_fwd(inner_rows, full_set[5])
    mid_value, pull_mid = jax.vjp(gelu_gate, gate_pre, up_pre)
    mid_rows = mid_value.astype(jnp.bfloat16)
    feed_sum = lax.psum_scatter(
        matmul_fwd(mid_rows, full_set[6]), "tp", scatter_dimension=0, tiled=True
    )
    post_ffw, pull_post = jax.vjp(rms_norm, feed_sum, gain_set[3])
    mixed_out = (hidden + post_ffw).astype(jnp.bfloat16)
    cot_float = cotangent.astype(jnp.float32)
    dfeed, gain_grad_four = pull_post(cot_float)
    feed_rows = lax.all_gather(dfeed.astype(jnp.bfloat16), "tp", axis=0, tiled=True)
    grad_down = contract_rows(mid_rows, feed_rows)
    dmid = matmul_back(feed_rows, full_set[6])
    dgate, dup = pull_mid(dmid)
    dgate_low = dgate.astype(jnp.bfloat16)
    dup_low = dup.astype(jnp.bfloat16)
    grad_gate = contract_rows(inner_rows, dgate_low)
    grad_up = contract_rows(inner_rows, dup_low)
    dinner_part = matmul_back(dgate_low, full_set[4]) + matmul_back(dup_low, full_set[5])
    dinner = lax.psum_scatter(dinner_part, "tp", scatter_dimension=0, tiled=True)
    dhidden_norm, gain_grad_three = pull_pre(dinner)
    dhidden = cot_float + dhidden_norm
    dbranch, gain_grad_two = pull_attn(dhidden)
    branch_rows = lax.all_gather(dbranch.astype(jnp.bfloat16), "tp", axis=0, tiled=True)
    grad_out = contract_rows(attended, branch_rows)
    dattended = matmul_back(branch_rows, full_set[3]).astype(jnp.bfloat16)
    dout = lax.optimization_barrier(dattended).astype(jnp.float32)
    dout = jnp.transpose(
        dout.reshape(count_of_rows, heads_kv, heads_per_group, HEAD_SIZE), (1, 2, 0, 3)
    )
    scaled = (dout / totals[..., None]).astype(jnp.bfloat16)
    dtotals = -jnp.sum(dout * accum, axis=-1) / (totals * totals)

    def backward_step(running, key_block, value_block, offset):
        dquery_sum, dkeys_all, dvalues_all = running
        key_count = key_block.shape[0]
        incoming_gradient, widened_heads = tile(key_block, offset)
        key_heads = key_block.reshape(key_count, heads_kv, HEAD_SIZE)
        value_heads = value_block.reshape(key_count, heads_kv, HEAD_SIZE)
        dprob = jnp.einsum(
            "cgqd,kcd->cgqk", scaled, value_heads, preferred_element_type=jnp.float32
        )
        dscores = (
            widened_heads
            * (dprob + dtotals[..., None])
            * (1.0 - incoming_gradient * incoming_gradient)
        ).astype(jnp.bfloat16)
        dquery_sum = dquery_sum + jnp.einsum(
            "cgqk,kcd->qcgd", dscores, key_heads, preferred_element_type=jnp.float32
        )
        key_part = jnp.einsum(
            "cgqk,qcgd->kcd", dscores, query_matrix, preferred_element_type=jnp.float32
        ).reshape(key_count, heads_kv * HEAD_SIZE)
        value_part = jnp.einsum(
            "cgqk,cgqd->kcd",
            widened_heads.astype(jnp.bfloat16),
            scaled,
            preferred_element_type=jnp.float32,
        ).reshape(key_count, heads_kv * HEAD_SIZE)
        old_keys = lax.dynamic_slice_in_dim(dkeys_all, offset, key_count, 0)
        old_values = lax.dynamic_slice_in_dim(dvalues_all, offset, key_count, 0)
        dkeys_all = lax.dynamic_update_slice_in_dim(dkeys_all, old_keys + key_part, offset, 0)
        dvalues_all = lax.dynamic_update_slice_in_dim(
            dvalues_all, old_values + value_part, offset, 0
        )
        return (dquery_sum, dkeys_all, dvalues_all)

    all_rows = count_of_rows * lax.axis_size("ctx")
    dquery_zero = jnp.zeros((count_of_rows, heads_kv, heads_per_group, HEAD_SIZE), jnp.float32)
    dkv_zero = jnp.zeros((all_rows, heads_kv * HEAD_SIZE), jnp.float32)
    dquery_sum, dkeys_all, dvalues_all = over_blocks(
        backward_step,
        (dquery_zero, dkv_zero, dkv_zero),
        (
            lax.all_gather(projected_keys, "ctx", axis=0, tiled=True),
            lax.all_gather(projected_values, "ctx", axis=0, tiled=True),
        ),
    )
    dkeys, dvalues = (
        lax.psum_scatter(dkeys_all, "ctx", scatter_dimension=0, tiled=True),
        lax.psum_scatter(dvalues_all, "ctx", scatter_dimension=0, tiled=True),
    )
    dkeys_low = dkeys.astype(jnp.bfloat16)
    dvalues_low = dvalues.astype(jnp.bfloat16)
    dquery_low = dquery_sum.reshape(count_of_rows, heads_kv * heads_per_group * HEAD_SIZE).astype(
        jnp.bfloat16
    )
    dquery_scaled = dquery_low * jnp.asarray(scale_query, jnp.bfloat16)
    grad_query = contract_rows(normed, dquery_scaled)
    grad_key = contract_rows(normed, dkeys_low)
    grad_value = contract_rows(normed, dvalues_low)
    dnormed_part = (
        matmul_back(dquery_scaled, full_set[0])
        + matmul_back(dkeys_low, full_set[1])
        + matmul_back(dvalues_low, full_set[2])
    )
    unit_rows = group_float * lax.rsqrt(
        jnp.mean(group_float * group_float, axis=-1, keepdims=True) + EPSILON
    )
    gain_grad_one = jnp.sum(dnormed_part * unit_rows, axis=0)
    gain_terms = jnp.stack([gain_grad_one, gain_grad_two, gain_grad_three, gain_grad_four])
    dnormed, gain_piece = (
        lax.psum_scatter(dnormed_part, "tp", scatter_dimension=0, tiled=True),
        lax.psum_scatter(gain_terms, "tp", scatter_dimension=0, tiled=True),
    )
    pre_attn, pull_in = jax.vjp(rms_norm, token_float, gain_set[0])
    dtoken_norm, unused_gain = pull_in(dnormed)
    grad_tokens = dhidden + dtoken_norm
    grads = (
        lax.psum_scatter(grad_query, "ctx", scatter_dimension=0, tiled=True),
        lax.psum_scatter(grad_key, "ctx", scatter_dimension=0, tiled=True),
        lax.psum_scatter(grad_value, "ctx", scatter_dimension=0, tiled=True),
        lax.psum_scatter(grad_out, "ctx", scatter_dimension=1, tiled=True),
        lax.psum_scatter(grad_gate, "ctx", scatter_dimension=0, tiled=True),
        lax.psum_scatter(grad_up, "ctx", scatter_dimension=0, tiled=True),
        lax.psum_scatter(grad_down, "ctx", scatter_dimension=1, tiled=True),
        lax.psum_scatter(gain_piece, "ctx", scatter_dimension=1, tiled=True),
    )
    return (
        mixed_out,
        grad_tokens,
        grads[0],
        grads[1],
        grads[2],
        grads[3],
        grads[4],
        grads[5],
        grads[6],
        grads[7],
    )


def solution(mesh):
    in_specs = (
        P(("ctx", "tp"), None),
        P(("ctx", "tp"), None),
        P("ctx", "tp"),
        P("ctx", "tp"),
        P("ctx", "tp"),
        P("tp", "ctx"),
        P("ctx", "tp"),
        P("ctx", "tp"),
        P("tp", "ctx"),
        P(None, "ctx"),
        P(),
        P(),
        P(),
    )
    out_specs = (
        P(("ctx", "tp"), None),
        P(("ctx", "tp"), None),
        P("ctx", "tp"),
        P("ctx", "tp"),
        P("ctx", "tp"),
        P("tp", "ctx"),
        P("ctx", "tp"),
        P("ctx", "tp"),
        P("tp", "ctx"),
        P("tp", "ctx"),
    )
    return jax.shard_map(
        on_device, mesh=mesh, in_specs=in_specs, out_specs=out_specs, check_vma=False
    )
```

profile of v0, /device:TPU:0, one launch (start us, length us, event | category | flops | bytes accessed | tf_op | source)
XLA Modules:
  0.0 2019.1 jit_solution(62295609188691258)
XLA Ops:
  10.0 10.6 all-gather
  20.9 41.9 %all-gather.15.cloned.1.call-done = bf16[512,2304]{1,0:T(8,128)(2,1)} async-done(((bf16[128,2304]{1,0:T(8,128)(2,1)}), bf16[512,2304]{1,0:T(8,128)(2,1)}) %all-gather.15.cloned.1.call-update) | async-done | bytes 2359312 | tf_op jit(solution)/shard_map/all_gather | solution.py:73
  65.2 22.4 %all-gather.17.cloned.1.call-done = bf16[2304,256]{1,0:T(8,128)(2,1)} async-done(((bf16[288,256]{1,0:T(8,128)(2,1)}), bf16[2304,256]{1,0:T(8,128)(2,1)}) %all-gather.17.cloned.1.call-update) | async-done | bytes 1179664 | tf_op jit(solution)/shard_map/all_gather | solution.py:64
  90.5 23.1 %all-gather.23.cloned.1.call-done = bf16[2304,256]{1,0:T(8,128)(2,1)} async-done(((bf16[288,256]{1,0:T(8,128)(2,1)}), bf16[2304,256]{1,0:T(8,128)(2,1)}) %all-gather.23.cloned.1.call-update) | async-done | bytes 1179664 | tf_op jit(solution)/shard_map/all_gather | solution.py:65
  117.6 26.8 %all-gather.21.cloned.1.call-done = bf16[2304,512]{1,0:T(8,128)(2,1)} async-done(((bf16[288,512]{1,0:T(8,128)(2,1)}), bf16[2304,512]{1,0:T(8,128)(2,1)}) %all-gather.21.cloned.1.call-update) | async-done | bytes 2359312 | tf_op jit(solution)/shard_map/all_gather | solution.py:63
  144.4 3.9 fusion.65
  148.5 26.1 %all-gather.19.cloned.1.call-done = bf16[4096,256]{1,0:T(8,128)(2,1)} async-done(((bf16[512,256]{1,0:T(8,128)(2,1)}), bf16[4096,256]{1,0:T(8,128)(2,1)}) %all-gather.19.cloned.1.call-update) | async-done | bytes 2097168 | tf_op jit(solution)/shard_map/all_gather | solution.py:146
  174.6 30.2 %all-gather.25.cloned.1.call-done = bf16[4096,256]{1,0:T(8,128)(2,1)} async-done(((bf16[512,256]{1,0:T(8,128)(2,1)}), bf16[4096,256]{1,0:T(8,128)(2,1)}) %all-gather.25.cloned.1.call-update) | async-done | bytes 2097168 | tf_op jit(solution)/shard_map/all_gather | solution.py:147
  204.8 60.7 %while.32 = (s32[]{:T(128)}, f32[1,2,512,256]{3,2,1,0:T(8,128)S(1)}, f32[1,2,512]{2,1,0:T(2,128)S(1)}, s32[8]{0:T(128)S(1)}, s32[32]{0:T(128)S(1)}, /*index=5*/b...) while((s32[]{:T(128)}, ...), condition=%wide.region_3.4_spmd.clone, body=%wide.region_1.3_spmd.clone.sunk | while | flops 540018880 | bytes 6308628 | solution.py:124
  266.1 5.7 fusion.99
  272.7 84.6 %reduce-scatter.17.cloned.1.call-done = f32[128,2304]{1,0:T(8,128)} async-done(((f32[512,2304]{1,0:T(8,128)}), f32[128,2304]{1,0:T(8,128)}) %reduce-scatter.17.cloned.1.call-update) | async-done | bytes 1179664 | tf_op jit(solution)/shard_map/reduce_scatter | solution.py:156
  363.3 60.3 %all-gather.31.cloned.1.call-done = bf16[2304,2304]{1,0:T(8,128)(2,1)} async-done(((bf16[288,2304]{1,0:T(8,128)(2,1)}), bf16[2304,2304]{1,0:T(8,128)(2,1)}) %all-gather.31.cloned.1.call-update) | async-done | bytes 10616848 | tf_op jit(solution)/shard_map/all_gather | solution.py:67
  423.6 52.5 %all-gather.29.cloned.1.call-done = bf16[512,2304]{1,0:T(8,128)(2,1)} async-done(((bf16[128,2304]{1,0:T(8,128)(2,1)}), bf16[512,2304]{1,0:T(8,128)(2,1)}) %all-gather.29.cloned.1.call-update) | async-done | bytes 2359312 | tf_op jit(solution)/shard_map/all_gather | solution.py:164
  476.1 11.6 fusion.100
  487.7 52.9 %all-gather.33.cloned.1.call-done = bf16[2304,2304]{1,0:T(8,128)(2,1)} async-done(((bf16[288,2304]{1,0:T(8,128)(2,1)}), bf16[2304,2304]{1,0:T(8,128)(2,1)}) %all-gather.33.cloned.1.call-update) | async-done | bytes 10616848 | tf_op jit(solution)/shard_map/all_gather | solution.py:68
  540.6 12.8 multiply_convert_fusion.1
  553.5 52.8 %all-gather.35.cloned.1.call-done = bf16[2304,2304]{0,1:T(8,128)(2,1)} async-done(((bf16[2304,288]{0,1:T(8,128)(2,1)}), bf16[2304,2304]{0,1:T(8,128)(2,1)}) %all-gather.35.cloned.1.call-update) | async-done | bytes 10616848 | tf_op jit(solution)/shard_map/all_gather | solution.py:69
  606.2 11.7 fusion.101
  618.0 85.4 %reduce-scatter.19.cloned.1.call-done = f32[128,2304]{1,0:T(8,128)} async-done(((f32[512,2304]{1,0:T(8,128)}), f32[128,2304]{1,0:T(8,128)}) %reduce-scatter.19.cloned.1.call-update) | async-done | bytes 1179664 | tf_op jit(solution)/shard_map/reduce_scatter | solution.py:169
  708.7 50.9 %all-gather.37.cloned.1.call-done = bf16[512,2304]{1,0:T(8,128)(2,1)} async-done(((bf16[128,2304]{1,0:T(8,128)(2,1)}), bf16[512,2304]{1,0:T(8,128)(2,1)}) %all-gather.37.cloned.1.call-update) | async-done | bytes 2359312 | tf_op jit(solution)/shard_map/all_gather | solution.py:176
  759.7 14.2 multiply_convert_fusion
  773.9 9.8 fusion.102
  783.7 11.4 convolution_add_fusion.2
  795.2 84.2 %reduce-scatter.21.cloned.1.call-done = f32[128,2304]{1,0:T(8,128)} async-done(((f32[512,2304]{1,0:T(8,128)}), f32[128,2304]{1,0:T(8,128)}) %reduce-scatter.21.cloned.1.call-update) | async-done | bytes 1179664 | tf_op jit(solution)/shard_map/reduce_scatter | solution.py:185
  884.2 50.9 %all-gather.39.cloned.1.call-done = bf16[512,2304]{1,0:T(8,128)(2,1)} async-done(((bf16[128,2304]{1,0:T(8,128)(2,1)}), bf16[512,2304]{1,0:T(8,128)(2,1)}) %all-gather.39.cloned.1.call-update) | async-done | bytes 2359312 | tf_op jit(solution)/shard_map/all_gather | solution.py:189
  935.1 3.8 convolution_convert_fusion
  946.2 176.0 %while.33 = (s32[]{:T(128)}, f32[512,1,2,256]{0,3,2,1:T(8,128)S(1)}, f32[4096,256]{1,0:T(8,128)}, f32[4096,256]{1,0:T(8,128)}, bf16[8,512,256]{2,1,0:T(8,128)(2,...) while((s32[]{:T(128)}, ...), condition=%wide.region_15.16_spmd.clone, body=%wide.region_14.15_spmd.clone.sunk | while | flops 1349780736 | bytes 22025092 | solution.py:124
  960.0 3.0 dynamic_update_slice.16
  1004.5 3.0 dynamic_update_slice.16
  1054.6 3.0 dynamic_update_slice.17
  1123.6 48.9 %reduce-scatter.23.cloned.1.call-done = f32[512,256]{1,0:T(8,128)} async-done(((f32[4096,256]{1,0:T(8,128)}), f32[512,256]{1,0:T(8,128)}) %reduce-scatter.23.cloned.1.call-update) | async-done | bytes 524304 | tf_op jit(solution)/shard_map/reduce_scatter | solution.py:245
  1175.0 3.6 convolution_add_fusion
  1178.5 48.9 %reduce-scatter.25.cloned.1.call-done = f32[512,256]{1,0:T(8,128)} async-done(((f32[4096,256]{1,0:T(8,128)}), f32[512,256]{1,0:T(8,128)}) %reduce-scatter.25.cloned.1.call-update) | async-done | bytes 524304 | tf_op jit(solution)/shard_map/reduce_scatter | solution.py:246
  1227.5 6.0 fusion.54
  1233.5 19.3 all-reduce
  1255.8 3.8 fusion.93
  1260.6 5.4 fusion.103
  1274.8 11.8 fusion.104
  1286.6 12.2 fusion.105
  1300.5 11.8 fusion.106
  1314.1 62.7 %reduce-scatter.27.cloned.1.call-done = f32[128,2304]{1,0:T(8,128)} async-done(((f32[512,2304]{1,0:T(8,128)}), f32[128,2304]{1,0:T(8,128)}) %reduce-scatter.27.cloned.1.call-update) | async-done | bytes 1179664 | tf_op jit(solution)/shard_map/reduce_scatter | solution.py:268
  1381.0 54.7 %reduce-scatter.29.cloned.1.call-done = f32[288,512]{1,0:T(8,128)} async-done(((f32[2304,512]{1,0:T(8,128)}), f32[288,512]{1,0:T(8,128)}) %reduce-scatter.29.cloned.1.call-update) | async-done | bytes 589840 | tf_op jit(solution)/shard_map/reduce_scatter | solution.py:275
  1435.7 57.9 %reduce-scatter.35.cloned.1.call-done = f32[512,288]{0,1:T(8,128)} async-done(((f32[512,2304]{0,1:T(8,128)}), f32[512,288]{0,1:T(8,128)}) %reduce-scatter.35.cloned.1.call-update) | async-done | bytes 589840 | tf_op jit(solution)/shard_map/reduce_scatter | solution.py:278
  1493.6 46.8 %reduce-scatter.31.cloned.1.call-done = f32[288,256]{1,0:T(8,128)} async-done(((f32[2304,256]{1,0:T(8,128)}), f32[288,256]{1,0:T(8,128)}) %reduce-scatter.31.cloned.1.call-update) | async-done | bytes 294928 | tf_op jit(solution)/shard_map/reduce_scatter | solution.py:276
  1540.4 46.3 %reduce-scatter.33.cloned.1.call-done = f32[288,256]{1,0:T(8,128)} async-done(((f32[2304,256]{1,0:T(8,128)}), f32[288,256]{1,0:T(8,128)}) %reduce-scatter.33.cloned.1.call-update) | async-done | bytes 294928 | tf_op jit(solution)/shard_map/reduce_scatter | solution.py:277
  1586.7 141.8 %reduce-scatter.37.cloned.1.call-done = f32[288,2304]{1,0:T(8,128)} async-done(((f32[2304,2304]{1,0:T(8,128)}), f32[288,2304]{1,0:T(8,128)}) %reduce-scatter.37.cloned.1.call-update) | async-done | bytes 2654224 | tf_op jit(solution)/shard_map/reduce_scatter | solution.py:279
  1728.5 141.6 %reduce-scatter.39.cloned.1.call-done = f32[288,2304]{1,0:T(8,128)} async-done(((f32[2304,2304]{1,0:T(8,128)}), f32[288,2304]{1,0:T(8,128)}) %reduce-scatter.39.cloned.1.call-update) | async-done | bytes 2654224 | tf_op jit(solution)/shard_map/reduce_scatter | solution.py:280
  1870.1 141.6 %reduce-scatter.41.cloned.1.call-done = f32[2304,288]{0,1:T(8,128)} async-done(((f32[2304,2304]{0,1:T(8,128)}), f32[2304,288]{0,1:T(8,128)}) %reduce-scatter.41.cloned.1.call-update) | async-done | bytes 2654224 | tf_op jit(solution)/shard_map/reduce_scatter | solution.py:281
  (372 shorter events, 236.2 us)
Async XLA Ops:
  7.2 55.6 %all-gather.15.cloned.1.call-start = ((), (), s32[]{:S(2)}) async-start(), calls=%async_computation.14 | async-start | bytes 2949120 | tf_op jit(solution)/shard_map/all_gather | solution.py:73
  7.9 79.7 %all-gather.17.cloned.1.call-start = ((), (), s32[]{:S(2)}) async-start(), calls=%async_computation.15 | async-start | bytes 1327104 | tf_op jit(solution)/shard_map/all_gather | solution.py:64
  8.7 104.9 %all-gather.23.cloned.1.call-start = ((), (), s32[]{:S(2)}) async-start(), calls=%async_computation.18 | async-start | bytes 1327104 | tf_op jit(solution)/shard_map/all_gather | solution.py:65
  9.4 135.0 %all-gather.21.cloned.1.call-start = ((), (), s32[]{:S(2)}) async-start(), calls=%async_computation.17 | async-start | bytes 2654208 | tf_op jit(solution)/shard_map/all_gather | solution.py:63
  10.0 164.6 %all-gather.19.cloned.1.call-start = ((), (), s32[]{:S(2)}) async-start(), calls=%async_computation.16 | async-start | bytes 2359296 | tf_op jit(solution)/shard_map/all_gather | solution.py:146
  20.9 123.5 %copy-start.18 = (f32[2304]{0:T(1024)}, f32[2304]{0:T(1024)S(1)}, u32[]{:S(2)}) copy-start(f32[2304]{0:T(1024)S(1)} %get-tuple-element.550) | copy-start | bytes 27652
  62.8 24.8 %copy-start.7 = (bf16[512,2304]{1,0:T(8,128)(2,1)S(1)}, bf16[512,2304]{1,0:T(8,128)(2,1)}, u32[]{:S(2)}) copy-start(bf16[512,2304]{1,0:T(8,128)(2,1)} %all-gather.15.cloned.1.call-done) | copy-start | bytes 7077892
  65.2 79.2 %copy-start.20 = (f32[512]{0:T(512)}, f32[512]{0:T(512)S(1)}, u32[]{:S(2)}) copy-start(f32[512]{0:T(512)S(1)} %add_rsqrt_fusion) | copy-start | bytes 6148
  90.4 26.8 %copy-start.25 = (s32[32]{0:T(128)S(1)}, s32[32]{0:T(128)}, u32[]{:S(2)}) copy-start(s32[32]{0:T(128)} %param.29) | copy-start | bytes 388
  90.4 26.9 %copy-start.26 = (s32[32]{0:T(128)S(1)}, s32[32]{0:T(128)}, u32[]{:S(2)}) copy-start(s32[32]{0:T(128)} %param.28) | copy-start | bytes 388
  90.4 27.0 %copy-start.24 = (s32[32,32]{1,0:T(8,128)S(1)}, s32[32,32]{1,0:T(8,128)}, u32[]{:S(2)}) copy-start(s32[32,32]{1,0:T(8,128)} %param.27) | copy-start | bytes 12292
  90.4 114.4 %all-gather.25.cloned.1.call-start = ((), (), s32[]{:S(2)}) async-start(), calls=%async_computation.19 | async-start | bytes 2359296 | tf_op jit(solution)/shard_map/all_gather | solution.py:147
  116.4 149.7 %all-gather.27.cloned.1.call-start = ((), (), s32[]{:S(2)}) async-start(), calls=%async_computation.20 | async-start | bytes 2654208 | tf_op jit(solution)/shard_map/all_gather | solution.py:66
  117.1 240.1 %reduce-scatter.17.cloned.1.call-start = ((), (), s32[]{:S(2)}) async-start(), calls=%async_computation.21 | async-start | bytes 5898240 | tf_op jit(solution)/shard_map/reduce_scatter | solution.py:156
  265.6 6.3 copy-start.29
  265.6 6.2 copy-start.31
  265.6 6.2 copy-start.33
  265.9 5.9 copy-start.4
  266.1 5.8 copy-start.11
  271.9 86.8 %copy-start.5 = (bf16[128,2304]{1,0:T(8,128)(2,1)S(1)}, bf16[128,2304]{1,0:T(8,128)(2,1)}, u32[]{:S(2)}) copy-start(bf16[128,2304]{1,0:T(8,128)(2,1)} %param.17) | copy-start | bytes 1769476
  271.9 151.7 %all-gather.31.cloned.1.call-start = ((), (), s32[]{:S(2)}) async-start(), calls=%async_computation.23 | async-start | bytes 11943936 | tf_op jit(solution)/shard_map/all_gather | solution.py:67
  272.6 203.4 %all-gather.29.cloned.1.call-start = ((), (), s32[]{:S(2)}) async-start(), calls=%async_computation.22 | async-start | bytes 2949120 | tf_op jit(solution)/shard_map/all_gather | solution.py:164
  361.4 179.2 %all-gather.33.cloned.1.call-start = ((), (), s32[]{:S(2)}) async-start(), calls=%async_computation.24 | async-start | bytes 11943936 | tf_op jit(solution)/shard_map/all_gather | solution.py:68
  362.2 244.1 %all-gather.35.cloned.1.call-start = ((), (), s32[]{:S(2)}) async-start(), calls=%async_computation.25 | async-start | bytes 11943936 | tf_op jit(solution)/shard_map/all_gather | solution.py:69
  362.7 340.6 %reduce-scatter.19.cloned.1.call-start = ((), (), s32[]{:S(2)}) async-start(), calls=%async_computation.26 | async-start | bytes 5898240 | tf_op jit(solution)/shard_map/reduce_scatter | solution.py:169
  617.9 87.0 %copy-start.9 = (bf16[128,2304]{1,0:T(8,128)(2,1)S(1)}, bf16[128,2304]{1,0:T(8,128)(2,1)}, u32[]{:S(2)}) copy-start(bf16[128,2304]{1,0:T(8,128)(2,1)} %param.18) | copy-start | bytes 1769476
  617.9 141.7 %all-gather.37.cloned.1.call-start = ((), (), s32[]{:S(2)}) async-start(), calls=%async_computation.27 | async-start | bytes 2949120 | tf_op jit(solution)/shard_map/all_gather | solution.py:176
  708.5 170.9 %reduce-scatter.21.cloned.1.call-start = ((), (), s32[]{:S(2)}) async-start(), calls=%async_computation.28 | async-start | bytes 5898240 | tf_op jit(solution)/shard_map/reduce_scatter | solution.py:185
  773.9 9.8 copy-start.36
  773.9 9.8 copy-start.35
  795.1 85.9 %copy-start = (f32[128,2304]{1,0:T(8,128)S(1)}, f32[128,2304]{1,0:T(8,128)}, u32[]{:S(2)}) copy-start(f32[128,2304]{1,0:T(8,128)} %reduce-scatter.17.cloned.1.call-done) | copy-start | bytes 3538948
  795.2 140.0 %all-gather.39.cloned.1.call-start = ((), (), s32[]{:S(2)}) async-start(), calls=%async_computation.29 | async-start | bytes 2949120 | tf_op jit(solution)/shard_map/all_gather | solution.py:189
  883.9 288.6 %reduce-scatter.23.cloned.1.call-start = ((), (), s32[]{:S(2)}) async-start(), calls=%async_computation.30 | async-start | bytes 4718592 | tf_op jit(solution)/shard_map/reduce_scatter | solution.py:245
  1052.0 5.6 copy-start.17
  1122.3 105.2 %reduce-scatter.25.cloned.1.call-start = ((), (), s32[]{:S(2)}) async-start(), calls=%async_computation.31 | async-start | bytes 4718592 | tf_op jit(solution)/shard_map/reduce_scatter | solution.py:246
  1122.9 189.5 %reduce-scatter.43.cloned.1.call-start = ((), (), s32[]{:S(2)}) async-start(), calls=%async_computation.40 | async-start | bytes 1327104
  1174.9 52.5 %copy-start.8 = (bf16[512,2304]{1,0:T(8,128)(2,1)S(1)}, bf16[512,2304]{1,0:T(8,128)(2,1)}, u32[]{:S(2)}) copy-start(bf16[512,2304]{1,0:T(8,128)(2,1)} %all-gather.15.cloned.1.call-done) | copy-start | bytes 7077892
  1175.0 52.5 %copy-start.21 = (f32[512]{0:T(512)S(1)}, f32[512]{0:T(512)}, u32[]{:S(2)}) copy-start(f32[512]{0:T(512)} %copy-done.20) | copy-start | bytes 6148
  1255.0 121.7 %reduce-scatter.27.cloned.1.call-start = ((), (), s32[]{:S(2)}) async-start(), calls=%async_computation.32 | async-start | bytes 5898240 | tf_op jit(solution)/shard_map/reduce_scatter | solution.py:268
  1255.6 180.0 %reduce-scatter.29.cloned.1.call-start = ((), (), s32[]{:S(2)}) async-start(), calls=%async_computation.33 | async-start | bytes 5308416 | tf_op jit(solution)/shard_map/reduce_scatter | solution.py:275
  1259.6 234.0 %reduce-scatter.35.cloned.1.call-start = ((), (), s32[]{:S(2)}) async-start(), calls=%async_computation.36 | async-start | bytes 5308416 | tf_op jit(solution)/shard_map/reduce_scatter | solution.py:278
  1266.0 274.3 %reduce-scatter.31.cloned.1.call-start = ((), (), s32[]{:S(2)}) async-start(), calls=%async_computation.34 | async-start | bytes 2654208 | tf_op jit(solution)/shard_map/reduce_scatter | solution.py:276
  1269.7 317.0 %reduce-scatter.33.cloned.1.call-start = ((), (), s32[]{:S(2)}) async-start(), calls=%async_computation.35 | async-start | bytes 2654208 | tf_op jit(solution)/shard_map/reduce_scatter | solution.py:277
  1273.1 455.3 %reduce-scatter.37.cloned.1.call-start = ((), (), s32[]{:S(2)}) async-start(), calls=%async_computation.37 | async-start | bytes 23887872 | tf_op jit(solution)/shard_map/reduce_scatter | solution.py:279
  1286.6 583.5 %reduce-scatter.39.cloned.1.call-start = ((), (), s32[]{:S(2)}) async-start(), calls=%async_computation.38 | async-start | bytes 23887872 | tf_op jit(solution)/shard_map/reduce_scatter | solution.py:280
  1298.9 712.8 %reduce-scatter.41.cloned.1.call-start = ((), (), s32[]{:S(2)}) async-start(), calls=%async_computation.39 | async-start | bytes 23887872 | tf_op jit(solution)/shard_map/reduce_scatter | solution.py:281
  1312.3 64.4 %copy-start.6 = (bf16[128,2304]{1,0:T(8,128)(2,1)S(1)}, bf16[128,2304]{1,0:T(8,128)(2,1)}, u32[]{:S(2)}) copy-start(bf16[128,2304]{1,0:T(8,128)(2,1)} %param.17) | copy-start | bytes 1769476
  1312.4 66.0 %copy-start.3 = (f32[128,2304]{1,0:T(8,128)S(1)}, f32[128,2304]{1,0:T(8,128)}, u32[]{:S(2)}) copy-start(f32[128,2304]{1,0:T(8,128)} %copy-done.2) | copy-start | bytes 3538948
  (23 other events, 65.8 us)
Sparse Core Ops, SparseCore 0:
  9.6 53.1 all-gather.14
  64.7 22.8 all-gather.16
  89.5 24.0 all-gather.22
  115.3 29.0 all-gather.20
  146.7 27.8 all-gather.18
  176.9 27.8 all-gather.24
  206.7 29.0 all-gather.26
  272.0 85.2 reduce-scatter.16
  359.2 64.3 all-gather.30
  425.6 50.4 all-gather.28
  478.0 62.6 all-gather.32
  542.4 63.8 all-gather.34
  618.0 85.2 reduce-scatter.18
  708.6 50.9 all-gather.36
  795.3 84.0 reduce-scatter.20
  884.1 50.9 all-gather.38
  1122.4 50.1 reduce-scatter.22
  1176.1 51.3 reduce-scatter.24
  1255.2 34.0 reduce-scatter.42
  1291.5 85.2 reduce-scatter.26
  1381.2 54.4 reduce-scatter.28
  1439.7 53.8 reduce-scatter.34
  1497.9 42.4 reduce-scatter.30
  1544.2 42.4 reduce-scatter.32
  1591.3 137.1 reduce-scatter.36
  1732.9 137.1 reduce-scatter.38
  1874.6 137.1 reduce-scatter.40
where the time goes:
time: 2030 us; the launch traced here: 2020 us
  waiting for transfers between devices  1540 us (76%)
  matrix products  274 us (13%)
  local copies, waits for them, and re-layouts  80.3 us (4%)
  loops' own time  52.9 us (3%)
  blocking collectives  30 us (1%)
  other arithmetic  21.3 us (1%)
    reduce_scatter x1, waiting for transfers between devices, on_device(): lax.psum_scatter(grad_gate, 'ctx', scatter_dimension=0, tiled=True)  142 us
    reduce_scatter x1, waiting for transfers between devices, on_device(): lax.psum_scatter(grad_up, 'ctx', scatter_dimension=0, tiled=True)  142 us
    reduce_scatter x1, waiting for transfers between devices, on_device(): lax.psum_scatter(grad_down, 'ctx', scatter_dimension=1, tiled=True)  142 us
    reduce_scatter x1, waiting for transfers between devices, on_device(): lax.psum_scatter(matmul_fwd(mid_rows, full_set[6]), 'tp', scatter_dimensi...  85.4 us
    reduce_scatter x1, waiting for transfers between devices, on_device(): lax.psum_scatter(matmul_fwd(attended, full_set[3]), 'tp', scatter_dimensi...  84.6 us
    reduce_scatter x1, waiting for transfers between devices, on_device(): lax.psum_scatter(dinner_part, 'tp', scatter_dimension=0, tiled=True)  84.2 us
    reduce_scatter x1, waiting for transfers between devices, on_device(): lax.psum_scatter(dnormed_part, 'tp', scatter_dimension=0, tiled=True)  62.7 us
    all_gather x1, waiting for transfers between devices, on_device(): lax.all_gather(weight_set[4], 'ctx', axis=0, tiled=True)  60.3 us
  transfers between devices with their start and end apart: 27, of which 25 were waited for; matrix products, arithmetic and copies ran while one was open for 7% of the time, Pallas kernels for 0%

commit v1 on v0

v1 whole, which is shorter than its diff:
```python
import functools

import jax
import jax.numpy as jnp
from jax import lax
from jax.experimental import pallas as pl
from jax.experimental.pallas import tpu as pltpu
from jax.sharding import PartitionSpec as P

QUERY_HEADS = 8
KEY_VALUE_HEADS = 4
HEAD_SIZE = 256
SCORE_SOFT_LIMIT = 50
BLOCK_TOKENS = 128
EPSILON = 1e-06
KEY_STEP = 4

F32 = jnp.float32
BF16 = jnp.bfloat16


def dot(a, b):
    return jnp.dot(a, b, preferred_element_type=F32)


def dot_back(a, b):
    return lax.dot_general(a, b, (((1,), (1,)), ((), ())), preferred_element_type=F32)


def dot_rows(a, b):
    return lax.dot_general(a, b, (((0,), (0,)), ((), ())), preferred_element_type=F32)


def inv_rms(v):
    return lax.rsqrt(jnp.mean(v * v, axis=-1, keepdims=True) + EPSILON)


def norm_input_grad(v, s, gain, c):
    cw = c * gain
    return s * cw - v * (s * s * s) * jnp.mean(cw * v, axis=-1, keepdims=True)


def swap(x, bit):
    size = lax.axis_size("ctx")
    return lax.ppermute(x, "ctx", [(i, i ^ (1 << bit)) for i in range(size)])


def ctx_bits():
    size = lax.axis_size("ctx")
    bits = size.bit_length() - 1
    assert size == 1 << bits and bits >= 1
    return bits


def rel_of(place):
    half = lax.axis_size("ctx") // 2
    return (place % half) * 2 + place // half


def gather_half(x, order):
    held = {0: x}
    for bit in order:
        held |= {rel ^ (1 << bit): swap(held[rel], bit) for rel in list(held)}
    return [held[rel_of(p)] for p in range(lax.axis_size("ctx"))]


def gather_ctx(a, b):
    outer = list(range(1, ctx_bits()))
    return gather_half(a, outer + [0]), gather_half(b, outer[::-1] + [0])


def gather_rows(w):
    half = w.shape[0] // 32 * 16
    a, b = gather_ctx(w[:half], w[half:])
    return jnp.concatenate([piece for pair in zip(a, b) for piece in pair], axis=0)


def scatter_half(sent, kept, order):
    got = swap(sent.astype(BF16), 0)
    now = {r: kept[r].astype(F32) + got[r].astype(F32) for r in range(kept.shape[0])}
    for bit in order:
        mask = 1 << (bit - 1)
        came = {r: swap(v.astype(BF16), bit) for r, v in now.items() if r & mask}
        now = {r: v + came[r | mask].astype(F32) for r, v in now.items() if not r & mask}
    return now[0]


def scatter_pair(sent_a, kept_a, sent_b, kept_b):
    outer = list(range(1, ctx_bits()))
    return scatter_half(sent_a, kept_a, outer[::-1]), scatter_half(sent_b, kept_b, outer)


def scatter_grad(left, right):
    size = lax.axis_size("ctx")
    width = left.shape[1] // 2
    cut = right.shape[1] // 2
    parts = []
    for columns in (right[:, :cut], right[:, cut:]):
        for rows in (left[:, width:], left[:, :width]):
            part = dot_rows(rows, columns).astype(BF16)
            parts.append(part.reshape(size // 2, 2 * width // size, cut))
    return jnp.concatenate(scatter_pair(*parts), axis=1)


def line(x, perm):
    return lax.ppermute(x, "tp", perm)


def gather_tp(x):
    size, me = lax.axis_size("tp"), lax.axis_index("tp")
    up, down = x, x
    ups, downs = {}, {}
    for s in range(1, size):
        up = line(up, [(i, i + 1) for i in range(s - 1, size - 1)])
        down = line(down, [(i, i - 1) for i in range(1, size - s + 1)])
        ups[s], downs[s] = up, down
    rest = [jnp.where(me + r < size, downs[r], ups[size - r]) for r in range(1, size)]
    return jnp.concatenate([x] + rest, axis=0)


def scatter_tp(part):
    size = lax.axis_size("tp")
    rows = part.shape[0] // size
    block = [part[r * rows : (r + 1) * rows] for r in range(size)]
    up = down = 0.0
    for s in range(1, size):
        up_send = (block[size - s].astype(F32) + up).astype(BF16)
        down_send = (block[s].astype(F32) + down).astype(BF16)
        up = line(up_send, [(i, i + 1) for i in range(s)]).astype(F32)
        down = line(down_send, [(i, i - 1) for i in range(size - s, size)]).astype(F32)
    return block[0].astype(F32) + up + down


def take_blocks(ref, index_ref, query_block, step, blocks):
    places = [index_ref[query_block, step * KEY_STEP + j] for j in range(KEY_STEP)]
    starts = [pl.multiple_of(p * BLOCK_TOKENS, BLOCK_TOKENS) for p in places]
    return starts, jnp.concatenate([ref[pl.ds(s, BLOCK_TOKENS), :] for s in starts], axis=0)


def stack_heads(x):
    heads = x.shape[1] // HEAD_SIZE
    return jnp.concatenate([x[:, h * HEAD_SIZE : (h + 1) * HEAD_SIZE] for h in range(heads)], axis=0)


def unstack_heads(x):
    rows = BLOCK_TOKENS
    return jnp.concatenate([x[h * rows : (h + 1) * rows] for h in range(x.shape[0] // rows)], axis=1)


def attend_kernel(index_ref, count_ref, q_ref, k_ref, v_ref, out_ref, total_ref, acc_ref):
    i = pl.program_id(0)
    count = count_ref[i]
    q = stack_heads(q_ref[...])
    acc_ref[...] = jnp.zeros_like(acc_ref)
    total_ref[...] = jnp.zeros_like(total_ref)

    def body(step, carry):
        starts, keys = take_blocks(k_ref, index_ref, i, step, KEY_STEP)
        values = jnp.concatenate([v_ref[pl.ds(s, BLOCK_TOKENS), :] for s in starts], axis=0)
        scores = dot_back(q, keys)
        grown = jnp.exp(SCORE_SOFT_LIMIT * jnp.tanh(scores * (1.0 / SCORE_SOFT_LIMIT)))
        pieces = []
        for j in range(KEY_STEP):
            seen = (step * KEY_STEP + j) < count
            piece = grown[:, j * BLOCK_TOKENS : (j + 1) * BLOCK_TOKENS]
            pieces.append(jnp.where(seen, piece, 0.0))
        total_ref[...] += functools.reduce(jnp.add, pieces)
        acc_ref[...] += dot(jnp.concatenate(pieces, axis=1).astype(BF16), values)
        return carry

    lax.fori_loop(0, (count + KEY_STEP - 1) // KEY_STEP, body, 0)
    totals = jnp.sum(total_ref[...], axis=1, keepdims=True)
    total_ref[...] = jnp.broadcast_to(totals, total_ref.shape)
    out_ref[...] = unstack_heads(acc_ref[...] / totals)


def attend_back_kernel(
    index_ref, count_ref, q_ref, dout_ref, out_ref, total_ref, k_ref, v_ref, dq_ref, dk_ref, dv_ref, acc_ref
):
    i = pl.program_id(0)

    @pl.when(i == 0)
    def _():
        dk_ref[...] = jnp.zeros_like(dk_ref)
        dv_ref[...] = jnp.zeros_like(dv_ref)

    count = count_ref[i]
    q = stack_heads(q_ref[...])
    dout = stack_heads(dout_ref[...]).astype(F32)
    inverse = 1.0 / total_ref[:, :1]
    scaled = (dout * inverse).astype(BF16)
    weighted = dout * stack_heads(out_ref[...]) * inverse
    ones = jnp.ones((8, HEAD_SIZE), F32)
    dtotal = -lax.dot_general(
        ones, weighted, (((1,), (1,)), ((), ())), precision=lax.Precision.HIGHEST, preferred_element_type=F32
    )[:1]
    acc_ref[...] = jnp.zeros_like(acc_ref)

    def body(step, carry):
        starts, keys = take_blocks(k_ref, index_ref, i, step, KEY_STEP)
        values = jnp.concatenate([v_ref[pl.ds(s, BLOCK_TOKENS), :] for s in starts], axis=0)
        soft = jnp.tanh(dot_back(keys, q) * (1.0 / SCORE_SOFT_LIMIT))
        grown = jnp.exp(SCORE_SOFT_LIMIT * soft)
        pieces = []
        for j in range(KEY_STEP):
            seen = (step * KEY_STEP + j) < count
            piece = grown[j * BLOCK_TOKENS : (j + 1) * BLOCK_TOKENS]
            pieces.append(jnp.where(seen, piece, 0.0))
        grown = jnp.concatenate(pieces, axis=0)
        dprob = dot_back(values, scaled)
        dscores = (grown * (dprob + dtotal) * (1.0 - soft * soft)).astype(BF16)
        acc_ref[...] += dot_rows(dscores, keys)
        dkeys = dot(dscores, q)
        dvalues = dot(grown.astype(BF16), scaled)
        for j in range(KEY_STEP):
            at = pl.ds(starts[j], BLOCK_TOKENS)
            dk_ref[at, :] += dkeys[j * BLOCK_TOKENS : (j + 1) * BLOCK_TOKENS]
            dv_ref[at, :] += dvalues[j * BLOCK_TOKENS : (j + 1) * BLOCK_TOKENS]
        return carry

    lax.fori_loop(0, (count + KEY_STEP - 1) // KEY_STEP, body, 0)
    dq_ref[...] = unstack_heads(acc_ref[...]).astype(BF16)


VMEM_LIMIT = 56 * 1024 * 1024


def whole_spec(shape):
    return pl.BlockSpec(shape, lambda i, *_: (0,) * len(shape), pipeline_mode=pl.Buffered(1))


def row_spec(rows, columns):
    return pl.BlockSpec((rows, columns), lambda i, *_: (i, 0))


def attend(index, count, q, k, v):
    rows, columns = q.shape
    blocks, stacked = rows // BLOCK_TOKENS, BLOCK_TOKENS * (columns // HEAD_SIZE)
    return pl.pallas_call(
        attend_kernel,
        grid_spec=pltpu.PrefetchScalarGridSpec(
            num_scalar_prefetch=2,
            grid=(blocks,),
            in_specs=[row_spec(BLOCK_TOKENS, columns), whole_spec(k.shape), whole_spec(v.shape)],
            out_specs=[row_spec(BLOCK_TOKENS, columns), row_spec(stacked, BLOCK_TOKENS)],
            scratch_shapes=[pltpu.VMEM((stacked, HEAD_SIZE), F32)],
        ),
        out_shape=[
            jax.ShapeDtypeStruct((rows, columns), F32),
            jax.ShapeDtypeStruct((blocks * stacked, BLOCK_TOKENS), F32),
        ],
        compiler_params=pltpu.CompilerParams(vmem_limit_bytes=VMEM_LIMIT),
        cost_estimate=pl.CostEstimate(flops=2 * rows * columns * k.shape[0], bytes_accessed=6 << 20, transcendentals=0),
    )(index, count, q, k, v)


def attend_back(index, count, q, dout, out, totals, k, v):
    rows, columns = q.shape
    blocks, stacked = rows // BLOCK_TOKENS, BLOCK_TOKENS * (columns // HEAD_SIZE)
    row = row_spec(BLOCK_TOKENS, columns)
    return pl.pallas_call(
        attend_back_kernel,
        grid_spec=pltpu.PrefetchScalarGridSpec(
            num_scalar_prefetch=2,
            grid=(blocks,),
            in_specs=[row, row, row, row_spec(stacked, BLOCK_TOKENS), whole_spec(k.shape), whole_spec(v.shape)],
            out_specs=[row, whole_spec(k.shape), whole_spec(v.shape)],
            scratch_shapes=[pltpu.VMEM((stacked, HEAD_SIZE), F32)],
        ),
        out_shape=[
            jax.ShapeDtypeStruct((rows, columns), BF16),
            jax.ShapeDtypeStruct(k.shape, F32),
            jax.ShapeDtypeStruct(v.shape, F32),
        ],
        compiler_params=pltpu.CompilerParams(vmem_limit_bytes=VMEM_LIMIT),
        cost_estimate=pl.CostEstimate(flops=5 * rows * columns * k.shape[0], bytes_accessed=16 << 20, transcendentals=0),
    )(index, count, q, dout, out, totals, k, v)


def visible_lists(block_mask, block_seq, block_place, per_device):
    size, tp = lax.axis_size("ctx"), lax.axis_size("tp")
    ctx, me = lax.axis_index("ctx"), lax.axis_index("tp")
    total = block_seq.shape[0]
    turned = (me + jnp.arange(tp, dtype=jnp.int32)) % tp
    inner = (turned[:, None] * per_device + jnp.arange(per_device, dtype=jnp.int32)[None, :]).reshape(-1)
    owner = ctx ^ jnp.array([rel_of(p) for p in range(size)], jnp.int32)
    of_group = tp * per_device
    query_ids = ctx * of_group + inner
    key_ids = (owner[:, None] * of_group + inner[None, :]).reshape(-1)
    every = jnp.arange(total, dtype=jnp.int32)

    def look_up(ids, table):
        return jnp.sum(jnp.where(ids[:, None] == every[None, :], table[None, :], 0), axis=1)

    places = jnp.arange(block_mask.shape[0], dtype=jnp.int32)
    query_pick = (look_up(query_ids, block_place)[:, None] == places[None, :]).astype(F32)
    key_pick = (look_up(key_ids, block_place)[:, None] == places[None, :]).astype(F32)
    hits = dot_back(dot(query_pick, block_mask.astype(F32)), key_pick)
    same = look_up(query_ids, block_seq)[:, None] == look_up(key_ids, block_seq)[None, :]
    seen = (hits > 0.5) & same
    before = (every[:, None] < every[None, :]).astype(F32)
    rank = dot(seen.astype(F32), before).astype(jnp.int32)
    wanted = seen[:, None, :] & (rank[:, None, :] == every[None, :, None])
    index = jnp.sum(jnp.where(wanted, every[None, None, :], 0), axis=2)
    index = jnp.pad(index, ((0, 0), (0, KEY_STEP)))
    return index, jnp.sum(seen.astype(jnp.int32), axis=1)


def to_places(x):
    size, ctx = lax.axis_size("ctx"), lax.axis_index("ctx")
    chunk = x.shape[1] // size
    return jnp.concatenate(
        [lax.dynamic_slice_in_dim(x, (ctx ^ rel_of(p)) * chunk, chunk, 1) for p in range(size)], axis=1
    )


def from_places(x):
    size, ctx = lax.axis_size("ctx"), lax.axis_index("ctx")
    chunk = x.shape[1] // size
    half = size // 2

    def place(natural):
        rel = ctx ^ natural
        return (rel % 2) * half + rel // 2

    return jnp.concatenate(
        [lax.dynamic_slice_in_dim(x, place(j) * chunk, chunk, 1) for j in range(size)], axis=1
    )


def sum_gains(terms):
    size, tp, me = lax.axis_size("ctx"), lax.axis_size("tp"), lax.axis_index("tp")
    rows, width = terms.shape
    chunk = width // size
    now = {p: terms[:, p * chunk : (p + 1) * chunk] for p in range(size)}
    now = {rel_of(p): v for p, v in now.items()}
    for bit in range(ctx_bits()):
        mask = 1 << bit
        sent = [r for r in now if r & mask]
        came = swap(jnp.concatenate([now[r] for r in sent], axis=0), bit)
        came = {r ^ mask: came[n * rows : (n + 1) * rows] for n, r in enumerate(sent)}
        now = {r: v + came[r] for r, v in now.items() if not r & mask}
    mine = now[0]
    per = rows // tp

    def rows_of(shift):
        return lax.dynamic_slice_in_dim(mine, ((me + shift) % tp) * per, per, 0)

    total = rows_of(0)
    for shift in range(1, tp):
        total = total + lax.ppermute(rows_of(shift), "tp", [(i, (i + shift) % tp) for i in range(tp)])
    return total


def on_device(
    tokens,
    cotangent,
    w_query,
    key_projection,
    value_projection,
    w_out,
    w_gate,
    w_up,
    w_down,
    norm_gains,
    block_mask,
    block_seq,
    block_place,
):
    per_device = tokens.shape[0] // BLOCK_TOKENS
    scale = HEAD_SIZE ** (-0.5)
    q_cols, kv_cols = w_query.shape[1], key_projection.shape[1]

    gain_pieces = gather_half(norm_gains, list(range(ctx_bits())))
    gains = 1.0 + jnp.concatenate(gain_pieces, axis=1).astype(F32)
    tokens = to_places(tokens)
    cot = to_places(cotangent).astype(F32)
    index, count = visible_lists(block_mask, block_seq, block_place, per_device)

    wide = gather_rows(jnp.concatenate([w_query, key_projection, value_projection], axis=1))
    rows_in = gather_tp(tokens).astype(F32)
    normed = (rows_in * inv_rms(rows_in) * gains[0]).astype(BF16)
    qkv = dot(normed, wide)
    q = (qkv[:, :q_cols] * scale).astype(BF16)
    keys_own = qkv[:, q_cols : q_cols + kv_cols].astype(BF16)
    values_own = qkv[:, q_cols + kv_cols :].astype(BF16)
    key_pieces, value_pieces = gather_ctx(keys_own, values_own)
    keys, values = jnp.concatenate(key_pieces, axis=0), jnp.concatenate(value_pieces, axis=0)

    out_t = gather_rows(w_out.T)
    gate_w = gather_rows(w_gate)
    up_w = gather_rows(w_up)
    down_t = gather_rows(w_down.T)

    outcome, totals = attend(index, count, q, keys, values)
    attended = outcome.astype(BF16)
    branch = scatter_tp(dot_back(attended, out_t).astype(BF16))

    xf = tokens.astype(F32)
    s_branch = inv_rms(branch)
    hidden = xf + branch * s_branch * gains[1]
    s_hidden = inv_rms(hidden)
    inner = gather_tp((hidden * s_hidden * gains[2]).astype(BF16))
    gate_pre = dot(inner, gate_w)
    up_pre = dot(inner, up_w)
    cube = 0.7978845608028654
    bend = jnp.tanh(cube * (gate_pre + 0.044715 * gate_pre * gate_pre * gate_pre))
    gelu = 0.5 * gate_pre * (1.0 + bend)
    mid = (gelu * up_pre).astype(BF16)
    feed = scatter_tp(dot_back(mid, down_t).astype(BF16))
    s_feed = inv_rms(feed)
    mixed = from_places((hidden + feed * s_feed * gains[3]).astype(BF16))
    term_four = jnp.sum(cot * feed * s_feed, axis=0)
    dfeed = gather_tp(norm_input_grad(feed, s_feed, gains[3], cot).astype(BF16))

    grad_down = scatter_grad(dfeed, mid).T
    dmid = dot(dfeed, down_t)
    slope = 0.5 * (1.0 + bend) + 0.5 * gate_pre * (1.0 - bend * bend) * cube * (
        1.0 + 3 * 0.044715 * gate_pre * gate_pre
    )
    dgate = (dmid * up_pre * slope).astype(BF16)
    dup = (dmid * gelu).astype(BF16)
    dinner = scatter_tp((dot_back(dgate, gate_w) + dot_back(dup, up_w)).astype(BF16))
    grad_gate = scatter_grad(inner, dgate)
    grad_up = scatter_grad(inner, dup)
    term_three = jnp.sum(dinner * hidden * s_hidden, axis=0)
    dhidden = cot + norm_input_grad(hidden, s_hidden, gains[2], dinner)
    term_two = jnp.sum(dhidden * branch * s_branch, axis=0)
    dbranch = gather_tp(norm_input_grad(branch, s_branch, gains[1], dhidden).astype(BF16))
    grad_out = scatter_grad(dbranch, attended).T
    dattended = dot(dbranch, out_t).astype(BF16)

    dq, dk, dv = attend_back(index, count, q, dattended, outcome, totals, keys, values)
    dq = dq * jnp.asarray(scale, BF16)
    size = lax.axis_size("ctx")
    group = keys_own.shape[0]
    parts = []
    for d in (dk, dv):
        parts += [d[size // 2 * group :].reshape(size // 2, group, kv_cols), d[: size // 2 * group].reshape(size // 2, group, kv_cols)]
    dkeys, dvalues = scatter_pair(*parts)
    dqkv = jnp.concatenate([dq, dkeys.astype(BF16), dvalues.astype(BF16)], axis=1)
    dnormed_part = dot_back(dqkv, wide)
    term_one = jnp.sum(dnormed_part * rows_in * inv_rms(rows_in), axis=0)
    grad_query = scatter_grad(normed, dqkv[:, :q_cols])
    grad_kv = scatter_grad(normed, dqkv[:, q_cols:])
    grad_gains = sum_gains(jnp.stack([term_one, term_two, term_three, term_four]))
    dnormed = scatter_tp(dnormed_part.astype(BF16))
    grad_tokens = from_places(dhidden + norm_input_grad(xf, inv_rms(xf), gains[0], dnormed))
    return (
        mixed,
        grad_tokens,
        grad_query,
        grad_kv[:, :kv_cols],
        grad_kv[:, kv_cols:],
        grad_out,
        grad_gate,
        grad_up,
        grad_down,
        grad_gains,
    )


def solution(mesh):
    rows, weight, turned = P(("ctx", "tp"), None), P("ctx", "tp"), P("tp", "ctx")
    in_specs = (rows, rows, weight, weight, weight, turned, weight, weight, turned, P(None, "ctx"), P(), P(), P())
    out_specs = (rows, rows, weight, weight, weight, turned, weight, weight, turned, turned)
    return jax.shard_map(on_device, mesh=mesh, in_specs=in_specs, out_specs=out_specs, check_vma=False)
```

time: 2030 us -> 1040 us (0.51)
  waiting for transfers between devices: 1540 us -> 503 us
  starting transfers between devices: 2.54 us -> 215 us
  matrix products: 274 us -> 125 us
  loops' own time: 52.9 us -> 0 us
  other arithmetic: 21.3 us -> 63.5 us
  Pallas kernels: 0 us -> 30.9 us
  blocking collectives: 30 us -> 0 us
    reduce_scatter x13 -> x0, waiting for transfers between devices: 1050 us -> none  [the longest x1 142 us: on_device(): lax.psum_scatter(grad_gate, 'ctx', scatter_dimension=0, tiled=True)]
    ppermute x0 -> x201, waiting for transfers between devices: none -> 503 us  [the longest x150 302 us: swap(): return lax.ppermute(x, 'ctx', [(i, i ^ 1 << bit) for i in range(size)])]
    all_gather x13 -> x0, waiting for transfers between devices: 491 us -> none  [the longest x1 60.3 us: on_device(): lax.all_gather(weight_set[4], 'ctx', axis=0, tiled=True)]
    ppermute x0 -> x201, starting transfers between devices: none -> 215 us  [the longest x48 118 us: line(): return lax.ppermute(x, 'tp', perm)]
    dot_general x94 -> x36, matrix products: 274 us -> 125 us  [the longest x6 42.9 us: dot(): return jnp.dot(a, b, preferred_element_type=F32)]
    unnamed x78 -> x305, local copies, waits for them, and re-layouts: 12.4 us -> 70.1 us
    another operation x2 -> x0, loops' own time: 52.9 us -> none  [over_blocks(): running, _ = lax.scan(advance, running, (key_split, value_split, offsets))]
    dynamic_update_slice x16 -> x0, local copies, waits for them, and re-layouts: 45.3 us -> none  [the longest x8 22.7 us: backward_step(): lax.dynamic_update_slice_in_dim(dvalues_all, old_values + value_part, off...]
  transfers between devices with their start and end apart: 27 -> 201, of which waited for: 25 -> 84; matrix products, arithmetic and copies ran while one was open for 7% -> 17% of each run, Pallas kernels for 0% -> 3%
where the time goes in v1:
time: 1040 us; the launch traced here: 1030 us
  waiting for transfers between devices  503 us (48%)
  starting transfers between devices  215 us (21%)
  matrix products  125 us (12%)
  local copies, waits for them, and re-layouts  91.2 us (9%)
  other arithmetic  63.5 us (6%)
  Pallas kernels  30.9 us (3%)
    ppermute x150, waiting for transfers between devices, swap(): return lax.ppermute(x, 'ctx', [(i, i ^ 1 << bit) for i in range(size)])  302 us
    ppermute x48, waiting for transfers between devices, line(): return lax.ppermute(x, 'tp', perm)  190 us
    ppermute x48, starting transfers between devices, line(): return lax.ppermute(x, 'tp', perm)  118 us
    ppermute x150, starting transfers between devices, swap(): return lax.ppermute(x, 'ctx', [(i, i ^ 1 << bit) for i in range(size)])  93.5 us
    unnamed x305, local copies, waits for them, and re-layouts  70.1 us
    dot_general x6, matrix products, dot(): return jnp.dot(a, b, preferred_element_type=F32)  42.9 us
    dot_general x6, matrix products, dot_back(): lax.dot_general(a, b, (((1,), (1,)), ((), ())), preferred_element_type=F32)  42.6 us
    dot_general x24, matrix products, dot_rows(): lax.dot_general(a, b, (((0,), (0,)), ((), ())), preferred_element_type=F32)  39.1 us
  transfers between devices with their start and end apart: 201, of which 84 were waited for; matrix products, arithmetic and copies ran while one was open for 17% of the time, Pallas kernels for 3%

profile of v1, /device:TPU:0, one launch (start us, length us, event | category | flops | bytes accessed | tf_op | source)
XLA Modules:
  0.0 1031.3 jit_solution(10478022626216178711)
XLA Ops:
  38.1 10.2 collective-permute-done.43
  96.6 11.5 %collective-permute-done.68 = bf16[144,2304]{1,0:T(8,128)(2,1)S(1)} collective-permute-done((bf16[144,2304]{1,0:T(8,128)(2,1)S(1)}, bf16[144,2304]{1,0:T(8,128)(2,1)S(1)}, u32[]{:S(2)}, u32[]{:S(2)}) %collective-permute-start.68) | collective-permute-done | bytes 663584 | tf_op jit(solution)/shard_map/ppermute | solution.py:45
  116.5 13.9 %collective-permute-done.81 = bf16[144,2304]{1,0:T(8,128)(2,1)S(1)} collective-permute-done((bf16[144,2304]{1,0:T(8,128)(2,1)S(1)}, bf16[144,2304]{1,0:T(8,128)(2,1)S(1)}, u32[]{:S(2)}, u32[]{:S(2)}) %collective-permute-start.81) | collective-permute-done | bytes 663584 | tf_op jit(solution)/shard_map/ppermute | solution.py:45
  131.8 10.7 %collective-permute-done.82 = bf16[144,2304]{1,0:T(8,128)(2,1)S(1)} collective-permute-done((bf16[144,2304]{1,0:T(8,128)(2,1)S(1)}, bf16[144,2304]{1,0:T(8,128)(2,1)S(1)}, u32[]{:S(2)}, u32[]{:S(2)}) %collective-permute-start.82) | collective-permute-done | bytes 663584 | tf_op jit(solution)/shard_map/ppermute | solution.py:45
  145.3 11.9 %collective-permute-done.84 = bf16[144,2304]{1,0:T(8,128)(2,1)S(1)} collective-permute-done((bf16[144,2304]{1,0:T(8,128)(2,1)S(1)}, bf16[144,2304]{1,0:T(8,128)(2,1)S(1)}, u32[]{:S(2)}, u32[]{:S(2)}) %collective-permute-start.84) | collective-permute-done | bytes 663584 | tf_op jit(solution)/shard_map/ppermute | solution.py:45
  163.2 9.4 collective-permute-done.96
  177.7 9.3 collective-permute-done.98
  194.6 14.9 %collective-permute-done.71 = bf16[144,2304]{1,0:T(8,128)(2,1)S(1)} collective-permute-done((bf16[144,2304]{1,0:T(8,128)(2,1)S(1)}, bf16[144,2304]{1,0:T(8,128)(2,1)S(1)}, u32[]{:S(2)}, u32[]{:S(2)}) %collective-permute-start.71) | collective-permute-done | bytes 663584 | tf_op jit(solution)/shard_map/ppermute | solution.py:45
  219.3 13.9 %collective-permute-done.85 = bf16[144,2304]{1,0:T(8,128)(2,1)S(1)} collective-permute-done((bf16[144,2304]{1,0:T(8,128)(2,1)S(1)}, bf16[144,2304]{1,0:T(8,128)(2,1)S(1)}, u32[]{:S(2)}, u32[]{:S(2)}) %collective-permute-start.85) | collective-permute-done | bytes 663584 | tf_op jit(solution)/shard_map/ppermute | solution.py:45
  243.7 12.4 %collective-permute-done.99 = bf16[144,2304]{1,0:T(8,128)(2,1)S(1)} collective-permute-done((bf16[144,2304]{1,0:T(8,128)(2,1)S(1)}, bf16[144,2304]{1,0:T(8,128)(2,1)S(1)}, u32[]{:S(2)}, u32[]{:S(2)}) %collective-permute-start.99) | collective-permute-done | bytes 663584 | tf_op jit(solution)/shard_map/ppermute | solution.py:45
  264.3 12.4 %collective-permute-done.5 = bf16[128,2304]{1,0:T(8,128)(2,1)S(1)} collective-permute-done((bf16[128,2304]{1,0:T(8,128)(2,1)S(1)}, bf16[128,2304]{1,0:T(8,128)(2,1)S(1)}, u32[]{:S(2)}, u32[]{:S(2)}) %collective-permute-start.5) | collective-permute-done | bytes 589856 | tf_op jit(solution)/shard_map/ppermute | solution.py:106
  287.9 5.5 collective-permute-done.27
  305.7 7.1 collective-permute-done.36
  317.7 10.9 %shard_map.213 = (f32[512,512]{1,0:T(8,128)}, f32[1024,128]{1,0:T(8,128)}) custom-call(s32[4,36]{1,0:T(4,128)} %pad.4.index_ref, s32[4]{0:T(128)} %get-tuple-element.166.count_ref, bf16[512,512]{1,0:T(8,128)(2,1)} %fusion.78.q_ref, bf16[4096,256]{1,0:T(8,128)(2,1)} %copy-done.83, bf16[4096,256]{1,0:T(8,128)(2,1)} %copy-done.82), custom_call_target="tpu_custom_call" | custom-call | flops 2147483648 | bytes 6291456 | tf_op jit(solution)/shard_map/pallas_call | solution.py:239
  338.9 9.2 collective-permute-done.55
  358.3 7.7 collective-permute-done.56
  367.6 11.8 %collective-permute-start.57 = (bf16[128,2304]{1,0:T(8,128)(2,1)S(1)}, bf16[128,2304]{1,0:T(8,128)(2,1)S(1)}, u32[]{:S(2)}, u32[]{:S(2)}) collective-permute-start(bf16[128,2304]{1,0:T(8,128)(2,1)S(1)} %get-tuple-element.79), channel_id=1, source_target_pairs={{0,1},{1,2},{2,3},{4,5},{5,6},{6,7},{8,9},{9,10},{10,11},{12,13},{... | collective-permute-start | bytes 1769480 | tf_op jit(solution)/shard_map/ppermute | solution.py:106
  381.2 7.5 collective-permute-done.60
  393.6 5.1 collective-permute-start.62
  398.8 9.9 collective-permute-done.61
  412.5 11.2 %collective-permute-done.65 = bf16[128,2304]{1,0:T(8,128)(2,1)S(1)} collective-permute-done((bf16[128,2304]{1,0:T(8,128)(2,1)S(1)}, bf16[128,2304]{1,0:T(8,128)(2,1)S(1)}, u32[]{:S(2)}, u32[]{:S(2)}) %collective-permute-start.65) | collective-permute-done | bytes 589856 | tf_op jit(solution)/shard_map/ppermute | solution.py:106
  426.0 11.9 %collective-permute-done.66 = bf16[128,2304]{1,0:T(8,128)(2,1)S(1)} collective-permute-done((bf16[128,2304]{1,0:T(8,128)(2,1)S(1)}, bf16[128,2304]{1,0:T(8,128)(2,1)S(1)}, u32[]{:S(2)}, u32[]{:S(2)}) %collective-permute-start.66) | collective-permute-done | bytes 589856 | tf_op jit(solution)/shard_map/ppermute | solution.py:106
  438.1 12.9 %fusion.193 = f32[512,2304]{1,0:T(8,128)} fusion(bf16[2304,2304]{1,0:T(8,128)(2,1)} %constant_dynamic-update-slice_fusion.51, bf16[128,2304]{1,0:T(8,128)(2,1)S(1)} %broadcast_select_fusion.2, bf16[128,2304]{1,0:T(8,128)(2,1)S(1)} %broadcast_select_fusion.6, bf16[128,2304]{1,0:T(8,128)(2,1)S(1)} %broadcast_select_fusion.10, ...), kind=kOutput, calls=%fused_computation.574 | convolution fusion | flops 5445255168 | bytes 17694720 | tf_op jit(solution)/shard_map/dot_general | solution.py:23
  451.0 10.6 %multiply_convert_fusion.1 = (bf16[512,2304]{1,0:T(8,128)(2,1)S(1)}, f32[512,2304]{1,0:T(8,128)}) fusion(f32[512,2304]{1,0:T(8,128)} %fusion.193, bf16[2304,2304]{1,0:T(8,128)(2,1)S(1)} %constant_dynamic-update-slice_fusion.66, bf16[128,2304]{1,0:T(8,128)(2,1)S(1)} %broadcast_select_fusion.2, bf16[128,2304]{1,0:T(8,128)(2,1)S(1)} %broadcast_select_fusion.6, ...), kind=kOutput, calls=%fused_computation.31 | convolution fusion | flops 5457051648 | bytes 24772608 | tf_op jit(solution)/shard_map/dot_general | solution.py:23
  461.6 10.8 %convolution_convert_fusion.12 = bf16[512,2304]{1,0:T(8,128)(2,1)S(1)} fusion(bf16[512,2304]{1,0:T(8,128)(2,1)S(1)} %get-tuple-element.170, bf16[2304,2304]{1,0:T(8,128)(2,1)} %constant_dynamic-update-slice_fusion.81), kind=kOutput, calls=%fused_computation.32 | convolution fusion | flops 5436997632 | bytes 15335424 | tf_op jit(solution)/shard_map/dot_general | solution.py:27
  474.7 8.2 collective-permute-done.109
  488.3 7.3 collective-permute-done.110
  498.2 10.0 collective-permute-start.111
  523.2 5.8 collective-permute-start.116
  529.1 9.2 collective-permute-done.115
  546.8 9.3 collective-permute-done.119
  559.5 8.6 collective-permute-done.120
  569.3 14.5 %fusion.11 = (bf16[512,2304]{1,0:T(8,128)(2,1)S(1)}, bf16[512,2304]{1,0:T(8,128)(2,1)S(1)}) fusion(f32[512,2304]{1,0:T(8,128)} %fusion.193, f32[512,2304]{1,0:T(8,128)} %get-tuple-element.171, bf16[2304,2304]{1,0:T(8,128)(2,1)} %constant_dynamic-update-slice_fusion.81, bf16[128,2304]{1,0:T(8,128)(2,1)S(1)} %broadcast_select_fusion.1, ...), kind=kOutput, calls=%fused_computation.29 | convolution fusion | flops 5472387072 | bytes 27131904 | tf_op jit(solution)/shard_map/dot_general | solution.py:23
  593.6 11.4 %fusion.208 = f32[512,2304]{1,0:T(8,128)} fusion(bf16[512,2304]{1,0:T(8,128)(2,1)S(1)} %get-tuple-element.40, bf16[2304,2304]{1,0:T(8,128)(2,1)} %copy-done.70), kind=kOutput, calls=%fused_computation.587 | convolution fusion | flops 5435817984 | bytes 17694720 | tf_op jit(solution)/shard_map/dot_general | solution.py:27
  604.9 11.4 %fusion.12 = bf16[512,2304]{1,0:T(8,128)(2,1)S(1)} fusion(f32[512,2304]{1,0:T(8,128)} %fusion.208, bf16[512,2304]{1,0:T(8,128)(2,1)} %copy-done.104, bf16[2304,2304]{1,0:T(8,128)(2,1)} %constant_dynamic-update-slice_fusion.51), kind=kOutput, calls=%fused_computation.34 | convolution fusion | flops 5438177280 | bytes 20054016 | tf_op jit(solution)/shard_map/dot_general | solution.py:27
  625.0 6.7 collective-permute-done.121
  648.3 14.0 %collective-permute-start.123 = (bf16[128,2304]{1,0:T(8,128)(2,1)S(1)}, bf16[128,2304]{1,0:T(8,128)(2,1)S(1)}, u32[]{:S(2)}, u32[]{:S(2)}) collective-permute-start(bf16[128,2304]{1,0:T(8,128)(2,1)S(1)} %get-tuple-element.67), channel_id=1, source_target_pairs={{0,1},{1,2},{2,3},{4,5},{5,6},{6,7},{8,9},{9,10},{10,11},{12,13},{... | collective-permute-start | bytes 1769480 | tf_op jit(solution)/shard_map/ppermute | solution.py:106
  678.1 9.9 collective-permute-done.127
  699.9 10.4 %collective-permute-done.128 = bf16[128,2304]{1,0:T(8,128)(2,1)S(1)} collective-permute-done((bf16[128,2304]{1,0:T(8,128)(2,1)S(1)}, bf16[128,2304]{1,0:T(8,128)(2,1)S(1)}, u32[]{:S(2)}, u32[]{:S(2)}) %collective-permute-start.128) | collective-permute-done | bytes 589856 | tf_op jit(solution)/shard_map/ppermute | solution.py:106
  720.5 6.8 collective-permute-done.131
  738.4 21.8 %collective-permute-done.185 = bf16[288,1152]{1,0:T(8,128)(2,1)S(1)} collective-permute-done((bf16[288,1152]{1,0:T(8,128)(2,1)S(1)}, bf16[288,1152]{1,0:T(8,128)(2,1)S(1)}, u32[]{:S(2)}, u32[]{:S(2)}) %collective-permute-start.185) | collective-permute-done | bytes 663584 | tf_op jit(solution)/shard_map/ppermute | solution.py:45
  764.4 22.4 %collective-permute-done.193 = bf16[288,1152]{1,0:T(8,128)(2,1)S(1)} collective-permute-done((bf16[288,1152]{1,0:T(8,128)(2,1)S(1)}, bf16[288,1152]{1,0:T(8,128)(2,1)S(1)}, u32[]{:S(2)}, u32[]{:S(2)}) %collective-permute-start.193) | collective-permute-done | bytes 663584 | tf_op jit(solution)/shard_map/ppermute | solution.py:45
  791.0 14.1 %collective-permute-done.132 = bf16[128,2304]{1,0:T(8,128)(2,1)S(1)} collective-permute-done((bf16[128,2304]{1,0:T(8,128)(2,1)S(1)}, bf16[128,2304]{1,0:T(8,128)(2,1)S(1)}, u32[]{:S(2)}, u32[]{:S(2)}) %collective-permute-start.132) | collective-permute-done | bytes 589856 | tf_op jit(solution)/shard_map/ppermute | solution.py:106
  809.5 20.1 %shard_map.214 = (bf16[512,512]{1,0:T(8,128)(2,1)}, f32[4096,256]{1,0:T(8,128)}, f32[4096,256]{1,0:T(8,128)}) custom-call(s32[4,36]{1,0:T(4,128)} %pad.4.index_ref, s32[4]{0:T(128)} %get-tuple-element.166.count_ref, bf16[512,512]{1,0:T(8,128)(2,1)} %fusion.78.q_ref, bf16[512,512]{1,0:T(8,128)(2,1)} %convolution_convert_fusion.26.dout_ref, ...), custom_call_target="tpu_custom_call" | custom-call | flops 5368709120 | bytes 16777216 | tf_op jit(solution)/shard_map/pallas_call | solution.py:261
  849.9 22.9 %collective-permute-done.186 = bf16[288,1152]{1,0:T(8,128)(2,1)S(1)} collective-permute-done((bf16[288,1152]{1,0:T(8,128)(2,1)S(1)}, bf16[288,1152]{1,0:T(8,128)(2,1)S(1)}, u32[]{:S(2)}, u32[]{:S(2)}) %collective-permute-start.186) | collective-permute-done | bytes 663584 | tf_op jit(solution)/shard_map/ppermute | solution.py:45
  880.6 16.2 %collective-permute-done.194 = bf16[288,1152]{1,0:T(8,128)(2,1)S(1)} collective-permute-done((bf16[288,1152]{1,0:T(8,128)(2,1)S(1)}, bf16[288,1152]{1,0:T(8,128)(2,1)S(1)}, u32[]{:S(2)}, u32[]{:S(2)}) %collective-permute-start.194) | collective-permute-done | bytes 663584 | tf_op jit(solution)/shard_map/ppermute | solution.py:45
  980.3 6.8 collective-permute-done.200
  1010.0 6.7 collective-permute-start.143
  (845 shorter events, 490.9 us)
Async XLA Ops:
  0.7 23.0 %collective-permute-start.6 = (bf16[4,288]{1,0:T(4,128)(2,1)}, bf16[4,288]{1,0:T(4,128)(2,1)S(1)}, u32[]{:S(2)}, u32[]{:S(2)}) collective-permute-start(bf16[4,288]{1,0:T(4,128)(2,1)} %param.23), channel_id=1, source_target_pairs={{0,8},{4,12},{8,0},{12,4},{16,24},{20,28},{24,16},{28,20},{1,9},{5... | collective-permute-start | bytes 6920 | tf_op jit(solution)/shard_map/ppermute | solution.py:45
  3.7 23.3 %collective-permute-start.7 = (bf16[4,288]{1,0:T(4,128)(2,1)}, bf16[4,288]{1,0:T(4,128)(2,1)S(1)}, u32[]{:S(2)}, u32[]{:S(2)}) collective-permute-start(bf16[4,288]{1,0:T(4,128)(2,1)} %param.23), channel_id=1, source_target_pairs={{0,16},{4,20},{8,24},{12,28},{16,0},{20,4},{24,8},{28,12},{1,17},{... | collective-permute-start | bytes 6920 | tf_op jit(solution)/shard_map/ppermute | solution.py:45
  7.6 86.8 %collective-permute-start.67 = (bf16[144,2304]{1,0:T(8,128)(2,1)}, bf16[144,2304]{1,0:T(8,128)(2,1)S(1)}, u32[]{:S(2)}, u32[]{:S(2)}) collective-permute-start(bf16[144,2304]{1,0:T(8,128)(2,1)} %get-tuple-element.88), channel_id=1, source_target_pairs={{0,8},{4,12},{8,0},{12,4},{16,24},{20,28},{24,16},{28,20},{1,9},{5... | collective-permute-start | bytes 1990664 | tf_op jit(solution)/shard_map/ppermute | solution.py:45
  27.0 85.5 %collective-permute-start.69 = (bf16[144,2304]{1,0:T(8,128)(2,1)}, bf16[144,2304]{1,0:T(8,128)(2,1)S(1)}, u32[]{:S(2)}, u32[]{:S(2)}) collective-permute-start(bf16[144,2304]{1,0:T(8,128)(2,1)} %get-tuple-element.88), channel_id=1, source_target_pairs={{0,16},{4,20},{8,24},{12,28},{16,0},{20,4},{24,8},{28,12},{1,17},{... | collective-permute-start | bytes 1990664 | tf_op jit(solution)/shard_map/ppermute | solution.py:45
  93.7 118.1 %collective-permute-start.73 = (bf16[144,2304]{1,0:T(8,128)(2,1)}, bf16[144,2304]{1,0:T(8,128)(2,1)S(1)}, u32[]{:S(2)}, u32[]{:S(2)}) collective-permute-start(bf16[144,2304]{1,0:T(8,128)(2,1)} %get-tuple-element.88), channel_id=1, source_target_pairs={{0,4},{4,0},{8,12},{12,8},{16,20},{20,16},{24,28},{28,24},{1,5},{5... | collective-permute-start | bytes 1990664 | tf_op jit(solution)/shard_map/ppermute | solution.py:45
  94.4 81.5 %collective-permute-start = (bf16[128,2304]{1,0:T(8,128)(2,1)S(1)}, bf16[128,2304]{1,0:T(8,128)(2,1)S(1)}, u32[]{:S(2)}, u32[]{:S(2)}) collective-permute-start(bf16[128,2304]{1,0:T(8,128)(2,1)S(1)} %concatenate.81), channel_id=1, source_target_pairs={{1,0},{2,1},{3,2},{5,4},{6,5},{7,6},{9,8},{10,9},{11,10},{13,12},{... | collective-permute-start | bytes 1769480 | tf_op jit(solution)/shard_map/ppermute | solution.py:106
  108.1 68.3 %collective-permute-start.1 = (bf16[128,2304]{1,0:T(8,128)(2,1)S(1)}, bf16[128,2304]{1,0:T(8,128)(2,1)S(1)}, u32[]{:S(2)}, u32[]{:S(2)}) collective-permute-start(bf16[128,2304]{1,0:T(8,128)(2,1)S(1)} %concatenate.81), channel_id=1, source_target_pairs={{0,1},{1,2},{2,3},{4,5},{5,6},{6,7},{8,9},{9,10},{10,11},{12,13},{... | collective-permute-start | bytes 1769480 | tf_op jit(solution)/shard_map/ppermute | solution.py:106
  114.0 28.5 %collective-permute-start.82 = (bf16[144,2304]{1,0:T(8,128)(2,1)S(1)}, bf16[144,2304]{1,0:T(8,128)(2,1)S(1)}, u32[]{:S(2)}, u32[]{:S(2)}) collective-permute-start(bf16[144,2304]{1,0:T(8,128)(2,1)S(1)} %copy-done.48), channel_id=1, source_target_pairs={{0,8},{4,12},{8,0},{12,4},{16,24},{20,28},{24,16},{28,20},{1,9},{5... | collective-permute-start | bytes 1990664 | tf_op jit(solution)/shard_map/ppermute | solution.py:45
  188.7 24.0 %collective-permute-start.74 = (bf16[144,2304]{1,0:T(8,128)(2,1)S(1)}, bf16[144,2304]{1,0:T(8,128)(2,1)S(1)}, u32[]{:S(2)}, u32[]{:S(2)}) collective-permute-start(bf16[144,2304]{1,0:T(8,128)(2,1)S(1)} %copy-done.50), channel_id=1, source_target_pairs={{0,4},{4,0},{8,12},{12,8},{16,20},{20,16},{24,28},{28,24},{1,5},{5... | collective-permute-start | bytes 1990664 | tf_op jit(solution)/shard_map/ppermute | solution.py:45
  188.7 46.9 %collective-permute-start.87 = (bf16[144,2304]{1,0:T(8,128)(2,1)S(1)}, bf16[144,2304]{1,0:T(8,128)(2,1)S(1)}, u32[]{:S(2)}, u32[]{:S(2)}) collective-permute-start(bf16[144,2304]{1,0:T(8,128)(2,1)S(1)} %copy-done.49), channel_id=1, source_target_pairs={{0,4},{4,0},{8,12},{12,8},{16,20},{20,16},{24,28},{28,24},{1,5},{5... | collective-permute-start | bytes 1990664 | tf_op jit(solution)/shard_map/ppermute | solution.py:45
  209.5 27.5 %collective-permute-start.88 = (bf16[144,2304]{1,0:T(8,128)(2,1)S(1)}, bf16[144,2304]{1,0:T(8,128)(2,1)S(1)}, u32[]{:S(2)}, u32[]{:S(2)}) collective-permute-start(bf16[144,2304]{1,0:T(8,128)(2,1)S(1)} %copy-done.48), channel_id=1, source_target_pairs={{0,4},{4,0},{8,12},{12,8},{16,20},{20,16},{24,28},{28,24},{1,5},{5... | collective-permute-start | bytes 1990664 | tf_op jit(solution)/shard_map/ppermute | solution.py:45
  210.4 50.9 %collective-permute-start.101 = (bf16[144,2304]{1,0:T(8,128)(2,1)S(1)}, bf16[144,2304]{1,0:T(8,128)(2,1)S(1)}, u32[]{:S(2)}, u32[]{:S(2)}) collective-permute-start(bf16[144,2304]{1,0:T(8,128)(2,1)S(1)} %copy-done.47), channel_id=1, source_target_pairs={{0,4},{4,0},{8,12},{12,8},{16,20},{20,16},{24,28},{28,24},{1,5},{5... | collective-permute-start | bytes 1990664 | tf_op jit(solution)/shard_map/ppermute | solution.py:45
  233.2 30.2 %collective-permute-start.102 = (bf16[144,2304]{1,0:T(8,128)(2,1)S(1)}, bf16[144,2304]{1,0:T(8,128)(2,1)S(1)}, u32[]{:S(2)}, u32[]{:S(2)}) collective-permute-start(bf16[144,2304]{1,0:T(8,128)(2,1)S(1)} %copy-done.46), channel_id=1, source_target_pairs={{0,4},{4,0},{8,12},{12,8},{16,20},{20,16},{24,28},{28,24},{1,5},{5... | collective-permute-start | bytes 1990664 | tf_op jit(solution)/shard_map/ppermute | solution.py:45
  242.8 92.3 %collective-permute-start.103 = (bf16[144,2304]{1,0:T(8,128)(2,1)S(1)}, bf16[144,2304]{1,0:T(8,128)(2,1)}, u32[]{:S(2)}, u32[]{:S(2)}) collective-permute-start(bf16[144,2304]{1,0:T(8,128)(2,1)S(1)} %collective-permute-done.95), channel_id=1, source_target_pairs={{0,4},{4,0},{8,12},{12,8},{16,20},{20,16},{24,28},{28,24},{1,5},{5... | collective-permute-start | bytes 1990664 | tf_op jit(solution)/shard_map/ppermute | solution.py:45
  256.1 81.8 %collective-permute-start.104 = (bf16[144,2304]{1,0:T(8,128)(2,1)S(1)}, bf16[144,2304]{1,0:T(8,128)(2,1)S(1)}, u32[]{:S(2)}, u32[]{:S(2)}) collective-permute-start(bf16[144,2304]{1,0:T(8,128)(2,1)S(1)} %collective-permute-done.96), channel_id=1, source_target_pairs={{0,4},{4,0},{8,12},{12,8},{16,20},{20,16},{24,28},{28,24},{1,5},{5... | collective-permute-start | bytes 1990664 | tf_op jit(solution)/shard_map/ppermute | solution.py:45
  314.4 38.4 %collective-permute-start.105 = (bf16[144,2304]{1,0:T(8,128)(2,1)S(1)}, bf16[144,2304]{1,0:T(8,128)(2,1)}, u32[]{:S(2)}, u32[]{:S(2)}) collective-permute-start(bf16[144,2304]{1,0:T(8,128)(2,1)S(1)} %collective-permute-done.97), channel_id=1, source_target_pairs={{0,4},{4,0},{8,12},{12,8},{16,20},{20,16},{24,28},{28,24},{1,5},{5... | collective-permute-start | bytes 1990664 | tf_op jit(solution)/shard_map/ppermute | solution.py:45
  314.8 41.3 %collective-permute-start.106 = (bf16[144,2304]{1,0:T(8,128)(2,1)S(1)}, bf16[144,2304]{1,0:T(8,128)(2,1)}, u32[]{:S(2)}, u32[]{:S(2)}) collective-permute-start(bf16[144,2304]{1,0:T(8,128)(2,1)S(1)} %collective-permute-done.98), channel_id=1, source_target_pairs={{0,4},{4,0},{8,12},{12,8},{16,20},{20,16},{24,28},{28,24},{1,5},{5... | collective-permute-start | bytes 1990664 | tf_op jit(solution)/shard_map/ppermute | solution.py:45
  338.0 29.7 %collective-permute-start.79 = (bf16[144,2304]{1,0:T(8,128)(2,1)S(1)}, bf16[144,2304]{1,0:T(8,128)(2,1)S(1)}, u32[]{:S(2)}, u32[]{:S(2)}) collective-permute-start(bf16[144,2304]{1,0:T(8,128)(2,1)S(1)} %collective-permute-done.71), channel_id=1, source_target_pairs={{0,4},{4,0},{8,12},{12,8},{16,20},{20,16},{24,28},{28,24},{1,5},{5... | collective-permute-start | bytes 1990664 | tf_op jit(solution)/shard_map/ppermute | solution.py:45
  348.1 32.2 %collective-permute-start.80 = (bf16[144,2304]{1,0:T(8,128)(2,1)S(1)}, bf16[144,2304]{1,0:T(8,128)(2,1)S(1)}, u32[]{:S(2)}, u32[]{:S(2)}) collective-permute-start(bf16[144,2304]{1,0:T(8,128)(2,1)S(1)} %collective-permute-done.72), channel_id=1, source_target_pairs={{0,4},{4,0},{8,12},{12,8},{16,20},{20,16},{24,28},{28,24},{1,5},{5... | collective-permute-start | bytes 1990664 | tf_op jit(solution)/shard_map/ppermute | solution.py:45
  356.1 37.5 %collective-permute-start.93 = (bf16[144,2304]{1,0:T(8,128)(2,1)S(1)}, bf16[144,2304]{1,0:T(8,128)(2,1)S(1)}, u32[]{:S(2)}, u32[]{:S(2)}) collective-permute-start(bf16[144,2304]{1,0:T(8,128)(2,1)S(1)} %collective-permute-done.85), channel_id=1, source_target_pairs={{0,4},{4,0},{8,12},{12,8},{16,20},{20,16},{24,28},{28,24},{1,5},{5... | collective-permute-start | bytes 1990664 | tf_op jit(solution)/shard_map/ppermute | solution.py:45
  366.0 32.7 %collective-permute-start.94 = (bf16[144,2304]{1,0:T(8,128)(2,1)S(1)}, bf16[144,2304]{1,0:T(8,128)(2,1)S(1)}, u32[]{:S(2)}, u32[]{:S(2)}) collective-permute-start(bf16[144,2304]{1,0:T(8,128)(2,1)S(1)} %collective-permute-done.86), channel_id=1, source_target_pairs={{0,4},{4,0},{8,12},{12,8},{16,20},{20,16},{24,28},{28,24},{1,5},{5... | collective-permute-start | bytes 1990664 | tf_op jit(solution)/shard_map/ppermute | solution.py:45
  366.3 22.4 %collective-permute-start.60 = (bf16[128,2304]{1,0:T(8,128)(2,1)S(1)}, bf16[128,2304]{1,0:T(8,128)(2,1)S(1)}, u32[]{:S(2)}, u32[]{:S(2)}) collective-permute-start(bf16[128,2304]{1,0:T(8,128)(2,1)S(1)} %get-tuple-element.80), channel_id=1, source_target_pairs={{1,0},{2,1},{3,2},{5,4},{6,5},{7,6},{9,8},{10,9},{11,10},{13,12},{... | collective-permute-start | bytes 1769480 | tf_op jit(solution)/shard_map/ppermute | solution.py:106
  380.3 30.4 %collective-permute-start.107 = (bf16[144,2304]{1,0:T(8,128)(2,1)S(1)}, bf16[144,2304]{1,0:T(8,128)(2,1)S(1)}, u32[]{:S(2)}, u32[]{:S(2)}) collective-permute-start(bf16[144,2304]{1,0:T(8,128)(2,1)S(1)} %collective-permute-done.99), channel_id=1, source_target_pairs={{0,4},{4,0},{8,12},{12,8},{16,20},{20,16},{24,28},{28,24},{1,5},{5... | collective-permute-start | bytes 1990664 | tf_op jit(solution)/shard_map/ppermute | solution.py:45
  388.7 22.9 %collective-permute-start.108 = (bf16[144,2304]{1,0:T(8,128)(2,1)}, bf16[144,2304]{1,0:T(8,128)(2,1)S(1)}, u32[]{:S(2)}, u32[]{:S(2)}) collective-permute-start(bf16[144,2304]{1,0:T(8,128)(2,1)} %collective-permute-done.100), channel_id=1, source_target_pairs={{0,4},{4,0},{8,12},{12,8},{16,20},{20,16},{24,28},{28,24},{1,5},{5... | collective-permute-start | bytes 1990664 | tf_op jit(solution)/shard_map/ppermute | solution.py:45
  664.1 28.9 %collective-permute-start.175 = (bf16[4,288,1152]{2,1,0:T(8,128)(2,1)}, bf16[4,288,1152]{2,1,0:T(8,128)(2,1)S(1)}, u32[]{:S(2)}, u32[]{:S(2)}) collective-permute-start(bf16[4,288,1152]{2,1,0:T(8,128)(2,1)} %bitcast.48), channel_id=1, source_target_pairs={{0,4},{4,0},{8,12},{12,8},{16,20},{20,16},{24,28},{28,24},{1,5},{5... | collective-permute-start | bytes 7962632 | tf_op jit(solution)/shard_map/ppermute | solution.py:45
  664.2 29.4 %collective-permute-start.171 = (bf16[4,288,1152]{2,1,0:T(8,128)(2,1)S(1)}, bf16[4,288,1152]{2,1,0:T(8,128)(2,1)S(1)}, u32[]{:S(2)}, u32[]{:S(2)}) collective-permute-start(bf16[4,288,1152]{2,1,0:T(8,128)(2,1)S(1)} %bitcast.330), channel_id=1, source_target_pairs={{0,4},{4,0},{8,12},{12,8},{16,20},{20,16},{24,28},{28,24},{1,5},{5... | collective-permute-start | bytes 7962632 | tf_op jit(solution)/shard_map/ppermute | solution.py:45
  664.7 47.3 %collective-permute-start.183 = (bf16[4,288,1152]{2,1,0:T(8,128)(2,1)}, bf16[4,288,1152]{2,1,0:T(8,128)(2,1)S(1)}, u32[]{:S(2)}, u32[]{:S(2)}) collective-permute-start(bf16[4,288,1152]{2,1,0:T(8,128)(2,1)} %bitcast.58), channel_id=1, source_target_pairs={{0,4},{4,0},{8,12},{12,8},{16,20},{20,16},{24,28},{28,24},{1,5},{5... | collective-permute-start | bytes 7962632 | tf_op jit(solution)/shard_map/ppermute | solution.py:45
  667.8 46.1 %collective-permute-start.179 = (bf16[4,288,1152]{2,1,0:T(8,128)(2,1)}, bf16[4,288,1152]{2,1,0:T(8,128)(2,1)S(1)}, u32[]{:S(2)}, u32[]{:S(2)}) collective-permute-start(bf16[4,288,1152]{2,1,0:T(8,128)(2,1)} %bitcast.331), channel_id=1, source_target_pairs={{0,4},{4,0},{8,12},{12,8},{16,20},{20,16},{24,28},{28,24},{1,5},{5... | collective-permute-start | bytes 7962632 | tf_op jit(solution)/shard_map/ppermute | solution.py:45
  688.0 28.1 %collective-permute-start.191 = (bf16[4,288,1152]{2,1,0:T(8,128)(2,1)}, bf16[4,288,1152]{2,1,0:T(8,128)(2,1)S(1)}, u32[]{:S(2)}, u32[]{:S(2)}) collective-permute-start(bf16[4,288,1152]{2,1,0:T(8,128)(2,1)} %bitcast.68), channel_id=1, source_target_pairs={{0,4},{4,0},{8,12},{12,8},{16,20},{20,16},{24,28},{28,24},{1,5},{5... | collective-permute-start | bytes 7962632 | tf_op jit(solution)/shard_map/ppermute | solution.py:45
  693.1 25.2 %collective-permute-start.187 = (bf16[4,288,1152]{2,1,0:T(8,128)(2,1)}, bf16[4,288,1152]{2,1,0:T(8,128)(2,1)S(1)}, u32[]{:S(2)}, u32[]{:S(2)}) collective-permute-start(bf16[4,288,1152]{2,1,0:T(8,128)(2,1)} %bitcast.63), channel_id=1, source_target_pairs={{0,4},{4,0},{8,12},{12,8},{16,20},{20,16},{24,28},{28,24},{1,5},{5... | collective-permute-start | bytes 7962632 | tf_op jit(solution)/shard_map/ppermute | solution.py:45
  716.1 124.6 %collective-permute-start.176 = (bf16[288,1152]{1,0:T(8,128)(2,1)}, bf16[288,1152]{1,0:T(8,128)(2,1)}, u32[]{:S(2)}, u32[]{:S(2)}) collective-permute-start(bf16[288,1152]{1,0:T(8,128)(2,1)} %get-tuple-element.51), channel_id=1, source_target_pairs={{0,8},{4,12},{8,0},{12,4},{16,24},{20,28},{24,16},{28,20},{1,9},{5... | collective-permute-start | bytes 1990664 | tf_op jit(solution)/shard_map/ppermute | solution.py:45
  727.3 117.3 %collective-permute-start.172 = (bf16[288,1152]{1,0:T(8,128)(2,1)}, bf16[288,1152]{1,0:T(8,128)(2,1)}, u32[]{:S(2)}, u32[]{:S(2)}) collective-permute-start(bf16[288,1152]{1,0:T(8,128)(2,1)} %get-tuple-element.49), channel_id=1, source_target_pairs={{0,16},{4,20},{8,24},{12,28},{16,0},{20,4},{24,8},{28,12},{1,17},{... | collective-permute-start | bytes 1990664 | tf_op jit(solution)/shard_map/ppermute | solution.py:45
  728.4 31.7 %collective-permute-start.185 = (bf16[288,1152]{1,0:T(8,128)(2,1)S(1)}, bf16[288,1152]{1,0:T(8,128)(2,1)S(1)}, u32[]{:S(2)}, u32[]{:S(2)}) collective-permute-start(bf16[288,1152]{1,0:T(8,128)(2,1)S(1)} %get-tuple-element.48), channel_id=1, source_target_pairs={{0,8},{4,12},{8,0},{12,4},{16,24},{20,28},{24,16},{28,20},{1,9},{5... | collective-permute-start | bytes 1990664 | tf_op jit(solution)/shard_map/ppermute | solution.py:45
  731.7 117.1 %collective-permute-start.184 = (bf16[288,1152]{1,0:T(8,128)(2,1)}, bf16[288,1152]{1,0:T(8,128)(2,1)}, u32[]{:S(2)}, u32[]{:S(2)}) collective-permute-start(bf16[288,1152]{1,0:T(8,128)(2,1)} %get-tuple-element.47), channel_id=1, source_target_pairs={{0,8},{4,12},{8,0},{12,4},{16,24},{20,28},{24,16},{28,20},{1,9},{5... | collective-permute-start | bytes 1990664 | tf_op jit(solution)/shard_map/ppermute | solution.py:45
  736.1 26.2 %collective-permute-start.181 = (bf16[288,1152]{1,0:T(8,128)(2,1)S(1)}, bf16[288,1152]{1,0:T(8,128)(2,1)S(1)}, u32[]{:S(2)}, u32[]{:S(2)}) collective-permute-start(bf16[288,1152]{1,0:T(8,128)(2,1)S(1)} %get-tuple-element.46), channel_id=1, source_target_pairs={{0,16},{4,20},{8,24},{12,28},{16,0},{20,4},{24,8},{28,12},{1,17},{... | collective-permute-start | bytes 1990664 | tf_op jit(solution)/shard_map/ppermute | solution.py:45
  760.2 26.6 %collective-permute-start.193 = (bf16[288,1152]{1,0:T(8,128)(2,1)S(1)}, bf16[288,1152]{1,0:T(8,128)(2,1)S(1)}, u32[]{:S(2)}, u32[]{:S(2)}) collective-permute-start(bf16[288,1152]{1,0:T(8,128)(2,1)S(1)} %get-tuple-element.44), channel_id=1, source_target_pairs={{0,8},{4,12},{8,0},{12,4},{16,24},{20,28},{24,16},{28,20},{1,9},{5... | collective-permute-start | bytes 1990664 | tf_op jit(solution)/shard_map/ppermute | solution.py:45
  762.3 26.9 %collective-permute-start.189 = (bf16[288,1152]{1,0:T(8,128)(2,1)S(1)}, bf16[288,1152]{1,0:T(8,128)(2,1)S(1)}, u32[]{:S(2)}, u32[]{:S(2)}) collective-permute-start(bf16[288,1152]{1,0:T(8,128)(2,1)S(1)} %get-tuple-element.42), channel_id=1, source_target_pairs={{0,16},{4,20},{8,24},{12,28},{16,0},{20,4},{24,8},{28,12},{1,17},{... | collective-permute-start | bytes 1990664 | tf_op jit(solution)/shard_map/ppermute | solution.py:45
  805.1 36.8 %collective-permute-start.178 = (bf16[288,1152]{1,0:T(8,128)(2,1)}, bf16[288,1152]{1,0:T(8,128)(2,1)}, u32[]{:S(2)}, u32[]{:S(2)}) collective-permute-start(bf16[288,1152]{1,0:T(8,128)(2,1)} %fusion.41), channel_id=1, source_target_pairs={{0,16},{4,20},{8,24},{12,28},{16,0},{20,4},{24,8},{28,12},{1,17},{... | collective-permute-start | bytes 1990664 | tf_op jit(solution)/shard_map/ppermute | solution.py:45
  806.2 39.6 %collective-permute-start.174 = (bf16[288,1152]{1,0:T(8,128)(2,1)}, bf16[288,1152]{1,0:T(8,128)(2,1)}, u32[]{:S(2)}, u32[]{:S(2)}) collective-permute-start(bf16[288,1152]{1,0:T(8,128)(2,1)} %fusion.47), channel_id=1, source_target_pairs={{0,8},{4,12},{8,0},{12,4},{16,24},{20,28},{24,16},{28,20},{1,9},{5... | collective-permute-start | bytes 1990664 | tf_op jit(solution)/shard_map/ppermute | solution.py:45
  840.8 35.0 %collective-permute-start.180 = (bf16[288,1152]{1,0:T(8,128)(2,1)S(1)}, bf16[288,1152]{1,0:T(8,128)(2,1)S(1)}, u32[]{:S(2)}, u32[]{:S(2)}) collective-permute-start(bf16[288,1152]{1,0:T(8,128)(2,1)S(1)} %copy-done.57), channel_id=1, source_target_pairs={{0,16},{4,20},{8,24},{12,28},{16,0},{20,4},{24,8},{28,12},{1,17},{... | collective-permute-start | bytes 1990664 | tf_op jit(solution)/shard_map/ppermute | solution.py:45
  841.9 31.0 %collective-permute-start.186 = (bf16[288,1152]{1,0:T(8,128)(2,1)S(1)}, bf16[288,1152]{1,0:T(8,128)(2,1)S(1)}, u32[]{:S(2)}, u32[]{:S(2)}) collective-permute-start(bf16[288,1152]{1,0:T(8,128)(2,1)S(1)} %copy-done.54), channel_id=1, source_target_pairs={{0,16},{4,20},{8,24},{12,28},{16,0},{20,4},{24,8},{28,12},{1,17},{... | collective-permute-start | bytes 1990664 | tf_op jit(solution)/shard_map/ppermute | solution.py:45
  844.7 35.4 %collective-permute-start.192 = (bf16[288,1152]{1,0:T(8,128)(2,1)S(1)}, bf16[288,1152]{1,0:T(8,128)(2,1)S(1)}, u32[]{:S(2)}, u32[]{:S(2)}) collective-permute-start(bf16[288,1152]{1,0:T(8,128)(2,1)S(1)} %copy-done.56), channel_id=1, source_target_pairs={{0,8},{4,12},{8,0},{12,4},{16,24},{20,28},{24,16},{28,20},{1,9},{5... | collective-permute-start | bytes 1990664 | tf_op jit(solution)/shard_map/ppermute | solution.py:45
  845.9 31.0 %collective-permute-start.182 = (bf16[288,1152]{1,0:T(8,128)(2,1)S(1)}, bf16[288,1152]{1,0:T(8,128)(2,1)S(1)}, u32[]{:S(2)}, u32[]{:S(2)}) collective-permute-start(bf16[288,1152]{1,0:T(8,128)(2,1)S(1)} %copy-done.53), channel_id=1, source_target_pairs={{0,8},{4,12},{8,0},{12,4},{16,24},{20,28},{24,16},{28,20},{1,9},{5... | collective-permute-start | bytes 1990664 | tf_op jit(solution)/shard_map/ppermute | solution.py:45
  848.8 49.6 %collective-permute-start.188 = (bf16[288,1152]{1,0:T(8,128)(2,1)S(1)}, bf16[288,1152]{1,0:T(8,128)(2,1)S(1)}, u32[]{:S(2)}, u32[]{:S(2)}) collective-permute-start(bf16[288,1152]{1,0:T(8,128)(2,1)S(1)} %copy-done.55), channel_id=1, source_target_pairs={{0,16},{4,20},{8,24},{12,28},{16,0},{20,4},{24,8},{28,12},{1,17},{... | collective-permute-start | bytes 1990664 | tf_op jit(solution)/shard_map/ppermute | solution.py:45
  872.9 23.9 %collective-permute-start.194 = (bf16[288,1152]{1,0:T(8,128)(2,1)S(1)}, bf16[288,1152]{1,0:T(8,128)(2,1)S(1)}, u32[]{:S(2)}, u32[]{:S(2)}) collective-permute-start(bf16[288,1152]{1,0:T(8,128)(2,1)S(1)} %copy-done.52), channel_id=1, source_target_pairs={{0,16},{4,20},{8,24},{12,28},{16,0},{20,4},{24,8},{28,12},{1,17},{... | collective-permute-start | bytes 1990664 | tf_op jit(solution)/shard_map/ppermute | solution.py:45
  875.8 23.2 %collective-permute-start.190 = (bf16[288,1152]{1,0:T(8,128)(2,1)S(1)}, bf16[288,1152]{1,0:T(8,128)(2,1)S(1)}, u32[]{:S(2)}, u32[]{:S(2)}) collective-permute-start(bf16[288,1152]{1,0:T(8,128)(2,1)S(1)} %copy-done.51), channel_id=1, source_target_pairs={{0,8},{4,12},{8,0},{12,4},{16,24},{20,28},{24,16},{28,20},{1,9},{5... | collective-permute-start | bytes 1990664 | tf_op jit(solution)/shard_map/ppermute | solution.py:45
  876.8 66.9 %collective-permute-start.137 = (bf16[4,512,256]{2,1,0:T(8,128)(2,1)S(1)}, bf16[4,512,256]{2,1,0:T(8,128)(2,1)S(1)}, u32[]{:S(2)}, u32[]{:S(2)}) collective-permute-start(bf16[4,512,256]{2,1,0:T(8,128)(2,1)S(1)} %bitcast.325), channel_id=1, source_target_pairs={{0,4},{4,0},{8,12},{12,8},{16,20},{20,16},{24,28},{28,24},{1,5},{5... | collective-permute-start | bytes 3145736 | tf_op jit(solution)/shard_map/ppermute | solution.py:45
  880.1 66.7 %collective-permute-start.133 = (bf16[4,512,256]{2,1,0:T(8,128)(2,1)S(1)}, bf16[4,512,256]{2,1,0:T(8,128)(2,1)S(1)}, u32[]{:S(2)}, u32[]{:S(2)}) collective-permute-start(bf16[4,512,256]{2,1,0:T(8,128)(2,1)S(1)} %bitcast.324), channel_id=1, source_target_pairs={{0,4},{4,0},{8,12},{12,8},{16,20},{20,16},{24,28},{28,24},{1,5},{5... | collective-permute-start | bytes 3145736 | tf_op jit(solution)/shard_map/ppermute | solution.py:45
  (264 other events, 5113.4 us)

commit v2 on v1

v2 whole, which is shorter than its diff:
```python
import functools
import itertools

import jax
import jax.numpy as jnp
from jax import lax
from jax.experimental import pallas as pl
from jax.experimental.pallas import tpu as pltpu
from jax.sharding import PartitionSpec as P

QUERY_HEADS = 8
KEY_VALUE_HEADS = 4
HEAD_SIZE = 256
SCORE_SOFT_LIMIT = 50
BLOCK_TOKENS = 128
EPSILON = 1e-06
KEY_STEP = 4

F32 = jnp.float32
BF16 = jnp.bfloat16


def dot(a, b):
    return jnp.dot(a, b, preferred_element_type=F32)


def dot_back(a, b):
    return lax.dot_general(a, b, (((1,), (1,)), ((), ())), preferred_element_type=F32)


def dot_rows(a, b):
    return lax.dot_general(a, b, (((0,), (0,)), ((), ())), preferred_element_type=F32)


def inv_rms(v):
    return lax.rsqrt(jnp.mean(v * v, axis=-1, keepdims=True) + EPSILON)


def norm_input_grad(v, s, gain, c):
    cw = c * gain
    return s * cw - v * (s * s * s) * jnp.mean(cw * v, axis=-1, keepdims=True)


def outer_bits(odd):
    size = lax.axis_size("ctx")
    bits = size.bit_length() - 1
    assert size == 1 << bits and bits >= 1
    order = list(range(bits - 1, 0, -1))
    return order[::-1] if odd else order


def steps_of_hops():
    return len(outer_bits(0))


def places():
    return list(itertools.product((0, 1), repeat=steps_of_hops()))


def flipped(t, s, value):
    return t[:s] + (value,) + t[s + 1 :]


def distances(odd):
    order = outer_bits(odd)
    return [c + sum(b << o for b, o in zip(t, order)) for c in (0, 1) for t in places()]


def owners():
    ctx = lax.axis_index("ctx")
    rel = jnp.where(ctx % 2 == 0, jnp.array(distances(0), jnp.int32), jnp.array(distances(1), jnp.int32))
    return ctx ^ rel


def tie(x, earlier):
    return lax.optimization_barrier((x, earlier))[0]


def tie_all(x, earlier):
    for e in earlier:
        x = tie(x, e)
    return x


def cut_rows(x, count):
    rows = x.shape[0] // count
    return [x[i * rows : (i + 1) * rows] for i in range(count)]


class Lanes:
    def __init__(self):
        self.sent = {"far": [], "near": []}
        self.depth = {"far": 2, "near": 1}

    def send(self, lane, x, pairs, after=()):
        done, depth = self.sent[lane], self.depth[lane]
        if len(done) >= depth:
            x = tie(x, done[-depth])
        x = tie_all(x, after)
        done.append(lax.ppermute(x, "ctx", pairs))
        return done[-1]

    def hop(self, x, s, after):
        orders = outer_bits(0), outer_bits(1)
        return self.send("far", x, [(i, i ^ (1 << orders[i % 2][s])) for i in range(lax.axis_size("ctx"))], after)

    def near(self, x):
        return self.send("near", x, [(i, i ^ 1) for i in range(lax.axis_size("ctx"))])


class Gather:
    def __init__(self, lanes, x):
        self.lanes, self.held, self.other = lanes, {(0,) * steps_of_hops(): x}, {}
        self.todo, self.after = self.plan(), ()

    def plan(self):
        held = self.held
        for s in range(steps_of_hops()):
            for t in list(held):
                held[flipped(t, s, 1)] = self.lanes.hop(held[t], s, self.after)
                self.after = ()
                yield

    def step(self, count=1, after=()):
        self.after = after
        for _ in range(count):
            next(self.todo, None)
        return self

    def pieces(self):
        for _ in self.todo:
            pass
        for t, v in self.held.items():
            self.other[t[::-1]] = self.lanes.near(v)
        return [half[t] for half in (self.held, self.other) for t in places()]

    def rows(self):
        return jnp.concatenate(self.pieces(), axis=0)


class Scatter:
    def __init__(self, lanes, sent, kept, after=()):
        self.lanes, self.came = lanes, []
        lanes.depth = {"far": 1, "near": 4}
        self.got = [lanes.near(tie_all(v.astype(BF16), after)) for v in sent]
        spots = places()
        back = [spots.index(t[::-1]) for t in spots]
        pairs = [(kept[i], self.got[back[i]]) for i in range(len(spots))]
        self.now = {t: k.astype(F32) + g.astype(F32) for t, (k, g) in zip(spots, pairs)}
        self.pack()

    def pack(self):
        self.gone = [t for t in self.now if t[len(self.came)]]
        self.out = jnp.concatenate([self.now[t].astype(BF16) for t in self.gone], axis=0)

    def hop(self, after=()):
        s = len(self.came)
        came = self.lanes.hop(self.out, s, after)
        self.came.append(came)
        parts = dict(zip(self.gone, cut_rows(came, len(self.gone))))
        self.now = {t: v + parts[flipped(t, s, 1)].astype(F32) for t, v in self.now.items() if not t[s]}
        if s + 1 < steps_of_hops():
            self.pack()
        return self

    def result(self):
        while len(self.came) < steps_of_hops():
            self.hop()
        (value,) = self.now.values()
        return value


def owner_at(p):
    ctx = lax.axis_index("ctx")
    return ctx ^ jnp.where(ctx % 2 == 0, distances(0)[p], distances(1)[p])


def scatter_grad(lanes, left, right, after=()):
    size = lax.axis_size("ctx")
    chunk = left.shape[1] // size
    part = dot_rows(left, right).astype(BF16)
    half = [owner_at(n) // 2 for n in range(size // 2)]
    core = lax.axis_index("ctx") % 2

    def chunks(side):
        return [lax.dynamic_slice_in_dim(part, (2 * at + side) * chunk, chunk, 0) for at in half]

    return Scatter(lanes, chunks(1 - core), chunks(core), after)


def gather_tp(x, axis=0):
    return lax.all_gather(x, "tp", axis=axis, tiled=True)


def scatter_tp(part):
    return lax.psum_scatter(part.astype(BF16), "tp", scatter_dimension=0, tiled=True).astype(F32)


def gather_line(x, axis=0, steps=None):
    size, me = lax.axis_size("tp"), lax.axis_index("tp")
    up, down = x, x
    ups, downs = {}, {}
    for s in range(1, size):
        up = lax.ppermute(up, "tp", [(i, i + 1) for i in range(s - 1, size - 1)])
        down = lax.ppermute(down, "tp", [(i, i - 1) for i in range(1, size - s + 1)])
        ups[s], downs[s] = up, down
        if steps is not None:
            steps.append([up, down])
    length = x.shape[axis]
    shape = x.shape[:axis] + (size * length,) + x.shape[axis + 1 :]
    out = lax.dynamic_update_slice_in_dim(jnp.zeros(shape, x.dtype), x, me * length, axis)
    for s in range(1, size):
        came = jnp.where(me >= s, ups[s], downs[size - s])
        out = lax.dynamic_update_slice_in_dim(out, came, (me - s + size) % size * length, axis)
    return out


def exchange_tp(take, axis):
    size, me = lax.axis_size("tp"), lax.axis_index("tp")
    came = [take(me)] + [None] * (size - 1)
    for r in sorted(range(1, size), key=lambda r: -min(r, size - r)):
        came[size - r] = lax.ppermute(take((me + r) % size), "tp", [(i, (i + r) % size) for i in range(size)])
    length = came[0].shape[axis]
    turned = jnp.concatenate(came + came[:-1], axis=axis)
    return lax.dynamic_slice_in_dim(turned, (size - me) % size * length, size * length, axis)


def take_blocks(ref, index_ref, query_block, step, blocks):
    places = [index_ref[query_block, step * KEY_STEP + j] for j in range(KEY_STEP)]
    starts = [pl.multiple_of(p * BLOCK_TOKENS, BLOCK_TOKENS) for p in places]
    return starts, jnp.concatenate([ref[pl.ds(s, BLOCK_TOKENS), :] for s in starts], axis=0)


def stack_heads(x):
    heads = x.shape[1] // HEAD_SIZE
    return jnp.concatenate([x[:, h * HEAD_SIZE : (h + 1) * HEAD_SIZE] for h in range(heads)], axis=0)


def unstack_heads(x):
    rows = BLOCK_TOKENS
    return jnp.concatenate([x[h * rows : (h + 1) * rows] for h in range(x.shape[0] // rows)], axis=1)


def attend_kernel(index_ref, count_ref, q_ref, k_ref, v_ref, out_ref, total_ref, acc_ref):
    i = pl.program_id(0)
    count = count_ref[i]
    q = stack_heads(q_ref[...])
    acc_ref[...] = jnp.zeros_like(acc_ref)
    total_ref[...] = jnp.zeros_like(total_ref)

    def body(step, carry):
        starts, keys = take_blocks(k_ref, index_ref, i, step, KEY_STEP)
        values = jnp.concatenate([v_ref[pl.ds(s, BLOCK_TOKENS), :] for s in starts], axis=0)
        scores = dot_back(q, keys)
        grown = jnp.exp(SCORE_SOFT_LIMIT * jnp.tanh(scores * (1.0 / SCORE_SOFT_LIMIT)))
        pieces = []
        for j in range(KEY_STEP):
            seen = (step * KEY_STEP + j) < count
            piece = grown[:, j * BLOCK_TOKENS : (j + 1) * BLOCK_TOKENS]
            pieces.append(jnp.where(seen, piece, 0.0))
        total_ref[...] += functools.reduce(jnp.add, pieces)
        acc_ref[...] += dot(jnp.concatenate(pieces, axis=1).astype(BF16), values)
        return carry

    lax.fori_loop(0, (count + KEY_STEP - 1) // KEY_STEP, body, 0)
    totals = jnp.sum(total_ref[...], axis=1, keepdims=True)
    total_ref[...] = jnp.broadcast_to(totals, total_ref.shape)
    out_ref[...] = unstack_heads(acc_ref[...] / totals)


def attend_back_kernel(
    index_ref, count_ref, q_ref, dout_ref, out_ref, total_ref, k_ref, v_ref, dq_ref, dkv_ref, acc_ref
):
    i = pl.program_id(0)

    @pl.when(i == 0)
    def _():
        dkv_ref[...] = jnp.zeros_like(dkv_ref)

    count = count_ref[i]
    q = stack_heads(q_ref[...])
    dout = stack_heads(dout_ref[...]).astype(F32)
    inverse = 1.0 / total_ref[:, :1]
    scaled = (dout * inverse).astype(BF16)
    weighted = dout * stack_heads(out_ref[...]) * inverse
    ones = jnp.ones((8, HEAD_SIZE), F32)
    dtotal = -lax.dot_general(
        ones, weighted, (((1,), (1,)), ((), ())), precision=lax.Precision.HIGHEST, preferred_element_type=F32
    )[:1]
    acc_ref[...] = jnp.zeros_like(acc_ref)

    def body(step, carry):
        starts, keys = take_blocks(k_ref, index_ref, i, step, KEY_STEP)
        values = jnp.concatenate([v_ref[pl.ds(s, BLOCK_TOKENS), :] for s in starts], axis=0)
        soft = jnp.tanh(dot_back(keys, q) * (1.0 / SCORE_SOFT_LIMIT))
        grown = jnp.exp(SCORE_SOFT_LIMIT * soft)
        pieces = []
        for j in range(KEY_STEP):
            seen = (step * KEY_STEP + j) < count
            piece = grown[j * BLOCK_TOKENS : (j + 1) * BLOCK_TOKENS]
            pieces.append(jnp.where(seen, piece, 0.0))
        grown = jnp.concatenate(pieces, axis=0)
        dprob = dot_back(values, scaled)
        dscores = (grown * (dprob + dtotal) * (1.0 - soft * soft)).astype(BF16)
        acc_ref[...] += dot_rows(dscores, keys)
        dkeys = dot(dscores, q)
        dvalues = dot(grown.astype(BF16), scaled)
        for j in range(KEY_STEP):
            at = pl.ds(starts[j], BLOCK_TOKENS)
            dkv_ref[at, :HEAD_SIZE] += dkeys[j * BLOCK_TOKENS : (j + 1) * BLOCK_TOKENS]
            dkv_ref[at, HEAD_SIZE:] += dvalues[j * BLOCK_TOKENS : (j + 1) * BLOCK_TOKENS]
        return carry

    lax.fori_loop(0, (count + KEY_STEP - 1) // KEY_STEP, body, 0)
    dq_ref[...] = unstack_heads(acc_ref[...]).astype(BF16)


VMEM_LIMIT = 56 * 1024 * 1024


def whole_spec(rows, columns, at=0):
    return pl.BlockSpec((rows, columns), lambda i, *_: (0, at), pipeline_mode=pl.Buffered(1))


def row_spec(rows, columns):
    return pl.BlockSpec((rows, columns), lambda i, *_: (i, 0))


def attend(index, count, q, kv):
    rows, columns = q.shape
    blocks, stacked = rows // BLOCK_TOKENS, BLOCK_TOKENS * (columns // HEAD_SIZE)
    return pl.pallas_call(
        attend_kernel,
        grid_spec=pltpu.PrefetchScalarGridSpec(
            num_scalar_prefetch=2,
            grid=(blocks,),
            in_specs=[row_spec(BLOCK_TOKENS, columns), whole_spec(kv.shape[0], HEAD_SIZE), whole_spec(kv.shape[0], HEAD_SIZE, 1)],
            out_specs=[row_spec(BLOCK_TOKENS, columns), row_spec(stacked, BLOCK_TOKENS)],
            scratch_shapes=[pltpu.VMEM((stacked, HEAD_SIZE), F32)],
        ),
        out_shape=[
            jax.ShapeDtypeStruct((rows, columns), F32),
            jax.ShapeDtypeStruct((blocks * stacked, BLOCK_TOKENS), F32),
        ],
        compiler_params=pltpu.CompilerParams(vmem_limit_bytes=VMEM_LIMIT),
        cost_estimate=pl.CostEstimate(flops=2 * rows * columns * kv.shape[0], bytes_accessed=6 << 20, transcendentals=0),
    )(index, count, q, kv, kv)


def attend_back(index, count, q, dout, out, totals, kv):
    rows, columns = q.shape
    blocks, stacked = rows // BLOCK_TOKENS, BLOCK_TOKENS * (columns // HEAD_SIZE)
    row = row_spec(BLOCK_TOKENS, columns)
    return pl.pallas_call(
        attend_back_kernel,
        grid_spec=pltpu.PrefetchScalarGridSpec(
            num_scalar_prefetch=2,
            grid=(blocks,),
            in_specs=[row, row, row, row_spec(stacked, BLOCK_TOKENS)]
            + [whole_spec(kv.shape[0], HEAD_SIZE), whole_spec(kv.shape[0], HEAD_SIZE, 1)],
            out_specs=[row, whole_spec(*kv.shape)],
            scratch_shapes=[pltpu.VMEM((stacked, HEAD_SIZE), F32)],
        ),
        out_shape=[
            jax.ShapeDtypeStruct((rows, columns), BF16),
            jax.ShapeDtypeStruct(kv.shape, F32),
        ],
        compiler_params=pltpu.CompilerParams(vmem_limit_bytes=VMEM_LIMIT),
        cost_estimate=pl.CostEstimate(flops=5 * rows * columns * kv.shape[0], bytes_accessed=16 << 20, transcendentals=0),
    )(index, count, q, dout, out, totals, kv, kv)


GELU = 0.7978845608028654
CUBIC = 0.044715
TILE = 256


def ffn_in_kernel(x_ref, gate_w_ref, up_w_ref, gate_ref, up_ref, mid_ref):
    x = x_ref[...]
    gate_pre = dot(x, gate_w_ref[...])
    up_pre = dot(x, up_w_ref[...])
    bend = jnp.tanh(GELU * (gate_pre + CUBIC * gate_pre * gate_pre * gate_pre))
    gate_ref[...] = gate_pre
    up_ref[...] = up_pre
    mid_ref[...] = (0.5 * gate_pre * (1.0 + bend) * up_pre).astype(BF16)


def ffn_in(x, pair_w):
    rows, depth = x.shape
    columns = pair_w.shape[1] // 2
    steps = columns // TILE
    tile = pl.BlockSpec((rows, TILE), lambda i: (0, i))
    return pl.pallas_call(
        ffn_in_kernel,
        grid=(steps,),
        in_specs=[
            pl.BlockSpec((rows, depth), lambda i: (0, 0), pipeline_mode=pl.Buffered(1)),
            pl.BlockSpec((depth, TILE), lambda i: (0, i)),
            pl.BlockSpec((depth, TILE), lambda i: (0, i + steps)),
        ],
        out_specs=[tile] * 3,
        out_shape=[jax.ShapeDtypeStruct((rows, columns), t) for t in (F32, F32, BF16)],
        compiler_params=pltpu.CompilerParams(vmem_limit_bytes=VMEM_LIMIT),
        cost_estimate=pl.CostEstimate(flops=4 * rows * depth * columns, bytes_accessed=4 * depth * columns, transcendentals=0),
        name="ffn_in",
    )(x, pair_w, pair_w)


def ffn_back_kernel(x_ref, gate_ref, up_ref, w_ref, dgate_ref, dup_ref):
    dmid = dot(x_ref[...], w_ref[...])
    gate_pre, up_pre = gate_ref[...], up_ref[...]
    square = gate_pre * gate_pre
    bend = jnp.tanh(GELU * (gate_pre + CUBIC * square * gate_pre))
    slope = 0.5 * (1.0 + bend) + 0.5 * gate_pre * (1.0 - bend * bend) * GELU * (1.0 + 3 * CUBIC * square)
    dgate_ref[...] = (dmid * up_pre * slope).astype(BF16)
    dup_ref[...] = (dmid * (0.5 * gate_pre * (1.0 + bend))).astype(BF16)


def ffn_back(x, gate_pre, up_pre, down_t):
    rows, depth = x.shape
    columns = down_t.shape[1]
    tile = pl.BlockSpec((rows, TILE), lambda i: (0, i))
    return pl.pallas_call(
        ffn_back_kernel,
        grid=(columns // TILE,),
        in_specs=[
            pl.BlockSpec((rows, depth), lambda i: (0, 0), pipeline_mode=pl.Buffered(1)),
            tile,
            tile,
            pl.BlockSpec((depth, TILE), lambda i: (0, i)),
        ],
        out_specs=[tile] * 2,
        out_shape=[jax.ShapeDtypeStruct((rows, columns), BF16)] * 2,
        compiler_params=pltpu.CompilerParams(vmem_limit_bytes=VMEM_LIMIT),
        cost_estimate=pl.CostEstimate(flops=2 * rows * depth * columns, bytes_accessed=2 * depth * columns, transcendentals=0),
        name="ffn_back",
    )(x, gate_pre, up_pre, down_t)


def rows_kernel(terms, *refs):
    xs, w_ref, out_ref = refs[:terms], refs[terms], refs[terms + 1]
    depth = xs[0].shape[1]
    total = 0.0
    for m in range(terms):
        total = total + dot_back(xs[m][...], w_ref[:, m * depth : (m + 1) * depth])
    out_ref[...] = total.astype(BF16)


def rows_call(xs, w, name):
    rows, depth = xs[0].shape
    width, terms = w.shape[0], len(xs)
    return pl.pallas_call(
        functools.partial(rows_kernel, terms),
        grid=(width // TILE,),
        in_specs=[pl.BlockSpec((rows, depth), lambda i: (0, 0), pipeline_mode=pl.Buffered(1))] * terms
        + [pl.BlockSpec((TILE, terms * depth), lambda i: (i, 0))],
        out_specs=pl.BlockSpec((rows, TILE), lambda i: (0, i)),
        out_shape=jax.ShapeDtypeStruct((rows, width), BF16),
        compiler_params=pltpu.CompilerParams(vmem_limit_bytes=VMEM_LIMIT),
        cost_estimate=pl.CostEstimate(
            flops=2 * rows * depth * width * terms, bytes_accessed=2 * depth * width * terms, transcendentals=0
        ),
        name=name,
    )(*xs, w)


def visible_lists(block_mask, block_seq, block_place, per_device):
    tp = lax.axis_size("tp")
    ctx = lax.axis_index("ctx")
    total = block_seq.shape[0]
    owner = owners()
    of_group = tp * per_device
    inner = jnp.arange(of_group, dtype=jnp.int32)
    query_ids = ctx * of_group + inner
    key_ids = (owner[:, None] * of_group + inner[None, :]).reshape(-1)
    every = jnp.arange(total, dtype=jnp.int32)

    def look_up(ids, table):
        return jnp.sum(jnp.where(ids[:, None] == every[None, :], table[None, :], 0), axis=1)

    places = jnp.arange(block_mask.shape[0], dtype=jnp.int32)
    query_pick = (look_up(query_ids, block_place)[:, None] == places[None, :]).astype(F32)
    key_pick = (look_up(key_ids, block_place)[:, None] == places[None, :]).astype(F32)
    hits = dot_back(dot(query_pick, block_mask.astype(F32)), key_pick)
    same = look_up(query_ids, block_seq)[:, None] == look_up(key_ids, block_seq)[None, :]
    seen = (hits > 0.5) & same
    before = (every[:, None] < every[None, :]).astype(F32)
    rank = dot(seen.astype(F32), before).astype(jnp.int32)
    wanted = seen[:, None, :] & (rank[:, None, :] == every[None, :, None])
    index = jnp.sum(jnp.where(wanted, every[None, None, :], 0), axis=2)
    index = jnp.pad(index, ((0, 0), (0, KEY_STEP)))
    return index, jnp.sum(seen.astype(jnp.int32), axis=1)


def gather_small(x):
    size = lax.axis_size("ctx")
    orders = outer_bits(0), outer_bits(1)
    held = {(0,) * steps_of_hops(): x}
    rows = x.shape[0]

    def send(pairs):
        came = lax.ppermute(jnp.concatenate(list(held.values()), axis=0), "ctx", pairs)
        return {t: came[n * rows : (n + 1) * rows] for n, t in enumerate(held)}

    for s in range(steps_of_hops()):
        came = send([(i, i ^ (1 << orders[i % 2][s])) for i in range(size)])
        held |= {flipped(t, s, 1): v for t, v in came.items()}
    other = {t[::-1]: v for t, v in send([(i, i ^ 1) for i in range(size)]).items()}
    blocks = jnp.stack([half[t] for half in (held, other) for t in places()])
    spots = []
    for j in range(size):
        found = [jnp.where(owner_at(p) == j, p, 0) for p in range(size)]
        spots.append(functools.reduce(jnp.add, found))
    return jnp.concatenate([lax.dynamic_index_in_dim(blocks, at, 0, keepdims=False) for at in spots], axis=1)


def sum_gains(terms):
    size, tp, me = lax.axis_size("ctx"), lax.axis_size("tp"), lax.axis_index("tp")
    orders = outer_bits(0), outer_bits(1)
    rows, width = terms.shape
    chunk, half = width // size, size // 2
    spots = places()
    parts = [lax.dynamic_slice_in_dim(terms, owner_at(p) * chunk, chunk, 1) for p in range(size)]

    def send(values, pairs):
        came = lax.ppermute(jnp.concatenate(values, axis=0), "ctx", pairs)
        return [came[n * rows : (n + 1) * rows] for n in range(len(values))]

    came = send(parts[half:], [(i, i ^ 1) for i in range(size)])
    now = {t: parts[n] + came[spots.index(t[::-1])] for n, t in enumerate(spots)}
    for s in range(steps_of_hops()):
        gone = [t for t in now if t[s]]
        came = send([now[t] for t in gone], [(i, i ^ (1 << orders[i % 2][s])) for i in range(size)])
        came = {flipped(t, s, 0): v for t, v in zip(gone, came)}
        now = {t: v + came[t] for t, v in now.items() if not t[s]}
    (mine,) = now.values()
    per = rows // tp

    def rows_of(shift):
        return lax.dynamic_slice_in_dim(mine, ((me + shift) % tp) * per, per, 0)

    total = rows_of(0)
    for shift in range(1, tp):
        total = total + lax.ppermute(rows_of(shift), "tp", [(i, (i + shift) % tp) for i in range(tp)])
    return total


def on_device(
    tokens,
    cotangent,
    w_query,
    key_projection,
    value_projection,
    w_out,
    w_gate,
    w_up,
    w_down,
    norm_gains,
    block_mask,
    block_seq,
    block_place,
):
    per_device = tokens.shape[0] // BLOCK_TOKENS
    scale = HEAD_SIZE ** (-0.5)
    q_cols, kv_cols = w_query.shape[1], key_projection.shape[1]
    in_cols = q_cols + 2 * kv_cols
    lanes = Lanes()

    def gather_weight(w):
        return lax.all_gather(w, "ctx", axis=0, tiled=True)

    wide = gather_weight(jnp.concatenate([w_query, key_projection, value_projection, w_out.T], axis=1))
    gains = 1.0 + gather_small(norm_gains).astype(F32)
    cot = cotangent.astype(F32)
    index, count = visible_lists(block_mask, block_seq, block_place, per_device)

    rows_in = gather_line(tokens)
    pair_w = gather_weight(tie_all(jnp.concatenate([w_gate, w_up], axis=1), [wide, rows_in]))
    half = wide.shape[0] // 2
    core = lax.axis_index("ctx") % 2
    out_half = lax.dynamic_slice_in_dim(wide, core * half, half, 0)[:, in_cols:]
    out_steps, inner_steps = [], []
    out_half = gather_line(tie(out_half, rows_in), axis=1, steps=out_steps)
    wide = wide[:, :in_cols]
    rows_in = rows_in.astype(F32)
    normed = (rows_in * inv_rms(rows_in) * gains[0]).astype(BF16)
    qkv = dot(normed, wide)
    q = (qkv[:, :q_cols] * scale).astype(BF16)
    kv_own = qkv[:, q_cols:].astype(BF16)
    kv = tie_all(Gather(lanes, kv_own).rows(), out_steps[0])

    outcome, totals = attend(index, count, q, kv)
    attended = tie_all(outcome.astype(BF16), out_steps[1])
    rows = tokens.shape[0]
    own_heads = exchange_tp(lambda i: lax.dynamic_slice_in_dim(attended, i * rows, rows, 0), 1)
    out_other = lanes.near(tie(out_half, attended))
    out_t = jnp.zeros((2 * half, out_half.shape[1]), BF16)
    out_t = lax.dynamic_update_slice_in_dim(out_t, out_half, core * half, 0)
    out_t = lax.dynamic_update_slice_in_dim(out_t, out_other, (1 - core) * half, 0)
    branch = dot_back(own_heads, out_t)
    size = lax.axis_size("ctx")

    xf = tokens.astype(F32)
    s_branch = inv_rms(branch)
    hidden = xf + branch * s_branch * gains[1]
    s_hidden = inv_rms(hidden)
    inner = gather_line((hidden * s_hidden * gains[2]).astype(BF16), steps=inner_steps)
    down_t = gather_weight(tie_all(w_down.T, [pair_w] + inner_steps[0]))
    gate_pre, up_pre, mid = ffn_in(inner, pair_w)
    feed = scatter_tp(rows_call([mid], down_t, "ffn_out"))
    s_feed = inv_rms(feed)
    mixed = (hidden + feed * s_feed * gains[3]).astype(BF16)
    term_four = jnp.sum(cot * feed * s_feed, axis=0)
    dfeed = gather_tp(norm_input_grad(feed, s_feed, gains[3], cot).astype(BF16))

    down = scatter_grad(lanes, dfeed, mid)
    dgate, dup = ffn_back(dfeed, gate_pre, up_pre, down_t)
    dinner_part = rows_call([tie(dgate, down.out), dup], pair_w, "ffn_back_in")
    down.hop()
    gate = scatter_grad(lanes, inner, tie(dgate, dinner_part), [down.came[0]])
    down.hop()
    gate.hop()
    dinner = tie_all(scatter_tp(dinner_part), [down.came[1], gate.out])
    down_sum = down.result()
    term_three = jnp.sum(dinner * hidden * s_hidden, axis=0)
    dhidden = cot + norm_input_grad(hidden, s_hidden, gains[2], dinner)
    term_two = jnp.sum(dhidden * branch * s_branch, axis=0)
    dbranch = norm_input_grad(branch, s_branch, gains[1], dhidden).astype(BF16)
    dheads = dot(dbranch, out_t).astype(BF16)
    head_cols = attended.shape[1]
    dattended = exchange_tp(lambda i: lax.dynamic_slice_in_dim(dheads, i * head_cols, head_cols, 1), 0)
    dattended = tie_all(dattended, [gate.came[0]])
    up = scatter_grad(lanes, inner, tie(dup, dheads))
    gate.hop([dheads])
    dbranch = gather_tp(dbranch)

    dq, dkv = attend_back(index, count, q, dattended, outcome, totals, kv)
    dq = dq * jnp.asarray(scale, BF16)
    dkv = tie_all(dkv, [gate.came[1]] + up.got)
    dkv = dkv.reshape(2, size // 2, kv_own.shape[0], 2 * kv_cols)
    dkv_own = Scatter(lanes, dkv[1], dkv[0]).result().astype(BF16)
    up.hop()
    grad_up = up.result()
    grad_gate = gate.result()
    dqkv = jnp.concatenate([dq, dkv_own], axis=1)
    dnormed_part = dot_back(dqkv, wide).astype(BF16)
    grad_out = scatter_grad(lanes, tie(dbranch, dnormed_part), attended).result()
    grad_query = scatter_grad(lanes, normed, tie(dq, dnormed_part)).result()
    term_one = jnp.sum(dnormed_part.astype(F32) * rows_in * inv_rms(rows_in), axis=0)
    grad_kv = scatter_grad(lanes, normed, tie(dkv_own, dnormed_part)).result()
    dnormed = tie_all(scatter_tp(dnormed_part), [grad_up, grad_out])
    grad_gains = sum_gains(jnp.stack([term_one, term_two, term_three, term_four]))
    grad_tokens = dhidden + norm_input_grad(xf, inv_rms(xf), gains[0], dnormed)
    return (
        mixed,
        grad_tokens,
        grad_query,
        grad_kv[:, :kv_cols],
        grad_kv[:, kv_cols:],
        grad_out.T,
        grad_gate,
        grad_up,
        down_sum.T,
        grad_gains,
    )


def solution(mesh):
    rows, weight, turned = P(("ctx", "tp"), None), P("ctx", "tp"), P("tp", "ctx")
    in_specs = (rows, rows, weight, weight, weight, turned, weight, weight, turned, P(None, "ctx"), P(), P(), P())
    out_specs = (rows, rows, weight, weight, weight, turned, weight, weight, turned, turned)
    return jax.shard_map(on_device, mesh=mesh, in_specs=in_specs, out_specs=out_specs, check_vma=False)
```

time: 1040 us -> 761 us (0.73)
  waiting for transfers between devices: 503 us -> 343 us
  starting transfers between devices: 215 us -> 85.5 us
  matrix products: 125 us -> 52.3 us
  Pallas kernels: 30.9 us -> 97.3 us
  other arithmetic: 63.5 us -> 103 us
  local copies, waits for them, and re-layouts: 91.2 us -> 53.4 us
  between operations: 3.27 us -> 16.4 us
    ppermute x198 -> x80, waiting for transfers between devices: 493 us -> 217 us  [the longest x9 103 us: gather_line(): lax.ppermute(down, 'tp', [(i, i - 1) for i in range(1, size - s + 1)])]
    ppermute x198 -> x80, starting transfers between devices: 212 us -> 79.3 us  [the longest x50 22.7 us: send(): done.append(lax.ppermute(x, 'ctx', pairs))]
    reduce_scatter x0 -> x3, waiting for transfers between devices: none -> 67.2 us  [scatter_tp(): lax.psum_scatter(part.astype(BF16), 'tp', scatter_dimension=0, tiled=True)]
    pallas_call x0 -> x4, Pallas kernels: none -> 65.2 us  [the longest x2 30.5 us: rows_call(): pl.pallas_call(functools.partial(rows_kernel, terms), grid=(width // TILE...]
    all_gather x0 -> x5, waiting for transfers between devices: none -> 58.9 us  [the longest x2 49.6 us: gather_tp(): return lax.all_gather(x, 'tp', axis=axis, tiled=True)]
    unnamed x305 -> x176, local copies, waits for them, and re-layouts: 70.1 us -> 21.4 us
    dot_general x6 -> x3, matrix products: 42.9 us -> 10 us  [dot(): return jnp.dot(a, b, preferred_element_type=F32)]
    dot_general x6 -> x3, matrix products: 42.6 us -> 9.83 us  [dot_back(): lax.dot_general(a, b, (((1,), (1,)), ((), ())), preferred_element_type=F32)]
  transfers between devices with their start and end apart: 201 -> 91, of which waited for: 84 -> 37; matrix products, arithmetic and copies ran while one was open for 17% -> 22% of each run, Pallas kernels for 3% -> 11%
where the time goes in v2:
time: 761 us; the launch traced here: 751 us
  waiting for transfers between devices  343 us (45%)
  other arithmetic  103 us (14%)
  Pallas kernels  97.3 us (13%)
  starting transfers between devices  85.5 us (11%)
  local copies, waits for them, and re-layouts  53.4 us (7%)
  matrix products  52.3 us (7%)
  between operations  16.4 us (2%)
    ppermute x9, waiting for transfers between devices, gather_line(): lax.ppermute(down, 'tp', [(i, i - 1) for i in range(1, size - s + 1)])  103 us
    ppermute x50, waiting for transfers between devices, send(): done.append(lax.ppermute(x, 'ctx', pairs))  85.1 us
    reduce_scatter x3, waiting for transfers between devices, scatter_tp(): lax.psum_scatter(part.astype(BF16), 'tp', scatter_dimension=0, tiled=True)  67.2 us
    all_gather x2, waiting for transfers between devices, gather_tp(): return lax.all_gather(x, 'tp', axis=axis, tiled=True)  49.6 us
    dot_general x6, matrix products, dot_rows(): lax.dot_general(a, b, (((0,), (0,)), ((), ())), preferred_element_type=F32)  32.5 us
    pallas_call x2, Pallas kernels, rows_call(): pl.pallas_call(functools.partial(rows_kernel, terms), grid=(width // TILE...  30.5 us
    convert_element_type x13, other arithmetic, pack(): self.now[t].astype(BF16)  28.1 us
    ppermute x50, starting transfers between devices, send(): done.append(lax.ppermute(x, 'ctx', pairs))  22.7 us
  transfers between devices with their start and end apart: 91, of which 37 were waited for; matrix products, arithmetic and copies ran while one was open for 22% of the time, Pallas kernels for 11%

profile of v2, /device:TPU:0, one launch (start us, length us, event | category | flops | bytes accessed | tf_op | source)
XLA Modules:
  0.0 750.7 jit_solution(6672046835153264739)
XLA Ops:
  10.8 6.4 collective-permute-start
  17.2 10.6 %collective-permute-done.1 = bf16[128,2304]{1,0:T(8,128)(2,1)S(1)} collective-permute-done((bf16[128,2304]{1,0:T(8,128)(2,1)S(1)}, bf16[128,2304]{1,0:T(8,128)(2,1)S(1)}, u32[]{:S(2)}, u32[]{:S(2)}) %collective-permute-start.1) | collective-permute-done | bytes 589856 | tf_op jit(solution)/shard_map/ppermute | solution.py:205
  30.8 13.5 %collective-permute-done.2 = bf16[128,2304]{1,0:T(8,128)(2,1)} collective-permute-done((bf16[128,2304]{1,0:T(8,128)(2,1)S(1)}, bf16[128,2304]{1,0:T(8,128)(2,1)}, u32[]{:S(2)}, u32[]{:S(2)}) %collective-permute-start.2) | collective-permute-done | bytes 589856 | tf_op jit(solution)/shard_map/ppermute | solution.py:205
  45.7 3.4 pad_maximum_fusion
  49.8 10.5 %collective-permute-done.3 = bf16[128,2304]{1,0:T(8,128)(2,1)} collective-permute-done((bf16[128,2304]{1,0:T(8,128)(2,1)}, bf16[128,2304]{1,0:T(8,128)(2,1)}, u32[]{:S(2)}, u32[]{:S(2)}) %collective-permute-start.3) | collective-permute-done | bytes 589856 | tf_op jit(solution)/shard_map/ppermute | solution.py:205
  77.3 4.6 fusion.6
  85.6 5.3 collective-permute-start.16
  90.9 15.3 %collective-permute-done.17 = bf16[1152,512]{1,0:T(8,128)(2,1)} collective-permute-done((bf16[1152,512]{1,0:T(8,128)(2,1)}, bf16[1152,512]{1,0:T(8,128)(2,1)}, u32[]{:S(2)}, u32[]{:S(2)}) %collective-permute-start.17) | collective-permute-done | bytes 1179680 | tf_op jit(solution)/shard_map/ppermute | solution.py:205
  112.5 4.7 collective-permute-done.9
  122.9 12.7 %collective-permute-done.19 = bf16[1152,512]{1,0:T(8,128)(2,1)} collective-permute-done((bf16[1152,512]{1,0:T(8,128)(2,1)}, bf16[1152,512]{1,0:T(8,128)(2,1)}, u32[]{:S(2)}, u32[]{:S(2)}) %collective-permute-start.19) | collective-permute-done | bytes 1179680 | tf_op jit(solution)/shard_map/ppermute | solution.py:205
  143.0 11.4 %shard_map.222 = (f32[512,512]{1,0:T(8,128)}, f32[1024,128]{1,0:T(8,128)}) custom-call(s32[4,36]{1,0:T(4,128)} %pad.4.index_ref, s32[4]{0:T(128)} %get-tuple-element.287.count_ref, bf16[512,512]{1,0:T(8,128)(2,1)} %fusion.33.q_ref, bf16[4096,512]{1,0:T(8,128)(2,1)} %copy-done.2, bf16[4096,512]{1,0:T(8,128)(2,1)} %copy-done.2), custom_call_target="tpu_custom_call" | custom-call | flops 2147483648 | bytes 6291456 | tf_op jit(solution)/shard_map/pallas_call | solution.py:332
  156.5 7.7 %collective-permute-done.23 = bf16[1152,512]{1,0:T(8,128)(2,1)} collective-permute-done((bf16[1152,512]{1,0:T(8,128)(2,1)}, bf16[1152,512]{1,0:T(8,128)(2,1)}, u32[]{:S(2)}, u32[]{:S(2)}) %collective-permute-start.23) | collective-permute-done | bytes 1179680 | tf_op jit(solution)/shard_map/ppermute | solution.py:205
  172.1 13.5 %collective-permute-start.20 = (bf16[128,512]{1,0:T(8,128)(2,1)S(1)}, bf16[128,512]{1,0:T(8,128)(2,1)S(1)}, u32[]{:S(2)}, u32[]{:S(2)}) collective-permute-start(bf16[128,512]{1,0:T(8,128)(2,1)S(1)} %get-tuple-element.261), channel_id=1, source_target_pairs={{0,3},{1,0},{2,1},{3,2},{4,7},{5,4},{6,5},{7,6},{8,11},{9,8},{10,9... | collective-permute-start | bytes 393224 | tf_op jit(solution)/shard_map/ppermute | solution.py:222
  189.5 8.3 %collective-permute-done.21 = bf16[128,512]{1,0:T(8,128)(2,1)S(1)} collective-permute-done((bf16[128,512]{1,0:T(8,128)(2,1)S(1)}, bf16[128,512]{1,0:T(8,128)(2,1)S(1)}, u32[]{:S(2)}, u32[]{:S(2)}) %collective-permute-start.21) | collective-permute-done | bytes 131104 | tf_op jit(solution)/shard_map/ppermute | solution.py:222
  216.2 11.6 %collective-permute-done.26 = bf16[128,2304]{1,0:T(8,128)(2,1)S(1)} collective-permute-done((bf16[128,2304]{1,0:T(8,128)(2,1)}, bf16[128,2304]{1,0:T(8,128)(2,1)S(1)}, u32[]{:S(2)}, u32[]{:S(2)}) %collective-permute-start.26) | collective-permute-done | bytes 589856 | tf_op jit(solution)/shard_map/ppermute | solution.py:204
  227.8 4.8 collective-permute-done.27
  234.7 14.2 %collective-permute-done.28 = bf16[128,2304]{1,0:T(8,128)(2,1)S(1)} collective-permute-done((bf16[128,2304]{1,0:T(8,128)(2,1)S(1)}, bf16[128,2304]{1,0:T(8,128)(2,1)S(1)}, u32[]{:S(2)}, u32[]{:S(2)}) %collective-permute-start.28) | collective-permute-done | bytes 589856 | tf_op jit(solution)/shard_map/ppermute | solution.py:205
  250.9 13.4 %collective-permute-done.29 = bf16[128,2304]{1,0:T(8,128)(2,1)S(1)} collective-permute-done((bf16[128,2304]{1,0:T(8,128)(2,1)S(1)}, bf16[128,2304]{1,0:T(8,128)(2,1)S(1)}, u32[]{:S(2)}, u32[]{:S(2)}) %collective-permute-start.29) | collective-permute-done | bytes 589856 | tf_op jit(solution)/shard_map/ppermute | solution.py:205
  267.1 19.1 %ffn_in.1 = (f32[512,2304]{1,0:T(8,128)}, f32[512,2304]{1,0:T(8,128)}, bf16[512,2304]{1,0:T(8,128)(2,1)}) custom-call(bf16[512,2304]{1,0:T(8,128)(2,1)} %select_dynamic-update-slice_fusion.3.x_ref, bf16[2304,4608]{1,0:T(8,128)(2,1)} %all-gather.8.cloned.1.call-done.gate_w_ref.up_w_ref.refs_2_, ...), custom_call_target="tpu_custom_call" | custom-call | flops 10871635968 | bytes 21233664 | tf_op jit(solution)/shard_map/ffn_in/pallas_call | solution.py:393
  286.2 9.3 %all-gather.10.cloned.1.call-done.refs_1_.w_ref = bf16[2304,2304]{1,0:T(8,128)(2,1)} async-done(((bf16[288,2304]{1,0:T(8,128)(2,1)}), bf16[2304,2304]{1,0:T(8,128)(2,1)}) %all-gather.10.cloned.1.call-update) | async-done | bytes 10616848 | tf_op jit(solution)/shard_map/all_gather | solution.py:570
  295.5 12.4 %ffn_out.1 = bf16[512,2304]{1,0:T(8,128)(2,1)} custom-call(bf16[512,2304]{1,0:T(8,128)(2,1)} %get-tuple-element.112.refs_0_, bf16[2304,2304]{1,0:T(8,128)(2,1)} %all-gather.10.cloned.1.call-done.refs_1_.w_ref), custom_call_target="tpu_custom_call" | custom-call | flops 5435817984 | bytes 10616832 | tf_op jit(solution)/shard_map/ffn_out/pallas_call | solution.py:452
  307.9 48.1 %reduce-scatter.4.cloned.1.call-done = bf16[128,2304]{1,0:T(8,128)(2,1)} async-done(((bf16[512,2304]{1,0:T(8,128)(2,1)}), bf16[128,2304]{1,0:T(8,128)(2,1)}) %reduce-scatter.4.cloned.1.call-update) | async-done | bytes 589840 | tf_op jit(solution)/shard_map/reduce_scatter | solution.py:196
  362.4 49.6 %all-gather.12.cloned.1.call-done.x_ref = bf16[512,2304]{1,0:T(8,128)(2,1)} async-done(((bf16[128,2304]{1,0:T(8,128)(2,1)}), bf16[512,2304]{1,0:T(8,128)(2,1)}) %all-gather.12.cloned.1.call-update) | async-done | bytes 2359312 | tf_op jit(solution)/shard_map/all_gather | solution.py:192
  412.0 8.0 %convolution_convert_fusion.2 = bf16[2304,2304]{1,0:T(8,128)(2,1)S(1)} fusion(bf16[512,2304]{1,0:T(8,128)(2,1)} %all-gather.12.cloned.1.call-done.x_ref, bf16[512,2304]{1,0:T(8,128)(2,1)} %get-tuple-element.112.refs_0_), kind=kOutput, calls=%fused_computation.2 | convolution fusion | flops 5441126400 | bytes 15335424 | tf_op jit(solution)/shard_map/dot_general | solution.py:32
  426.0 15.6 %ffn_back.1 = (bf16[512,2304]{1,0:T(8,128)(2,1)}, bf16[512,2304]{1,0:T(8,128)(2,1)}) custom-call(bf16[512,2304]{1,0:T(8,128)(2,1)} %all-gather.12.cloned.1.call-done.x_ref, f32[512,2304]{1,0:T(8,128)} %get-tuple-element.116.gate_ref, f32[512,2304]{1,0:T(8,128)} %get-tuple-element.117.up_ref, bf16[2304,2304]{1,0:T(8,128)(2,1)} %all-gather.10.cloned.1.call-done.refs_1_.w_ref), custom_call_target="tpu_custom_call" | custom-call | flops 5435817984 | bytes 10616832 | tf_op jit(solution)/shard_map/ffn_back/pallas_call | solution.py:423
  447.9 18.1 %ffn_back_in.1 = bf16[512,2304]{1,0:T(8,128)(2,1)} custom-call(bf16[512,2304]{1,0:T(8,128)(2,1)} %get-tuple-element.127.refs_0_, bf16[512,2304]{1,0:T(8,128)(2,1)} %get-tuple-element.143.refs_1_, bf16[2304,4608]{1,0:T(8,128)(2,1)} %all-gather.8.cloned.1.call-done.gate_w_ref.up_w_ref.refs_2_), custom_call_target="tpu_custom_call" | custom-call | flops 10871635968 | bytes 21233664 | tf_op jit(solution)/shard_map/ffn_back_in/pallas_call | solution.py:452
  466.0 8.0 %convolution_convert_fusion.1 = bf16[2304,2304]{1,0:T(8,128)(2,1)S(1)} fusion(bf16[512,2304]{1,0:T(8,128)(2,1)} %select_dynamic-update-slice_fusion.3.x_ref, bf16[512,2304]{1,0:T(8,128)(2,1)} %get-tuple-element.127.refs_0_), kind=kOutput, calls=%fused_computation.1 | convolution fusion | flops 5441126400 | bytes 15335424 | tf_op jit(solution)/shard_map/dot_general | solution.py:32
  489.6 11.2 %collective-permute-done.36 = bf16[288,2304]{1,0:T(8,128)(2,1)} collective-permute-done((bf16[288,2304]{1,0:T(8,128)(2,1)S(1)}, bf16[288,2304]{1,0:T(8,128)(2,1)}, u32[]{:S(2)}, u32[]{:S(2)}) %collective-permute-start.36) | collective-permute-done | bytes 1327136 | tf_op jit(solution)/shard_map/ppermute | solution.py:100
  502.5 4.5 collective-permute-done.45
  507.2 19.1 %reduce-scatter.6.cloned.1.call-done = bf16[128,2304]{1,0:T(8,128)(2,1)} async-done(((bf16[512,2304]{1,0:T(8,128)(2,1)}), bf16[128,2304]{1,0:T(8,128)(2,1)}) %reduce-scatter.6.cloned.1.call-update) | async-done | bytes 589840 | tf_op jit(solution)/shard_map/reduce_scatter | solution.py:196
  527.4 5.8 collective-permute-done.40
  533.2 3.7 add_convert_fusion.3
  540.8 5.3 convolution_convert_fusion.7
  552.4 7.8 %convolution_convert_fusion = bf16[2304,2304]{1,0:T(8,128)(2,1)S(1)} fusion(bf16[512,2304]{1,0:T(8,128)(2,1)} %select_dynamic-update-slice_fusion.3.x_ref, bf16[512,2304]{1,0:T(8,128)(2,1)S(1)} %copy-done.71), kind=kOutput, calls=%fused_computation | convolution fusion | flops 5441126400 | bytes 15335424 | tf_op jit(solution)/shard_map/dot_general | solution.py:32
  572.6 20.7 %shard_map.223 = (bf16[512,512]{1,0:T(8,128)(2,1)}, f32[4096,512]{1,0:T(8,128)}) custom-call(s32[4,36]{1,0:T(4,128)} %pad.4.index_ref, s32[4]{0:T(128)} %get-tuple-element.287.count_ref, bf16[512,512]{1,0:T(8,128)(2,1)} %fusion.33.q_ref, bf16[512,512]{1,0:T(8,128)(2,1)} %constant_dynamic-slice_fusion.30.dout_ref, f32[512,512]{1,0:T(8,128)} %get-tuple-element.105.out_ref, ...), custom_call_target="tpu_custom_call" | custom-call | flops 5368709120 | bytes 16777216 | tf_op jit(solution)/shard_map/pallas_call | solution.py:354
  593.3 4.4 convert.10
  605.0 4.8 add_bitcast_fusion
  611.5 6.9 collective-permute-done.54
  625.6 3.9 collective-permute-done.56
  631.7 4.9 fusion.4
  645.1 16.7 %collective-permute-done.57 = bf16[576,2304]{1,0:T(8,128)(2,1)} collective-permute-done((bf16[576,2304]{1,0:T(8,128)(2,1)}, bf16[576,2304]{1,0:T(8,128)(2,1)}, u32[]{:S(2)}, u32[]{:S(2)}) %collective-permute-start.57) | collective-permute-done | bytes 2654240 | tf_op jit(solution)/shard_map/ppermute | solution.py:100
  661.8 3.7 add_convert_fusion
  674.4 9.2 %collective-permute-done.58 = bf16[288,2304]{1,0:T(8,128)(2,1)S(1)} collective-permute-done((bf16[288,2304]{1,0:T(8,128)(2,1)}, bf16[288,2304]{1,0:T(8,128)(2,1)S(1)}, u32[]{:S(2)}, u32[]{:S(2)}) %collective-permute-start.58) | collective-permute-done | bytes 1327136 | tf_op jit(solution)/shard_map/ppermute | solution.py:100
  691.1 3.7 collective-permute-start.82
  698.4 4.4 collective-permute-done.64
  704.3 4.6 convert_add_fusion
  716.3 3.8 convert_add_fusion.1
  724.7 8.7 %collective-permute-done.74 = bf16[576,512]{1,0:T(8,128)(2,1)S(1)} collective-permute-done((bf16[576,512]{1,0:T(8,128)(2,1)S(1)}, bf16[576,512]{1,0:T(8,128)(2,1)S(1)}, u32[]{:S(2)}, u32[]{:S(2)}) %collective-permute-start.74) | collective-permute-done | bytes 589856 | tf_op jit(solution)/shard_map/ppermute | solution.py:100
  (453 shorter events, 216.7 us)
Async XLA Ops:
  7.2 55.8 %all-gather.6.cloned.1.call-start = ((), (), s32[]{:S(2)}) async-start(), calls=%async_computation.3 | async-start | bytes 7962624 | tf_op jit(solution)/shard_map/all_gather | solution.py:570
  9.5 206.7 %all-gather.8.cloned.1.call-start = ((), (), s32[]{:S(2)}) async-start(), calls=%async_computation.4 | async-start | bytes 23887872 | tf_op jit(solution)/shard_map/all_gather | solution.py:570
  9.5 18.3 %collective-permute-start.1 = (bf16[128,2304]{1,0:T(8,128)(2,1)S(1)}, bf16[128,2304]{1,0:T(8,128)(2,1)S(1)}, u32[]{:S(2)}, u32[]{:S(2)}) collective-permute-start(bf16[128,2304]{1,0:T(8,128)(2,1)S(1)} %copy-done.10), channel_id=1, source_target_pairs={{1,0},{2,1},{3,2},{5,4},{6,5},{7,6},{9,8},{10,9},{11,10},{13,12},{... | collective-permute-start | bytes 1769480 | tf_op jit(solution)/shard_map/ppermute | solution.py:205
  10.8 18.5 %collective-permute-start = (bf16[128,2304]{1,0:T(8,128)(2,1)S(1)}, bf16[128,2304]{1,0:T(8,128)(2,1)}, u32[]{:S(2)}, u32[]{:S(2)}) collective-permute-start(bf16[128,2304]{1,0:T(8,128)(2,1)S(1)} %copy-done.10), channel_id=1, source_target_pairs={{0,1},{1,2},{2,3},{4,5},{5,6},{6,7},{8,9},{9,10},{10,11},{12,13},{... | collective-permute-start | bytes 1769480 | tf_op jit(solution)/shard_map/ppermute | solution.py:204
  27.8 16.6 %collective-permute-start.2 = (bf16[128,2304]{1,0:T(8,128)(2,1)S(1)}, bf16[128,2304]{1,0:T(8,128)(2,1)}, u32[]{:S(2)}, u32[]{:S(2)}) collective-permute-start(bf16[128,2304]{1,0:T(8,128)(2,1)S(1)} %collective-permute-done.1), channel_id=1, source_target_pairs={{1,0},{2,1},{5,4},{6,5},{9,8},{10,9},{13,12},{14,13},{17,16},{18,1... | collective-permute-start | bytes 1769480 | tf_op jit(solution)/shard_map/ppermute | solution.py:205
  29.4 19.7 %collective-permute-start.4 = (bf16[128,2304]{1,0:T(8,128)(2,1)}, bf16[128,2304]{1,0:T(8,128)(2,1)}, u32[]{:S(2)}, u32[]{:S(2)}) collective-permute-start(bf16[128,2304]{1,0:T(8,128)(2,1)} %collective-permute-done), channel_id=1, source_target_pairs={{1,2},{2,3},{5,6},{6,7},{9,10},{10,11},{13,14},{14,15},{17,18},{18... | collective-permute-start | bytes 1769480 | tf_op jit(solution)/shard_map/ppermute | solution.py:204
  63.0 232.5 %all-gather.10.cloned.1.call-start = ((), (), s32[]{:S(2)}) async-start(), calls=%async_computation.5 | async-start | bytes 11943936 | tf_op jit(solution)/shard_map/all_gather | solution.py:570
  75.9 30.3 %collective-permute-start.17 = (bf16[1152,512]{1,0:T(8,128)(2,1)}, bf16[1152,512]{1,0:T(8,128)(2,1)}, u32[]{:S(2)}, u32[]{:S(2)}) collective-permute-start(bf16[1152,512]{1,0:T(8,128)(2,1)} %dynamic-slice), channel_id=1, source_target_pairs={{1,0},{2,1},{3,2},{5,4},{6,5},{7,6},{9,8},{10,9},{11,10},{13,12},{... | collective-permute-start | bytes 3538952 | tf_op jit(solution)/shard_map/ppermute | solution.py:205
  84.0 25.0 %collective-permute-start.10 = (bf16[512,512]{1,0:T(8,128)(2,1)S(1)}, bf16[512,512]{1,0:T(8,128)(2,1)S(1)}, u32[]{:S(2)}, u32[]{:S(2)}) collective-permute-start(bf16[512,512]{1,0:T(8,128)(2,1)S(1)} %get-tuple-element.208), channel_id=1, source_target_pairs={{0,16},{4,12},{8,24},{12,4},{16,0},{20,28},{24,8},{28,20},{1,17},{... | collective-permute-start | bytes 1572872 | tf_op jit(solution)/shard_map/ppermute | solution.py:100
  85.4 23.6 %collective-permute-start.12 = (bf16[512,512]{1,0:T(8,128)(2,1)S(1)}, bf16[512,512]{1,0:T(8,128)(2,1)S(1)}, u32[]{:S(2)}, u32[]{:S(2)}) collective-permute-start(bf16[512,512]{1,0:T(8,128)(2,1)S(1)} %get-tuple-element.208), channel_id=1, source_target_pairs={{0,4},{4,0},{8,12},{12,8},{16,20},{20,16},{24,28},{28,24},{1,5},{5... | collective-permute-start | bytes 1572872 | tf_op jit(solution)/shard_map/ppermute | solution.py:100
  85.6 35.6 %collective-permute-start.16 = (bf16[1152,512]{1,0:T(8,128)(2,1)}, bf16[1152,512]{1,0:T(8,128)(2,1)}, u32[]{:S(2)}, u32[]{:S(2)}) collective-permute-start(bf16[1152,512]{1,0:T(8,128)(2,1)} %dynamic-slice), channel_id=1, source_target_pairs={{0,1},{1,2},{2,3},{4,5},{5,6},{6,7},{8,9},{9,10},{10,11},{12,13},{... | collective-permute-start | bytes 3538952 | tf_op jit(solution)/shard_map/ppermute | solution.py:204
  106.2 29.4 %collective-permute-start.19 = (bf16[1152,512]{1,0:T(8,128)(2,1)}, bf16[1152,512]{1,0:T(8,128)(2,1)}, u32[]{:S(2)}, u32[]{:S(2)}) collective-permute-start(bf16[1152,512]{1,0:T(8,128)(2,1)} %collective-permute-done.17), channel_id=1, source_target_pairs={{1,0},{2,1},{5,4},{6,5},{9,8},{10,9},{13,12},{14,13},{17,16},{18,1... | collective-permute-start | bytes 3538952 | tf_op jit(solution)/shard_map/ppermute | solution.py:205
  111.5 27.4 %collective-permute-start.11 = (bf16[512,512]{1,0:T(8,128)(2,1)S(1)}, bf16[512,512]{1,0:T(8,128)(2,1)S(1)}, u32[]{:S(2)}, u32[]{:S(2)}) collective-permute-start(bf16[512,512]{1,0:T(8,128)(2,1)S(1)} %collective-permute-done.10), channel_id=1, source_target_pairs={{0,8},{4,20},{8,0},{12,28},{16,24},{20,4},{24,16},{28,12},{1,9},{5... | collective-permute-start | bytes 1572872 | tf_op jit(solution)/shard_map/ppermute | solution.py:100
  117.2 21.8 %collective-permute-start.14 = (bf16[512,512]{1,0:T(8,128)(2,1)}, bf16[512,512]{1,0:T(8,128)(2,1)S(1)}, u32[]{:S(2)}, u32[]{:S(2)}) collective-permute-start(bf16[512,512]{1,0:T(8,128)(2,1)} %collective-permute-done.9), channel_id=1, source_target_pairs={{0,4},{4,0},{8,12},{12,8},{16,20},{20,16},{24,28},{28,24},{1,5},{5... | collective-permute-start | bytes 1572872 | tf_op jit(solution)/shard_map/ppermute | solution.py:100
  121.2 34.5 %collective-permute-start.18 = (bf16[1152,512]{1,0:T(8,128)(2,1)}, bf16[1152,512]{1,0:T(8,128)(2,1)}, u32[]{:S(2)}, u32[]{:S(2)}) collective-permute-start(bf16[1152,512]{1,0:T(8,128)(2,1)} %collective-permute-done.16), channel_id=1, source_target_pairs={{1,2},{2,3},{5,6},{6,7},{9,10},{10,11},{13,14},{14,15},{17,18},{18... | collective-permute-start | bytes 3538952 | tf_op jit(solution)/shard_map/ppermute | solution.py:204
  135.6 28.5 %collective-permute-start.23 = (bf16[1152,512]{1,0:T(8,128)(2,1)}, bf16[1152,512]{1,0:T(8,128)(2,1)}, u32[]{:S(2)}, u32[]{:S(2)}) collective-permute-start(bf16[1152,512]{1,0:T(8,128)(2,1)} %collective-permute-done.19), channel_id=1, source_target_pairs={{1,0},{5,4},{9,8},{13,12},{17,16},{21,20},{25,24},{29,28}} | collective-permute-start | bytes 3538952 | tf_op jit(solution)/shard_map/ppermute | solution.py:205
  172.1 28.9 %collective-permute-start.25 = (bf16[1152,2048]{1,0:T(8,128)(2,1)}, bf16[1152,2048]{1,0:T(8,128)(2,1)}, u32[]{:S(2)}, u32[]{:S(2)}) collective-permute-start(bf16[1152,2048]{1,0:T(8,128)(2,1)} %select_dynamic-update-slice_fusion), channel_id=1, source_target_pairs={{0,4},{4,0},{8,12},{12,8},{16,20},{20,16},{24,28},{28,24},{1,5},{5... | collective-permute-start | bytes 14155784 | tf_op jit(solution)/shard_map/ppermute | solution.py:100
  172.1 17.4 %collective-permute-start.20 = (bf16[128,512]{1,0:T(8,128)(2,1)S(1)}, bf16[128,512]{1,0:T(8,128)(2,1)S(1)}, u32[]{:S(2)}, u32[]{:S(2)}) collective-permute-start(bf16[128,512]{1,0:T(8,128)(2,1)S(1)} %get-tuple-element.261), channel_id=1, source_target_pairs={{0,3},{1,0},{2,1},{3,2},{4,7},{5,4},{6,5},{7,6},{8,11},{9,8},{10,9... | collective-permute-start | bytes 393224 | tf_op jit(solution)/shard_map/ppermute | solution.py:222
  214.9 17.7 %collective-permute-start.27 = (bf16[128,2304]{1,0:T(8,128)(2,1)}, bf16[128,2304]{1,0:T(8,128)(2,1)S(1)}, u32[]{:S(2)}, u32[]{:S(2)}) collective-permute-start(bf16[128,2304]{1,0:T(8,128)(2,1)} %get-tuple-element.204), channel_id=1, source_target_pairs={{1,0},{2,1},{3,2},{5,4},{6,5},{7,6},{9,8},{10,9},{11,10},{13,12},{... | collective-permute-start | bytes 1769480 | tf_op jit(solution)/shard_map/ppermute | solution.py:205
  232.6 123.5 %reduce-scatter.4.cloned.1.call-start = ((), (), s32[]{:S(2)}) async-start(), calls=%async_computation.6 | async-start | bytes 2949120 | tf_op jit(solution)/shard_map/reduce_scatter | solution.py:196
  232.7 16.2 %collective-permute-start.28 = (bf16[128,2304]{1,0:T(8,128)(2,1)S(1)}, bf16[128,2304]{1,0:T(8,128)(2,1)S(1)}, u32[]{:S(2)}, u32[]{:S(2)}) collective-permute-start(bf16[128,2304]{1,0:T(8,128)(2,1)S(1)} %collective-permute-done.27), channel_id=1, source_target_pairs={{1,0},{2,1},{5,4},{6,5},{9,8},{10,9},{13,12},{14,13},{17,16},{18,1... | collective-permute-start | bytes 1769480 | tf_op jit(solution)/shard_map/ppermute | solution.py:205
  234.0 16.2 %collective-permute-start.30 = (bf16[128,2304]{1,0:T(8,128)(2,1)S(1)}, bf16[128,2304]{1,0:T(8,128)(2,1)S(1)}, u32[]{:S(2)}, u32[]{:S(2)}) collective-permute-start(bf16[128,2304]{1,0:T(8,128)(2,1)S(1)} %collective-permute-done.26), channel_id=1, source_target_pairs={{1,2},{2,3},{5,6},{6,7},{9,10},{10,11},{13,14},{14,15},{17,18},{18... | collective-permute-start | bytes 1769480 | tf_op jit(solution)/shard_map/ppermute | solution.py:204
  307.9 104.1 %all-gather.12.cloned.1.call-start = ((), (), s32[]{:S(2)}) async-start(), calls=%async_computation.7 | async-start | bytes 2949120 | tf_op jit(solution)/shard_map/all_gather | solution.py:192
  361.8 164.4 %reduce-scatter.6.cloned.1.call-start = ((), (), s32[]{:S(2)}) async-start(), calls=%async_computation.8 | async-start | bytes 2949120 | tf_op jit(solution)/shard_map/reduce_scatter | solution.py:196
  425.5 16.1 %collective-permute-start.32 = (bf16[288,2304]{1,0:T(8,128)(2,1)}, bf16[288,2304]{1,0:T(8,128)(2,1)}, u32[]{:S(2)}, u32[]{:S(2)}) collective-permute-start(bf16[288,2304]{1,0:T(8,128)(2,1)} %get-tuple-element.119), channel_id=1, source_target_pairs={{0,4},{4,0},{8,12},{12,8},{16,20},{20,16},{24,28},{28,24},{1,5},{5... | collective-permute-start | bytes 3981320 | tf_op jit(solution)/shard_map/ppermute | solution.py:100
  425.5 16.1 %collective-permute-start.33 = (bf16[288,2304]{1,0:T(8,128)(2,1)}, bf16[288,2304]{1,0:T(8,128)(2,1)}, u32[]{:S(2)}, u32[]{:S(2)}) collective-permute-start(bf16[288,2304]{1,0:T(8,128)(2,1)} %get-tuple-element.120), channel_id=1, source_target_pairs={{0,4},{4,0},{8,12},{12,8},{16,20},{20,16},{24,28},{28,24},{1,5},{5... | collective-permute-start | bytes 3981320 | tf_op jit(solution)/shard_map/ppermute | solution.py:100
  426.0 54.3 %collective-permute-start.34 = (bf16[288,2304]{1,0:T(8,128)(2,1)}, bf16[288,2304]{1,0:T(8,128)(2,1)}, u32[]{:S(2)}, u32[]{:S(2)}) collective-permute-start(bf16[288,2304]{1,0:T(8,128)(2,1)} %get-tuple-element.123), channel_id=1, source_target_pairs={{0,4},{4,0},{8,12},{12,8},{16,20},{20,16},{24,28},{28,24},{1,5},{5... | collective-permute-start | bytes 3981320 | tf_op jit(solution)/shard_map/ppermute | solution.py:100
  446.4 33.1 %collective-permute-start.35 = (bf16[576,2304]{1,0:T(8,128)(2,1)}, bf16[576,2304]{1,0:T(8,128)(2,1)}, u32[]{:S(2)}, u32[]{:S(2)}) collective-permute-start(bf16[576,2304]{1,0:T(8,128)(2,1)} %pad_maximum_fusion.1), channel_id=1, source_target_pairs={{0,16},{4,12},{8,24},{12,4},{16,0},{20,28},{24,8},{28,20},{1,17},{... | collective-permute-start | bytes 7962632 | tf_op jit(solution)/shard_map/ppermute | solution.py:100
  480.1 187.0 %all-gather.14.cloned.1.call-start = ((), (), s32[]{:S(2)}) async-start(), calls=%async_computation.10 | async-start | bytes 2949120 | tf_op jit(solution)/shard_map/all_gather | solution.py:192
  482.9 18.0 %collective-permute-start.36 = (bf16[288,2304]{1,0:T(8,128)(2,1)S(1)}, bf16[288,2304]{1,0:T(8,128)(2,1)}, u32[]{:S(2)}, u32[]{:S(2)}) collective-permute-start(bf16[288,2304]{1,0:T(8,128)(2,1)S(1)} %add_convert_fusion.6), channel_id=1, source_target_pairs={{0,8},{4,20},{8,0},{12,28},{16,24},{20,4},{24,16},{28,12},{1,9},{5... | collective-permute-start | bytes 3981320 | tf_op jit(solution)/shard_map/ppermute | solution.py:100
  500.9 32.3 %collective-permute-start.40 = (bf16[576,2304]{1,0:T(8,128)(2,1)}, bf16[576,2304]{1,0:T(8,128)(2,1)}, u32[]{:S(2)}, u32[]{:S(2)}) collective-permute-start(bf16[576,2304]{1,0:T(8,128)(2,1)} %pad_maximum_fusion.2), channel_id=1, source_target_pairs={{0,16},{4,12},{8,24},{12,4},{16,0},{20,28},{24,8},{28,20},{1,17},{... | collective-permute-start | bytes 7962632 | tf_op jit(solution)/shard_map/ppermute | solution.py:100
  502.0 25.4 %collective-permute-start.37 = (bf16[288,2304]{1,0:T(8,128)(2,1)}, bf16[288,2304]{1,0:T(8,128)(2,1)}, u32[]{:S(2)}, u32[]{:S(2)}) collective-permute-start(bf16[288,2304]{1,0:T(8,128)(2,1)} %get-tuple-element.129), channel_id=1, source_target_pairs={{0,4},{4,0},{8,12},{12,8},{16,20},{20,16},{24,28},{28,24},{1,5},{5... | collective-permute-start | bytes 3981320 | tf_op jit(solution)/shard_map/ppermute | solution.py:100
  507.1 58.7 %collective-permute-start.46 = (bf16[288,2304]{1,0:T(8,128)(2,1)}, bf16[288,2304]{1,0:T(8,128)(2,1)}, u32[]{:S(2)}, u32[]{:S(2)}) collective-permute-start(bf16[288,2304]{1,0:T(8,128)(2,1)} %get-tuple-element.146), channel_id=1, source_target_pairs={{0,4},{4,0},{8,12},{12,8},{16,20},{20,16},{24,28},{28,24},{1,5},{5... | collective-permute-start | bytes 3981320 | tf_op jit(solution)/shard_map/ppermute | solution.py:100
  546.8 18.9 %collective-permute-start.43 = (bf16[128,512]{1,0:T(8,128)(2,1)S(1)}, bf16[128,512]{1,0:T(8,128)(2,1)S(1)}, u32[]{:S(2)}, u32[]{:S(2)}) collective-permute-start(bf16[128,512]{1,0:T(8,128)(2,1)S(1)} %get-tuple-element.254), channel_id=1, source_target_pairs={{0,1},{1,2},{2,3},{3,0},{4,5},{5,6},{6,7},{7,4},{8,9},{9,10},{10,1... | collective-permute-start | bytes 393224 | tf_op jit(solution)/shard_map/ppermute | solution.py:222
  546.8 19.4 %collective-permute-start.42 = (bf16[128,512]{1,0:T(8,128)(2,1)S(1)}, bf16[128,512]{1,0:T(8,128)(2,1)S(1)}, u32[]{:S(2)}, u32[]{:S(2)}) collective-permute-start(bf16[128,512]{1,0:T(8,128)(2,1)S(1)} %get-tuple-element.256), channel_id=1, source_target_pairs={{0,2},{1,3},{2,0},{3,1},{4,6},{5,7},{6,4},{7,5},{8,10},{9,11},{10,... | collective-permute-start | bytes 393224 | tf_op jit(solution)/shard_map/ppermute | solution.py:222
  548.5 17.8 %collective-permute-start.41 = (bf16[128,512]{1,0:T(8,128)(2,1)S(1)}, bf16[128,512]{1,0:T(8,128)(2,1)S(1)}, u32[]{:S(2)}, u32[]{:S(2)}) collective-permute-start(bf16[128,512]{1,0:T(8,128)(2,1)S(1)} %get-tuple-element.257), channel_id=1, source_target_pairs={{0,3},{1,0},{2,1},{3,2},{4,7},{5,4},{6,5},{7,6},{8,11},{9,8},{10,9... | collective-permute-start | bytes 393224 | tf_op jit(solution)/shard_map/ppermute | solution.py:222
  551.0 42.3 %collective-permute-start.44 = (bf16[288,2304]{1,0:T(8,128)(2,1)}, bf16[288,2304]{1,0:T(8,128)(2,1)}, u32[]{:S(2)}, u32[]{:S(2)}) collective-permute-start(bf16[288,2304]{1,0:T(8,128)(2,1)} %add_convert_fusion.3), channel_id=1, source_target_pairs={{0,8},{4,20},{8,0},{12,28},{16,24},{20,4},{24,16},{28,12},{1,9},{5... | collective-permute-start | bytes 3981320 | tf_op jit(solution)/shard_map/ppermute | solution.py:100
  565.7 27.6 %collective-permute-start.47 = (bf16[288,2304]{1,0:T(8,128)(2,1)}, bf16[288,2304]{1,0:T(8,128)(2,1)S(1)}, u32[]{:S(2)}, u32[]{:S(2)}) collective-permute-start(bf16[288,2304]{1,0:T(8,128)(2,1)} %get-tuple-element.147), channel_id=1, source_target_pairs={{0,4},{4,0},{8,12},{12,8},{16,20},{20,16},{24,28},{28,24},{1,5},{5... | collective-permute-start | bytes 3981320 | tf_op jit(solution)/shard_map/ppermute | solution.py:100
  565.7 27.6 %collective-permute-start.48 = (bf16[288,2304]{1,0:T(8,128)(2,1)}, bf16[288,2304]{1,0:T(8,128)(2,1)}, u32[]{:S(2)}, u32[]{:S(2)}) collective-permute-start(bf16[288,2304]{1,0:T(8,128)(2,1)} %get-tuple-element.149), channel_id=1, source_target_pairs={{0,4},{4,0},{8,12},{12,8},{16,20},{20,16},{24,28},{28,24},{1,5},{5... | collective-permute-start | bytes 3981320 | tf_op jit(solution)/shard_map/ppermute | solution.py:100
  566.3 27.1 %collective-permute-start.49 = (bf16[288,2304]{1,0:T(8,128)(2,1)}, bf16[288,2304]{1,0:T(8,128)(2,1)}, u32[]{:S(2)}, u32[]{:S(2)}) collective-permute-start(bf16[288,2304]{1,0:T(8,128)(2,1)} %get-tuple-element.151), channel_id=1, source_target_pairs={{0,4},{4,0},{8,12},{12,8},{16,20},{20,16},{24,28},{28,24},{1,5},{5... | collective-permute-start | bytes 3981320 | tf_op jit(solution)/shard_map/ppermute | solution.py:100
  566.3 27.0 %collective-permute-start.50 = (bf16[288,2304]{1,0:T(8,128)(2,1)}, bf16[288,2304]{1,0:T(8,128)(2,1)}, u32[]{:S(2)}, u32[]{:S(2)}) collective-permute-start(bf16[288,2304]{1,0:T(8,128)(2,1)} %get-tuple-element.153), channel_id=1, source_target_pairs={{0,4},{4,0},{8,12},{12,8},{16,20},{20,16},{24,28},{28,24},{1,5},{5... | collective-permute-start | bytes 3981320 | tf_op jit(solution)/shard_map/ppermute | solution.py:100
  604.6 115.5 %reduce-scatter.8.cloned.1.call-start = ((), (), s32[]{:S(2)}) async-start(), calls=%async_computation.9 | async-start | bytes 2949120 | tf_op jit(solution)/shard_map/reduce_scatter | solution.py:196
  611.0 18.9 %collective-permute-start.51 = (bf16[512,512]{1,0:T(8,128)(2,1)S(1)}, bf16[512,512]{1,0:T(8,128)(2,1)S(1)}, u32[]{:S(2)}, u32[]{:S(2)}) collective-permute-start(bf16[512,512]{1,0:T(8,128)(2,1)S(1)} %copy-done.37), channel_id=1, source_target_pairs={{0,4},{4,0},{8,12},{12,8},{16,20},{20,16},{24,28},{28,24},{1,5},{5... | collective-permute-start | bytes 1572872 | tf_op jit(solution)/shard_map/ppermute | solution.py:100
  629.5 32.3 %collective-permute-start.57 = (bf16[576,2304]{1,0:T(8,128)(2,1)}, bf16[576,2304]{1,0:T(8,128)(2,1)}, u32[]{:S(2)}, u32[]{:S(2)}) collective-permute-start(bf16[576,2304]{1,0:T(8,128)(2,1)} %pad_maximum_fusion.3), channel_id=1, source_target_pairs={{0,16},{4,12},{8,24},{12,4},{16,0},{20,28},{24,8},{28,20},{1,17},{... | collective-permute-start | bytes 7962632 | tf_op jit(solution)/shard_map/ppermute | solution.py:100
  639.5 31.5 %collective-permute-start.77 = (f32[16,288]{1,0:T(8,128)}, f32[16,288]{1,0:T(8,128)}, u32[]{:S(2)}, u32[]{:S(2)}) collective-permute-start(f32[16,288]{1,0:T(8,128)} %pad_maximum_fusion.10), channel_id=1, source_target_pairs={{0,4},{4,0},{8,12},{12,8},{16,20},{20,16},{24,28},{28,24},{1,5},{5... | collective-permute-start | bytes 55304 | tf_op jit(solution)/shard_map/ppermute | solution.py:526
  665.5 18.1 %collective-permute-start.58 = (bf16[288,2304]{1,0:T(8,128)(2,1)}, bf16[288,2304]{1,0:T(8,128)(2,1)S(1)}, u32[]{:S(2)}, u32[]{:S(2)}) collective-permute-start(bf16[288,2304]{1,0:T(8,128)(2,1)} %add_convert_fusion), channel_id=1, source_target_pairs={{0,8},{4,20},{8,0},{12,28},{16,24},{20,4},{24,16},{28,12},{1,9},{5... | collective-permute-start | bytes 3981320 | tf_op jit(solution)/shard_map/ppermute | solution.py:100
  691.1 17.8 %collective-permute-start.82 = (f32[1,288]{1,0:T(1,128)S(1)}, f32[1,288]{1,0:T(1,128)S(1)}, u32[]{:S(2)}, u32[]{:S(2)}) collective-permute-start(f32[1,288]{1,0:T(1,128)S(1)} %get-tuple-element.277), channel_id=1, source_target_pairs={{0,3},{1,0},{2,1},{3,2},{4,7},{5,4},{6,5},{7,6},{8,11},{9,8},{10,9... | collective-permute-start | bytes 3464 | tf_op jit(solution)/shard_map/ppermute | solution.py:544
  709.5 29.9 %collective-permute-start.71 = (bf16[288,512]{1,0:T(8,128)(2,1)}, bf16[288,512]{1,0:T(8,128)(2,1)}, u32[]{:S(2)}, u32[]{:S(2)}) collective-permute-start(bf16[288,512]{1,0:T(8,128)(2,1)} %get-tuple-element.180), channel_id=1, source_target_pairs={{0,4},{4,0},{8,12},{12,8},{16,20},{20,16},{24,28},{28,24},{1,5},{5... | collective-permute-start | bytes 884744 | tf_op jit(solution)/shard_map/ppermute | solution.py:100
  (119 other events, 1217.7 us)
Sparse Core Ops, SparseCore 0:
  10.5 51.5 all-gather.5
  64.5 117.9 all-gather.7
  232.7 62.6 all-gather.9
  308.0 48.0 reduce-scatter.3
  362.0 49.9 all-gather.11
  480.2 46.0 reduce-scatter.5
  604.8 49.0 all-gather.13
  656.1 46.9 reduce-scatter.7

commit v3 on v2

--- a/solution.py
+++ b/solution.py
@@ -141,6 +141,7 @@
 class Scatter:
     def __init__(self, lanes, sent, kept, after=()):
         self.lanes, self.came = lanes, []
+        self.sent = sent
         lanes.depth = {"far": 1, "near": 4}
         self.got = [lanes.near(tie_all(v.astype(BF16), after)) for v in sent]
         spots = places()
@@ -175,17 +176,25 @@
     return ctx ^ jnp.where(ctx % 2 == 0, distances(0)[p], distances(1)[p])
 
 
-def scatter_grad(lanes, left, right, after=()):
+def scatter_grads(lanes, pairs, after=()):
     size = lax.axis_size("ctx")
-    chunk = left.shape[1] // size
-    part = dot_rows(left, right).astype(BF16)
+    parts = [dot_rows(left, right).astype(BF16) for left, right in pairs]
+    chunk = parts[0].shape[0] // size
     half = [owner_at(n) // 2 for n in range(size // 2)]
     core = lax.axis_index("ctx") % 2
 
     def chunks(side):
-        return [lax.dynamic_slice_in_dim(part, (2 * at + side) * chunk, chunk, 0) for at in half]
+        found = []
+        for at in half:
+            cut = [lax.dynamic_slice_in_dim(part, (2 * at + side) * chunk, chunk, 0) for part in parts]
+            found.append(cut[0] if len(cut) == 1 else jnp.concatenate(cut, axis=1))
+        return found
 
     return Scatter(lanes, chunks(1 - core), chunks(core), after)
+
+
+def scatter_grad(lanes, left, right, after=()):
+    return scatter_grads(lanes, [(left, right)], after)
 
 
 def gather_tp(x, axis=0):
@@ -196,11 +205,12 @@
     return lax.psum_scatter(part.astype(BF16), "tp", scatter_dimension=0, tiled=True).astype(F32)
 
 
-def gather_line(x, axis=0, steps=None):
+def gather_line(x, axis=0, steps=None, after={}):
     size, me = lax.axis_size("tp"), lax.axis_index("tp")
     up, down = x, x
     ups, downs = {}, {}
     for s in range(1, size):
+        up, down = [tie_all(v, after.get(s, ())) for v in (up, down)]
         up = lax.ppermute(up, "tp", [(i, i + 1) for i in range(s - 1, size - 1)])
         down = lax.ppermute(down, "tp", [(i, i - 1) for i in range(1, size - s + 1)])
         ups[s], downs[s] = up, down
@@ -570,23 +580,24 @@
         return lax.all_gather(w, "ctx", axis=0, tiled=True)
 
     wide = gather_weight(jnp.concatenate([w_query, key_projection, value_projection, w_out.T], axis=1))
-    gains = 1.0 + gather_small(norm_gains).astype(F32)
+    gains = gather_small(norm_gains)
     cot = cotangent.astype(F32)
     index, count = visible_lists(block_mask, block_seq, block_place, per_device)
 
     rows_in = gather_line(tokens)
-    pair_w = gather_weight(tie_all(jnp.concatenate([w_gate, w_up], axis=1), [wide, rows_in]))
+    pair_w = gather_weight(tie_all(jnp.concatenate([w_gate, w_up], axis=1), [wide, rows_in, gains]))
+    gains = 1.0 + gains.astype(F32)
     half = wide.shape[0] // 2
     core = lax.axis_index("ctx") % 2
     out_half = lax.dynamic_slice_in_dim(wide, core * half, half, 0)[:, in_cols:]
     out_steps, inner_steps = [], []
-    out_half = gather_line(tie(out_half, rows_in), axis=1, steps=out_steps)
     wide = wide[:, :in_cols]
     rows_in = rows_in.astype(F32)
     normed = (rows_in * inv_rms(rows_in) * gains[0]).astype(BF16)
     qkv = dot(normed, wide)
     q = (qkv[:, :q_cols] * scale).astype(BF16)
     kv_own = qkv[:, q_cols:].astype(BF16)
+    out_half = gather_line(tie(out_half, rows_in), axis=1, steps=out_steps)
     kv = tie_all(Gather(lanes, kv_own).rows(), out_steps[0])
 
     outcome, totals = attend(index, count, q, kv)
@@ -630,33 +641,32 @@
     head_cols = attended.shape[1]
     dattended = exchange_tp(lambda i: lax.dynamic_slice_in_dim(dheads, i * head_cols, head_cols, 1), 0)
     dattended = tie_all(dattended, [gate.came[0]])
-    up = scatter_grad(lanes, inner, tie(dup, dheads))
+    up_part = dot_rows(inner, tie(dup, dheads)).astype(BF16)
+    grad_up = lax.psum_scatter(up_part, "ctx", scatter_dimension=0, tiled=True).astype(F32)
     gate.hop([dheads])
-    dbranch = gather_tp(dbranch)
+    dbranch = gather_line(tie(dbranch, dattended))
 
     dq, dkv = attend_back(index, count, q, dattended, outcome, totals, kv)
     dq = dq * jnp.asarray(scale, BF16)
-    dkv = tie_all(dkv, [gate.came[1]] + up.got)
+    dkv = tie_all(dkv, [gate.came[1]])
     dkv = dkv.reshape(2, size // 2, kv_own.shape[0], 2 * kv_cols)
     dkv_own = Scatter(lanes, dkv[1], dkv[0]).result().astype(BF16)
-    up.hop()
-    grad_up = up.result()
     grad_gate = gate.result()
     dqkv = jnp.concatenate([dq, dkv_own], axis=1)
-    dnormed_part = dot_back(dqkv, wide).astype(BF16)
-    grad_out = scatter_grad(lanes, tie(dbranch, dnormed_part), attended).result()
-    grad_query = scatter_grad(lanes, normed, tie(dq, dnormed_part)).result()
+    dnormed_part = tie(dot_back(dqkv, wide).astype(BF16), grad_up)
+    rest = scatter_grads(lanes, [(tie(dbranch, dnormed_part), attended), (normed, tie(dqkv, dnormed_part))]).result()
+    cuts = [0, attended.shape[1], attended.shape[1] + q_cols, attended.shape[1] + q_cols + kv_cols, rest.shape[1]]
+    grad_out, grad_query, grad_key, grad_value = [rest[:, i:j] for i, j in zip(cuts, cuts[1:])]
     term_one = jnp.sum(dnormed_part.astype(F32) * rows_in * inv_rms(rows_in), axis=0)
-    grad_kv = scatter_grad(lanes, normed, tie(dkv_own, dnormed_part)).result()
-    dnormed = tie_all(scatter_tp(dnormed_part), [grad_up, grad_out])
+    dnormed = tie_all(scatter_tp(dnormed_part), [])
     grad_gains = sum_gains(jnp.stack([term_one, term_two, term_three, term_four]))
     grad_tokens = dhidden + norm_input_grad(xf, inv_rms(xf), gains[0], dnormed)
     return (
         mixed,
         grad_tokens,
         grad_query,
-        grad_kv[:, :kv_cols],
-        grad_kv[:, kv_cols:],
+        grad_key,
+        grad_value,
         grad_out.T,
         grad_gate,
         grad_up,

time: 761 us -> 750 us (0.986)
  other arithmetic: 103 us -> 80.6 us
  local copies, waits for them, and re-layouts: 53.4 us -> 71.8 us
  waiting for transfers between devices: 343 us -> 330 us
  starting transfers between devices: 85.5 us -> 97.5 us
    ppermute x50 -> x32, waiting for transfers between devices: 85.1 us -> 47.5 us  [send(): done.append(lax.ppermute(x, 'ctx', pairs))]
    ppermute x3, waiting for transfers between devices: 0.89 us -> 20.7 us  [send(): came = lax.ppermute(jnp.concatenate(values, axis=0), 'ctx', pairs)]
    unnamed x176 -> x154, local copies, waits for them, and re-layouts: 21.4 us -> 37.8 us
    convert_element_type x13 -> x9, other arithmetic: 28.1 us -> 14.1 us  [pack(): self.now[t].astype(BF16)]
    add x5 -> x2, other arithmetic: 13.8 us -> 4.64 us  [hop(): v + parts[flipped(t, s, 1)].astype(F32)]
    ppermute x6, starting transfers between devices: 19.5 us -> 27.5 us  [exchange_tp(): lax.ppermute(take((me + r) % size), 'tp', [(i, (i + r) % size) for i in r...]
    ppermute x9 -> x12, starting transfers between devices: 20.7 us -> 26.6 us  [gather_line(): up = lax.ppermute(up, 'tp', [(i, i + 1) for i in range(s - 1, size - 1)])]
    ppermute x50 -> x32, starting transfers between devices: 22.7 us -> 17 us  [send(): done.append(lax.ppermute(x, 'ctx', pairs))]
  transfers between devices with their start and end apart: 91 -> 79, of which waited for: 37 -> 30; matrix products, arithmetic and copies ran while one was open for 22% -> 19% of each run, Pallas kernels for 11% -> 11%
where the time goes in v3:
time: 750 us; the launch traced here: 740 us
  waiting for transfers between devices  330 us (44%)
  starting transfers between devices  97.5 us (13%)
  Pallas kernels  97.5 us (13%)
  other arithmetic  80.6 us (11%)
  local copies, waits for them, and re-layouts  71.8 us (10%)
  matrix products  46.9 us (6%)
  between operations  16.1 us (2%)
    ppermute x12, waiting for transfers between devices, gather_line(): lax.ppermute(down, 'tp', [(i, i - 1) for i in range(1, size - s + 1)])  99.4 us
    reduce_scatter x3, waiting for transfers between devices, scatter_tp(): lax.psum_scatter(part.astype(BF16), 'tp', scatter_dimension=0, tiled=True)  72.4 us
    all_gather x1, waiting for transfers between devices, gather_tp(): return lax.all_gather(x, 'tp', axis=axis, tiled=True)  49.8 us
    ppermute x32, waiting for transfers between devices, send(): done.append(lax.ppermute(x, 'ctx', pairs))  47.5 us
    unnamed x154, local copies, waits for them, and re-layouts  37.8 us
    pallas_call x2, Pallas kernels, rows_call(): pl.pallas_call(functools.partial(rows_kernel, terms), grid=(width // TILE...  30.5 us
    dot_general x5, matrix products, dot_rows(): lax.dot_general(a, b, (((0,), (0,)), ((), ())), preferred_element_type=F32)  28.8 us
    ppermute x6, starting transfers between devices, exchange_tp(): lax.ppermute(take((me + r) % size), 'tp', [(i, (i + r) % size) for i in r...  27.5 us
  transfers between devices with their start and end apart: 79, of which 30 were waited for; matrix products, arithmetic and copies ran while one was open for 19% of the time, Pallas kernels for 11%

profile of v3, /device:TPU:0, one launch (start us, length us, event | category | flops | bytes accessed | tf_op | source)
XLA Modules:
  0.0 740.1 jit_solution(4096455207106818564)
XLA Ops:
  9.5 5.8 collective-permute-start
  18.4 3.6 pad_maximum_fusion
  27.8 4.2 collective-permute-done.1
  36.5 11.4 %collective-permute-done.2 = bf16[128,2304]{1,0:T(8,128)(2,1)} collective-permute-done((bf16[128,2304]{1,0:T(8,128)(2,1)S(1)}, bf16[128,2304]{1,0:T(8,128)(2,1)}, u32[]{:S(2)}, u32[]{:S(2)}) %collective-permute-start.2) | collective-permute-done | bytes 589856 | tf_op jit(solution)/shard_map/ppermute | solution.py:215
  54.5 8.7 %collective-permute-done.3 = bf16[128,2304]{1,0:T(8,128)(2,1)} collective-permute-done((bf16[128,2304]{1,0:T(8,128)(2,1)}, bf16[128,2304]{1,0:T(8,128)(2,1)}, u32[]{:S(2)}, u32[]{:S(2)}) %collective-permute-start.3) | collective-permute-done | bytes 589856 | tf_op jit(solution)/shard_map/ppermute | solution.py:215
  72.0 4.6 fusion.1
  80.4 6.0 collective-permute-start.16
  86.4 11.2 %collective-permute-done.17 = bf16[1152,512]{1,0:T(8,128)(2,1)} collective-permute-done((bf16[1152,512]{1,0:T(8,128)(2,1)}, bf16[1152,512]{1,0:T(8,128)(2,1)}, u32[]{:S(2)}, u32[]{:S(2)}) %collective-permute-start.17) | collective-permute-done | bytes 1179680 | tf_op jit(solution)/shard_map/ppermute | solution.py:215
  103.9 14.1 %collective-permute-done.9 = bf16[512,512]{1,0:T(8,128)(2,1)} collective-permute-done((bf16[512,512]{1,0:T(8,128)(2,1)S(1)}, bf16[512,512]{1,0:T(8,128)(2,1)}, u32[]{:S(2)}, u32[]{:S(2)}) %collective-permute-start.9) | collective-permute-done | bytes 524320 | tf_op jit(solution)/shard_map/ppermute | solution.py:100
  133.0 11.3 %shard_map.222 = (f32[512,512]{1,0:T(8,128)}, f32[1024,128]{1,0:T(8,128)}) custom-call(s32[4,36]{1,0:T(4,128)} %pad.4.index_ref, s32[4]{0:T(128)} %get-tuple-element.237.count_ref, bf16[512,512]{1,0:T(8,128)(2,1)} %fusion.28.q_ref, bf16[4096,512]{1,0:T(8,128)(2,1)} %copy-done.2, bf16[4096,512]{1,0:T(8,128)(2,1)} %copy-done.2), custom_call_target="tpu_custom_call" | custom-call | flops 2147483648 | bytes 6291456 | tf_op jit(solution)/shard_map/pallas_call | solution.py:342
  146.3 8.1 %collective-permute-done.23 = bf16[1152,512]{1,0:T(8,128)(2,1)} collective-permute-done((bf16[1152,512]{1,0:T(8,128)(2,1)}, bf16[1152,512]{1,0:T(8,128)(2,1)}, u32[]{:S(2)}, u32[]{:S(2)}) %collective-permute-start.23) | collective-permute-done | bytes 1179680 | tf_op jit(solution)/shard_map/ppermute | solution.py:215
  163.6 22.3 %collective-permute-start.20 = (bf16[128,512]{1,0:T(8,128)(2,1)}, bf16[128,512]{1,0:T(8,128)(2,1)}, u32[]{:S(2)}, u32[]{:S(2)}) collective-permute-start(bf16[128,512]{1,0:T(8,128)(2,1)} %get-tuple-element.211), channel_id=1, source_target_pairs={{0,3},{1,0},{2,1},{3,2},{4,7},{5,4},{6,5},{7,6},{8,11},{9,8},{10,9... | collective-permute-start | bytes 393224 | tf_op jit(solution)/shard_map/ppermute | solution.py:232
  191.6 6.7 collective-permute-done.21
  206.5 3.1 constant_dynamic-update-slice_fusion.28
  209.6 3.3 multiply_reduce_fusion.7
  220.2 11.4 %collective-permute-done.26 = bf16[128,2304]{1,0:T(8,128)(2,1)S(1)} collective-permute-done((bf16[128,2304]{1,0:T(8,128)(2,1)}, bf16[128,2304]{1,0:T(8,128)(2,1)S(1)}, u32[]{:S(2)}, u32[]{:S(2)}) %collective-permute-start.26) | collective-permute-done | bytes 589856 | tf_op jit(solution)/shard_map/ppermute | solution.py:214
  231.7 4.7 collective-permute-done.27
  238.4 14.0 %collective-permute-done.28 = bf16[128,2304]{1,0:T(8,128)(2,1)S(1)} collective-permute-done((bf16[128,2304]{1,0:T(8,128)(2,1)S(1)}, bf16[128,2304]{1,0:T(8,128)(2,1)S(1)}, u32[]{:S(2)}, u32[]{:S(2)}) %collective-permute-start.28) | collective-permute-done | bytes 589856 | tf_op jit(solution)/shard_map/ppermute | solution.py:215
  254.4 13.2 %collective-permute-done.29 = bf16[128,2304]{1,0:T(8,128)(2,1)S(1)} collective-permute-done((bf16[128,2304]{1,0:T(8,128)(2,1)S(1)}, bf16[128,2304]{1,0:T(8,128)(2,1)S(1)}, u32[]{:S(2)}, u32[]{:S(2)}) %collective-permute-start.29) | collective-permute-done | bytes 589856 | tf_op jit(solution)/shard_map/ppermute | solution.py:215
  270.5 19.2 %ffn_in.1 = (f32[512,2304]{1,0:T(8,128)}, f32[512,2304]{1,0:T(8,128)}, bf16[512,2304]{1,0:T(8,128)(2,1)}) custom-call(bf16[512,2304]{1,0:T(8,128)(2,1)} %select_dynamic-update-slice_fusion.6.x_ref, bf16[2304,4608]{1,0:T(8,128)(2,1)} %all-gather.7.cloned.1.call-done.gate_w_ref.up_w_ref.refs_2_, ...), custom_call_target="tpu_custom_call" | custom-call | flops 10871635968 | bytes 21233664 | tf_op jit(solution)/shard_map/ffn_in/pallas_call | solution.py:403
  289.7 9.9 %all-gather.9.cloned.1.call-done.refs_1_.w_ref = bf16[2304,2304]{1,0:T(8,128)(2,1)} async-done(((bf16[288,2304]{1,0:T(8,128)(2,1)}), bf16[2304,2304]{1,0:T(8,128)(2,1)}) %all-gather.9.cloned.1.call-update) | async-done | bytes 10616848 | tf_op jit(solution)/shard_map/all_gather | solution.py:580
  299.7 12.4 %ffn_out.1 = bf16[512,2304]{1,0:T(8,128)(2,1)} custom-call(bf16[512,2304]{1,0:T(8,128)(2,1)} %get-tuple-element.91.refs_0_, bf16[2304,2304]{1,0:T(8,128)(2,1)} %all-gather.9.cloned.1.call-done.refs_1_.w_ref), custom_call_target="tpu_custom_call" | custom-call | flops 5435817984 | bytes 10616832 | tf_op jit(solution)/shard_map/ffn_out/pallas_call | solution.py:462
  312.1 48.1 %reduce-scatter.5.cloned.1.call-done = bf16[128,2304]{1,0:T(8,128)(2,1)} async-done(((bf16[512,2304]{1,0:T(8,128)(2,1)}), bf16[128,2304]{1,0:T(8,128)(2,1)}) %reduce-scatter.5.cloned.1.call-update) | async-done | bytes 589840 | tf_op jit(solution)/shard_map/reduce_scatter | solution.py:205
  365.4 49.8 %all-gather.11.cloned.1.call-done.x_ref = bf16[512,2304]{1,0:T(8,128)(2,1)} async-done(((bf16[128,2304]{1,0:T(8,128)(2,1)}), bf16[512,2304]{1,0:T(8,128)(2,1)}) %all-gather.11.cloned.1.call-update) | async-done | bytes 2359312 | tf_op jit(solution)/shard_map/all_gather | solution.py:201
  415.2 8.0 %convolution_convert_fusion.2 = bf16[2304,2304]{1,0:T(8,128)(2,1)S(1)} fusion(bf16[512,2304]{1,0:T(8,128)(2,1)} %all-gather.11.cloned.1.call-done.x_ref, bf16[512,2304]{1,0:T(8,128)(2,1)} %get-tuple-element.91.refs_0_), kind=kOutput, calls=%fused_computation.2 | convolution fusion | flops 5441126400 | bytes 15335424 | tf_op jit(solution)/shard_map/dot_general | solution.py:32
  429.2 15.6 %ffn_back.1 = (bf16[512,2304]{1,0:T(8,128)(2,1)}, bf16[512,2304]{1,0:T(8,128)(2,1)}) custom-call(bf16[512,2304]{1,0:T(8,128)(2,1)} %all-gather.11.cloned.1.call-done.x_ref, f32[512,2304]{1,0:T(8,128)} %get-tuple-element.95.gate_ref, f32[512,2304]{1,0:T(8,128)} %get-tuple-element.96.up_ref, bf16[2304,2304]{1,0:T(8,128)(2,1)} %all-gather.9.cloned.1.call-done.refs_1_.w_ref), custom_call_target="tpu_custom_call" | custom-call | flops 5435817984 | bytes 10616832 | tf_op jit(solution)/shard_map/ffn_back/pallas_call | solution.py:433
  444.7 3.1 add_convert_fusion.5
  451.0 18.1 %ffn_back_in.1 = bf16[512,2304]{1,0:T(8,128)(2,1)} custom-call(bf16[512,2304]{1,0:T(8,128)(2,1)} %get-tuple-element.106.refs_0_, bf16[512,2304]{1,0:T(8,128)(2,1)} %get-tuple-element.131.refs_1_, bf16[2304,4608]{1,0:T(8,128)(2,1)} %all-gather.7.cloned.1.call-done.gate_w_ref.up_w_ref.refs_2_), custom_call_target="tpu_custom_call" | custom-call | flops 10871635968 | bytes 21233664 | tf_op jit(solution)/shard_map/ffn_back_in/pallas_call | solution.py:462
  469.1 8.0 %convolution_convert_fusion.1 = bf16[2304,2304]{1,0:T(8,128)(2,1)S(1)} fusion(bf16[512,2304]{1,0:T(8,128)(2,1)} %select_dynamic-update-slice_fusion.6.x_ref, bf16[512,2304]{1,0:T(8,128)(2,1)} %get-tuple-element.106.refs_0_), kind=kOutput, calls=%fused_computation.1 | convolution fusion | flops 5441126400 | bytes 15335424 | tf_op jit(solution)/shard_map/dot_general | solution.py:32
  487.9 3.1 add_convert_fusion.2
  492.8 11.3 %collective-permute-done.36 = bf16[288,2304]{1,0:T(8,128)(2,1)} collective-permute-done((bf16[288,2304]{1,0:T(8,128)(2,1)S(1)}, bf16[288,2304]{1,0:T(8,128)(2,1)}, u32[]{:S(2)}, u32[]{:S(2)}) %collective-permute-start.36) | collective-permute-done | bytes 1327136 | tf_op jit(solution)/shard_map/ppermute | solution.py:100
  505.2 24.2 %reduce-scatter.7.cloned.1.call-done = bf16[128,2304]{1,0:T(8,128)(2,1)} async-done(((bf16[512,2304]{1,0:T(8,128)(2,1)}), bf16[128,2304]{1,0:T(8,128)(2,1)}) %reduce-scatter.7.cloned.1.call-update) | async-done | bytes 589840 | tf_op jit(solution)/shard_map/reduce_scatter | solution.py:205
  530.7 5.6 collective-permute-done.40
  536.3 3.7 add_convert_fusion
  548.2 8.4 %convolution_convert_fusion = bf16[2304,2304]{1,0:T(8,128)(2,1)} fusion(bf16[512,2304]{1,0:T(8,128)(2,1)S(1)} %copy-done.13, bf16[512,2304]{1,0:T(8,128)(2,1)S(1)} %copy-done.57), kind=kOutput, calls=%fused_computation | convolution fusion | flops 5441126400 | bytes 15335424 | tf_op jit(solution)/shard_map/dot_general | solution.py:32
  565.8 5.8 collective-permute-done.42
  580.9 5.4 collective-permute-start.53
  589.5 20.9 %shard_map.223 = (bf16[512,512]{1,0:T(8,128)(2,1)}, f32[4096,512]{1,0:T(8,128)}) custom-call(s32[4,36]{1,0:T(4,128)} %pad.4.index_ref, s32[4]{0:T(128)} %get-tuple-element.237.count_ref, bf16[512,512]{1,0:T(8,128)(2,1)} %fusion.28.q_ref, bf16[512,512]{1,0:T(8,128)(2,1)} %constant_dynamic-slice_fusion.30.dout_ref, f32[512,512]{1,0:T(8,128)} %get-tuple-element.83.out_ref, ...), custom_call_target="tpu_custom_call" | custom-call | flops 5368709120 | bytes 16777216 | tf_op jit(solution)/shard_map/pallas_call | solution.py:364
  612.7 4.2 convert.10
  618.1 10.2 %collective-permute-done.55 = bf16[128,2304]{1,0:T(8,128)(2,1)S(1)} collective-permute-done((bf16[128,2304]{1,0:T(8,128)(2,1)S(1)}, bf16[128,2304]{1,0:T(8,128)(2,1)S(1)}, u32[]{:S(2)}, u32[]{:S(2)}) %collective-permute-start.55) | collective-permute-done | bytes 589856 | tf_op jit(solution)/shard_map/ppermute | solution.py:215
  632.8 12.6 %collective-permute-done.56 = bf16[128,2304]{1,0:T(8,128)(2,1)S(1)} collective-permute-done((bf16[128,2304]{1,0:T(8,128)(2,1)S(1)}, bf16[128,2304]{1,0:T(8,128)(2,1)S(1)}, u32[]{:S(2)}, u32[]{:S(2)}) %collective-permute-start.56) | collective-permute-done | bytes 589856 | tf_op jit(solution)/shard_map/ppermute | solution.py:215
  648.4 7.5 %collective-permute-done.52 = bf16[512,512]{1,0:T(8,128)(2,1)S(1)} collective-permute-done((bf16[512,512]{1,0:T(8,128)(2,1)S(1)}, bf16[512,512]{1,0:T(8,128)(2,1)S(1)}, u32[]{:S(2)}, u32[]{:S(2)}) %collective-permute-start.52) | collective-permute-done | bytes 524320 | tf_op jit(solution)/shard_map/ppermute | solution.py:100
  656.4 6.2 convolution_convert_fusion.5
  681.1 20.7 %collective-permute-done.66 = f32[8,288]{1,0:T(8,128)S(1)} collective-permute-done((f32[8,288]{1,0:T(8,128)S(1)}, f32[8,288]{1,0:T(8,128)S(1)}, u32[]{:S(2)}, u32[]{:S(2)}) %collective-permute-start.66) | collective-permute-done | bytes 9248 | tf_op jit(solution)/shard_map/ppermute | solution.py:536
  703.3 4.7 add_bitcast_fusion
  708.1 3.3 collective-permute-start.70
  713.9 4.2 convert_add_fusion
  718.7 7.6 %collective-permute-done.64 = bf16[288,1536]{1,0:T(8,128)(2,1)S(1)} collective-permute-done((bf16[288,1536]{1,0:T(8,128)(2,1)S(1)}, bf16[288,1536]{1,0:T(8,128)(2,1)S(1)}, u32[]{:S(2)}, u32[]{:S(2)}) %collective-permute-start.64) | collective-permute-done | bytes 884768 | tf_op jit(solution)/shard_map/ppermute | solution.py:100
  (405 shorter events, 194.5 us)
Async XLA Ops:
  7.2 58.7 %all-gather.5.cloned.1.call-start = ((), (), s32[]{:S(2)}) async-start(), calls=%async_computation.4 | async-start | bytes 7962624 | tf_op jit(solution)/shard_map/all_gather | solution.py:580
  9.5 210.7 %all-gather.7.cloned.1.call-start = ((), (), s32[]{:S(2)}) async-start(), calls=%async_computation.5 | async-start | bytes 23887872 | tf_op jit(solution)/shard_map/all_gather | solution.py:580
  9.5 25.5 %collective-permute-start = (bf16[128,2304]{1,0:T(8,128)(2,1)S(1)}, bf16[128,2304]{1,0:T(8,128)(2,1)}, u32[]{:S(2)}, u32[]{:S(2)}) collective-permute-start(bf16[128,2304]{1,0:T(8,128)(2,1)S(1)} %copy-done.17), channel_id=1, source_target_pairs={{0,1},{1,2},{2,3},{4,5},{5,6},{6,7},{8,9},{9,10},{10,11},{12,13},{... | collective-permute-start | bytes 1769480 | tf_op jit(solution)/shard_map/ppermute | solution.py:214
  15.3 16.7 %collective-permute-start.1 = (bf16[128,2304]{1,0:T(8,128)(2,1)S(1)}, bf16[128,2304]{1,0:T(8,128)(2,1)S(1)}, u32[]{:S(2)}, u32[]{:S(2)}) collective-permute-start(bf16[128,2304]{1,0:T(8,128)(2,1)S(1)} %copy-done.17), channel_id=1, source_target_pairs={{1,0},{2,1},{3,2},{5,4},{6,5},{7,6},{9,8},{10,9},{11,10},{13,12},{... | collective-permute-start | bytes 1769480 | tf_op jit(solution)/shard_map/ppermute | solution.py:215
  32.0 16.0 %collective-permute-start.2 = (bf16[128,2304]{1,0:T(8,128)(2,1)S(1)}, bf16[128,2304]{1,0:T(8,128)(2,1)}, u32[]{:S(2)}, u32[]{:S(2)}) collective-permute-start(bf16[128,2304]{1,0:T(8,128)(2,1)S(1)} %collective-permute-done.1), channel_id=1, source_target_pairs={{1,0},{2,1},{5,4},{6,5},{9,8},{10,9},{13,12},{14,13},{17,16},{18,1... | collective-permute-start | bytes 1769480 | tf_op jit(solution)/shard_map/ppermute | solution.py:215
  35.0 18.8 %collective-permute-start.4 = (bf16[128,2304]{1,0:T(8,128)(2,1)}, bf16[128,2304]{1,0:T(8,128)(2,1)}, u32[]{:S(2)}, u32[]{:S(2)}) collective-permute-start(bf16[128,2304]{1,0:T(8,128)(2,1)} %collective-permute-done), channel_id=1, source_target_pairs={{1,2},{2,3},{5,6},{6,7},{9,10},{10,11},{13,14},{14,15},{17,18},{18... | collective-permute-start | bytes 1769480 | tf_op jit(solution)/shard_map/ppermute | solution.py:214
  65.9 233.8 %all-gather.9.cloned.1.call-start = ((), (), s32[]{:S(2)}) async-start(), calls=%async_computation.6 | async-start | bytes 11943936 | tf_op jit(solution)/shard_map/all_gather | solution.py:580
  70.6 27.0 %collective-permute-start.17 = (bf16[1152,512]{1,0:T(8,128)(2,1)}, bf16[1152,512]{1,0:T(8,128)(2,1)}, u32[]{:S(2)}, u32[]{:S(2)}) collective-permute-start(bf16[1152,512]{1,0:T(8,128)(2,1)} %dynamic-slice), channel_id=1, source_target_pairs={{1,0},{2,1},{3,2},{5,4},{6,5},{7,6},{9,8},{10,9},{11,10},{13,12},{... | collective-permute-start | bytes 3538952 | tf_op jit(solution)/shard_map/ppermute | solution.py:215
  78.7 22.1 %collective-permute-start.10 = (bf16[512,512]{1,0:T(8,128)(2,1)S(1)}, bf16[512,512]{1,0:T(8,128)(2,1)}, u32[]{:S(2)}, u32[]{:S(2)}) collective-permute-start(bf16[512,512]{1,0:T(8,128)(2,1)S(1)} %get-tuple-element.164), channel_id=1, source_target_pairs={{0,16},{4,12},{8,24},{12,4},{16,0},{20,28},{24,8},{28,20},{1,17},{... | collective-permute-start | bytes 1572872 | tf_op jit(solution)/shard_map/ppermute | solution.py:100
  80.3 20.6 %collective-permute-start.12 = (bf16[512,512]{1,0:T(8,128)(2,1)S(1)}, bf16[512,512]{1,0:T(8,128)(2,1)}, u32[]{:S(2)}, u32[]{:S(2)}) collective-permute-start(bf16[512,512]{1,0:T(8,128)(2,1)S(1)} %get-tuple-element.164), channel_id=1, source_target_pairs={{0,4},{4,0},{8,12},{12,8},{16,20},{20,16},{24,28},{28,24},{1,5},{5... | collective-permute-start | bytes 1572872 | tf_op jit(solution)/shard_map/ppermute | solution.py:100
  80.4 40.0 %collective-permute-start.16 = (bf16[1152,512]{1,0:T(8,128)(2,1)}, bf16[1152,512]{1,0:T(8,128)(2,1)}, u32[]{:S(2)}, u32[]{:S(2)}) collective-permute-start(bf16[1152,512]{1,0:T(8,128)(2,1)} %dynamic-slice), channel_id=1, source_target_pairs={{0,1},{1,2},{2,3},{4,5},{5,6},{6,7},{8,9},{9,10},{10,11},{12,13},{... | collective-permute-start | bytes 3538952 | tf_op jit(solution)/shard_map/ppermute | solution.py:214
  97.6 26.1 %collective-permute-start.19 = (bf16[1152,512]{1,0:T(8,128)(2,1)}, bf16[1152,512]{1,0:T(8,128)(2,1)}, u32[]{:S(2)}, u32[]{:S(2)}) collective-permute-start(bf16[1152,512]{1,0:T(8,128)(2,1)} %collective-permute-done.17), channel_id=1, source_target_pairs={{1,0},{2,1},{5,4},{6,5},{9,8},{10,9},{13,12},{14,13},{17,16},{18,1... | collective-permute-start | bytes 3538952 | tf_op jit(solution)/shard_map/ppermute | solution.py:215
  99.3 18.7 %collective-permute-start.9 = (bf16[512,512]{1,0:T(8,128)(2,1)S(1)}, bf16[512,512]{1,0:T(8,128)(2,1)}, u32[]{:S(2)}, u32[]{:S(2)}) collective-permute-start(bf16[512,512]{1,0:T(8,128)(2,1)S(1)} %get-tuple-element.164), channel_id=1, source_target_pairs={{0,8},{4,20},{8,0},{12,28},{16,24},{20,4},{24,16},{28,12},{1,9},{5... | collective-permute-start | bytes 1572872 | tf_op jit(solution)/shard_map/ppermute | solution.py:100
  100.9 17.2 %collective-permute-start.13 = (bf16[512,512]{1,0:T(8,128)(2,1)}, bf16[512,512]{1,0:T(8,128)(2,1)}, u32[]{:S(2)}, u32[]{:S(2)}) collective-permute-start(bf16[512,512]{1,0:T(8,128)(2,1)} %collective-permute-done.10), channel_id=1, source_target_pairs={{0,4},{4,0},{8,12},{12,8},{16,20},{20,16},{24,28},{28,24},{1,5},{5... | collective-permute-start | bytes 1572872 | tf_op jit(solution)/shard_map/ppermute | solution.py:100
  103.4 23.6 %collective-permute-start.11 = (bf16[512,512]{1,0:T(8,128)(2,1)}, bf16[512,512]{1,0:T(8,128)(2,1)S(1)}, u32[]{:S(2)}, u32[]{:S(2)}) collective-permute-start(bf16[512,512]{1,0:T(8,128)(2,1)} %collective-permute-done.10), channel_id=1, source_target_pairs={{0,8},{4,20},{8,0},{12,28},{16,24},{20,4},{24,16},{28,12},{1,9},{5... | collective-permute-start | bytes 1572872 | tf_op jit(solution)/shard_map/ppermute | solution.py:100
  120.4 25.2 %collective-permute-start.18 = (bf16[1152,512]{1,0:T(8,128)(2,1)}, bf16[1152,512]{1,0:T(8,128)(2,1)}, u32[]{:S(2)}, u32[]{:S(2)}) collective-permute-start(bf16[1152,512]{1,0:T(8,128)(2,1)} %collective-permute-done.16), channel_id=1, source_target_pairs={{1,2},{2,3},{5,6},{6,7},{9,10},{10,11},{13,14},{14,15},{17,18},{18... | collective-permute-start | bytes 3538952 | tf_op jit(solution)/shard_map/ppermute | solution.py:214
  123.7 30.8 %collective-permute-start.23 = (bf16[1152,512]{1,0:T(8,128)(2,1)}, bf16[1152,512]{1,0:T(8,128)(2,1)}, u32[]{:S(2)}, u32[]{:S(2)}) collective-permute-start(bf16[1152,512]{1,0:T(8,128)(2,1)} %collective-permute-done.19), channel_id=1, source_target_pairs={{1,0},{5,4},{9,8},{13,12},{17,16},{21,20},{25,24},{29,28}} | collective-permute-start | bytes 3538952 | tf_op jit(solution)/shard_map/ppermute | solution.py:215
  162.8 43.7 %collective-permute-start.25 = (bf16[1152,2048]{1,0:T(8,128)(2,1)}, bf16[1152,2048]{1,0:T(8,128)(2,1)}, u32[]{:S(2)}, u32[]{:S(2)}) collective-permute-start(bf16[1152,2048]{1,0:T(8,128)(2,1)} %select_dynamic-update-slice_fusion), channel_id=1, source_target_pairs={{0,4},{4,0},{8,12},{12,8},{16,20},{20,16},{24,28},{28,24},{1,5},{5... | collective-permute-start | bytes 14155784 | tf_op jit(solution)/shard_map/ppermute | solution.py:100
  163.6 26.5 %collective-permute-start.20 = (bf16[128,512]{1,0:T(8,128)(2,1)}, bf16[128,512]{1,0:T(8,128)(2,1)}, u32[]{:S(2)}, u32[]{:S(2)}) collective-permute-start(bf16[128,512]{1,0:T(8,128)(2,1)} %get-tuple-element.211), channel_id=1, source_target_pairs={{0,3},{1,0},{2,1},{3,2},{4,7},{5,4},{6,5},{7,6},{8,11},{9,8},{10,9... | collective-permute-start | bytes 393224 | tf_op jit(solution)/shard_map/ppermute | solution.py:232
  218.9 17.4 %collective-permute-start.27 = (bf16[128,2304]{1,0:T(8,128)(2,1)}, bf16[128,2304]{1,0:T(8,128)(2,1)S(1)}, u32[]{:S(2)}, u32[]{:S(2)}) collective-permute-start(bf16[128,2304]{1,0:T(8,128)(2,1)} %get-tuple-element.160), channel_id=1, source_target_pairs={{1,0},{2,1},{3,2},{5,4},{6,5},{7,6},{9,8},{10,9},{11,10},{13,12},{... | collective-permute-start | bytes 1769480 | tf_op jit(solution)/shard_map/ppermute | solution.py:215
  236.4 123.9 %reduce-scatter.5.cloned.1.call-start = ((), (), s32[]{:S(2)}) async-start(), calls=%async_computation.7 | async-start | bytes 2949120 | tf_op jit(solution)/shard_map/reduce_scatter | solution.py:205
  236.4 16.0 %collective-permute-start.28 = (bf16[128,2304]{1,0:T(8,128)(2,1)S(1)}, bf16[128,2304]{1,0:T(8,128)(2,1)S(1)}, u32[]{:S(2)}, u32[]{:S(2)}) collective-permute-start(bf16[128,2304]{1,0:T(8,128)(2,1)S(1)} %collective-permute-done.27), channel_id=1, source_target_pairs={{1,0},{2,1},{5,4},{6,5},{9,8},{10,9},{13,12},{14,13},{17,16},{18,1... | collective-permute-start | bytes 1769480 | tf_op jit(solution)/shard_map/ppermute | solution.py:215
  237.7 16.0 %collective-permute-start.30 = (bf16[128,2304]{1,0:T(8,128)(2,1)S(1)}, bf16[128,2304]{1,0:T(8,128)(2,1)S(1)}, u32[]{:S(2)}, u32[]{:S(2)}) collective-permute-start(bf16[128,2304]{1,0:T(8,128)(2,1)S(1)} %collective-permute-done.26), channel_id=1, source_target_pairs={{1,2},{2,3},{5,6},{6,7},{9,10},{10,11},{13,14},{14,15},{17,18},{18... | collective-permute-start | bytes 1769480 | tf_op jit(solution)/shard_map/ppermute | solution.py:214
  253.7 15.8 %collective-permute-start.31 = (bf16[128,2304]{1,0:T(8,128)(2,1)S(1)}, bf16[128,2304]{1,0:T(8,128)(2,1)S(1)}, u32[]{:S(2)}, u32[]{:S(2)}) collective-permute-start(bf16[128,2304]{1,0:T(8,128)(2,1)S(1)} %collective-permute-done.30), channel_id=1, source_target_pairs={{2,3},{6,7},{10,11},{14,15},{18,19},{22,23},{26,27},{30,31}} | collective-permute-start | bytes 1769480 | tf_op jit(solution)/shard_map/ppermute | solution.py:214
  312.1 103.1 %all-gather.11.cloned.1.call-start = ((), (), s32[]{:S(2)}) async-start(), calls=%async_computation.8 | async-start | bytes 2949120 | tf_op jit(solution)/shard_map/all_gather | solution.py:201
  365.0 164.4 %reduce-scatter.7.cloned.1.call-start = ((), (), s32[]{:S(2)}) async-start(), calls=%async_computation.9 | async-start | bytes 2949120 | tf_op jit(solution)/shard_map/reduce_scatter | solution.py:205
  428.6 16.1 %collective-permute-start.32 = (bf16[288,2304]{1,0:T(8,128)(2,1)}, bf16[288,2304]{1,0:T(8,128)(2,1)}, u32[]{:S(2)}, u32[]{:S(2)}) collective-permute-start(bf16[288,2304]{1,0:T(8,128)(2,1)} %get-tuple-element.98), channel_id=1, source_target_pairs={{0,4},{4,0},{8,12},{12,8},{16,20},{20,16},{24,28},{28,24},{1,5},{5... | collective-permute-start | bytes 3981320 | tf_op jit(solution)/shard_map/ppermute | solution.py:100
  428.7 16.1 %collective-permute-start.33 = (bf16[288,2304]{1,0:T(8,128)(2,1)}, bf16[288,2304]{1,0:T(8,128)(2,1)}, u32[]{:S(2)}, u32[]{:S(2)}) collective-permute-start(bf16[288,2304]{1,0:T(8,128)(2,1)} %get-tuple-element.99), channel_id=1, source_target_pairs={{0,4},{4,0},{8,12},{12,8},{16,20},{20,16},{24,28},{28,24},{1,5},{5... | collective-permute-start | bytes 3981320 | tf_op jit(solution)/shard_map/ppermute | solution.py:100
  429.2 54.3 %collective-permute-start.34 = (bf16[288,2304]{1,0:T(8,128)(2,1)}, bf16[288,2304]{1,0:T(8,128)(2,1)}, u32[]{:S(2)}, u32[]{:S(2)}) collective-permute-start(bf16[288,2304]{1,0:T(8,128)(2,1)} %get-tuple-element.102), channel_id=1, source_target_pairs={{0,4},{4,0},{8,12},{12,8},{16,20},{20,16},{24,28},{28,24},{1,5},{5... | collective-permute-start | bytes 3981320 | tf_op jit(solution)/shard_map/ppermute | solution.py:100
  449.6 33.1 %collective-permute-start.35 = (bf16[576,2304]{1,0:T(8,128)(2,1)}, bf16[576,2304]{1,0:T(8,128)(2,1)}, u32[]{:S(2)}, u32[]{:S(2)}) collective-permute-start(bf16[576,2304]{1,0:T(8,128)(2,1)} %pad_maximum_fusion.1), channel_id=1, source_target_pairs={{0,16},{4,12},{8,24},{12,4},{16,0},{20,28},{24,8},{28,20},{1,17},{... | collective-permute-start | bytes 7962632 | tf_op jit(solution)/shard_map/ppermute | solution.py:100
  483.2 179.5 %reduce-scatter.9.cloned.1.call-start = ((), (), s32[]{:S(2)}) async-start(), calls=%async_computation.10 | async-start | bytes 11943936 | tf_op jit(solution)/shard_map/reduce_scatter | solution.py:645
  486.0 18.0 %collective-permute-start.36 = (bf16[288,2304]{1,0:T(8,128)(2,1)S(1)}, bf16[288,2304]{1,0:T(8,128)(2,1)}, u32[]{:S(2)}, u32[]{:S(2)}) collective-permute-start(bf16[288,2304]{1,0:T(8,128)(2,1)S(1)} %add_convert_fusion.3), channel_id=1, source_target_pairs={{0,8},{4,20},{8,0},{12,28},{16,24},{20,4},{24,16},{28,12},{1,9},{5... | collective-permute-start | bytes 3981320 | tf_op jit(solution)/shard_map/ppermute | solution.py:100
  504.0 32.3 %collective-permute-start.40 = (bf16[576,2304]{1,0:T(8,128)(2,1)}, bf16[576,2304]{1,0:T(8,128)(2,1)}, u32[]{:S(2)}, u32[]{:S(2)}) collective-permute-start(bf16[576,2304]{1,0:T(8,128)(2,1)} %pad_maximum_fusion.2), channel_id=1, source_target_pairs={{0,16},{4,12},{8,24},{12,4},{16,0},{20,28},{24,8},{28,20},{1,17},{... | collective-permute-start | bytes 7962632 | tf_op jit(solution)/shard_map/ppermute | solution.py:100
  505.2 25.5 %collective-permute-start.37 = (bf16[288,2304]{1,0:T(8,128)(2,1)}, bf16[288,2304]{1,0:T(8,128)(2,1)}, u32[]{:S(2)}, u32[]{:S(2)}) collective-permute-start(bf16[288,2304]{1,0:T(8,128)(2,1)} %get-tuple-element.108), channel_id=1, source_target_pairs={{0,4},{4,0},{8,12},{12,8},{16,20},{20,16},{24,28},{28,24},{1,5},{5... | collective-permute-start | bytes 3981320 | tf_op jit(solution)/shard_map/ppermute | solution.py:100
  556.6 172.1 %reduce-scatter.11.cloned.1.call-start = ((), (), s32[]{:S(2)}) async-start(), calls=%async_computation.11 | async-start | bytes 2949120 | tf_op jit(solution)/shard_map/reduce_scatter | solution.py:205
  556.6 30.2 %collective-permute-start.45 = (bf16[288,2304]{1,0:T(8,128)(2,1)}, bf16[288,2304]{1,0:T(8,128)(2,1)}, u32[]{:S(2)}, u32[]{:S(2)}) collective-permute-start(bf16[288,2304]{1,0:T(8,128)(2,1)} %get-tuple-element.123), channel_id=1, source_target_pairs={{0,4},{4,0},{8,12},{12,8},{16,20},{20,16},{24,28},{28,24},{1,5},{5... | collective-permute-start | bytes 3981320 | tf_op jit(solution)/shard_map/ppermute | solution.py:100
  561.6 51.0 %collective-permute-start.44 = (bf16[288,2304]{1,0:T(8,128)(2,1)}, bf16[288,2304]{1,0:T(8,128)(2,1)}, u32[]{:S(2)}, u32[]{:S(2)}) collective-permute-start(bf16[288,2304]{1,0:T(8,128)(2,1)} %add_convert_fusion), channel_id=1, source_target_pairs={{0,8},{4,20},{8,0},{12,28},{16,24},{20,4},{24,16},{28,12},{1,9},{5... | collective-permute-start | bytes 3981320 | tf_op jit(solution)/shard_map/ppermute | solution.py:100
  579.6 30.8 %collective-permute-start.54 = (bf16[128,2304]{1,0:T(8,128)(2,1)S(1)}, bf16[128,2304]{1,0:T(8,128)(2,1)S(1)}, u32[]{:S(2)}, u32[]{:S(2)}) collective-permute-start(bf16[128,2304]{1,0:T(8,128)(2,1)S(1)} %copy-done.20), channel_id=1, source_target_pairs={{1,0},{2,1},{3,2},{5,4},{6,5},{7,6},{9,8},{10,9},{11,10},{13,12},{... | collective-permute-start | bytes 1769480 | tf_op jit(solution)/shard_map/ppermute | solution.py:215
  580.9 30.8 %collective-permute-start.53 = (bf16[128,2304]{1,0:T(8,128)(2,1)S(1)}, bf16[128,2304]{1,0:T(8,128)(2,1)}, u32[]{:S(2)}, u32[]{:S(2)}) collective-permute-start(bf16[128,2304]{1,0:T(8,128)(2,1)S(1)} %copy-done.20), channel_id=1, source_target_pairs={{0,1},{1,2},{2,3},{4,5},{5,6},{6,7},{8,9},{9,10},{10,11},{12,13},{... | collective-permute-start | bytes 1769480 | tf_op jit(solution)/shard_map/ppermute | solution.py:214
  586.9 43.5 %collective-permute-start.46 = (bf16[288,2304]{1,0:T(8,128)(2,1)}, bf16[288,2304]{1,0:T(8,128)(2,1)S(1)}, u32[]{:S(2)}, u32[]{:S(2)}) collective-permute-start(bf16[288,2304]{1,0:T(8,128)(2,1)} %get-tuple-element.124), channel_id=1, source_target_pairs={{0,4},{4,0},{8,12},{12,8},{16,20},{20,16},{24,28},{28,24},{1,5},{5... | collective-permute-start | bytes 3981320 | tf_op jit(solution)/shard_map/ppermute | solution.py:100
  610.4 17.9 %collective-permute-start.55 = (bf16[128,2304]{1,0:T(8,128)(2,1)S(1)}, bf16[128,2304]{1,0:T(8,128)(2,1)S(1)}, u32[]{:S(2)}, u32[]{:S(2)}) collective-permute-start(bf16[128,2304]{1,0:T(8,128)(2,1)S(1)} %collective-permute-done.54), channel_id=1, source_target_pairs={{1,0},{2,1},{5,4},{6,5},{9,8},{10,9},{13,12},{14,13},{17,16},{18,1... | collective-permute-start | bytes 1769480 | tf_op jit(solution)/shard_map/ppermute | solution.py:215
  611.7 18.0 %collective-permute-start.57 = (bf16[128,2304]{1,0:T(8,128)(2,1)}, bf16[128,2304]{1,0:T(8,128)(2,1)S(1)}, u32[]{:S(2)}, u32[]{:S(2)}) collective-permute-start(bf16[128,2304]{1,0:T(8,128)(2,1)} %collective-permute-done.53), channel_id=1, source_target_pairs={{1,2},{2,3},{5,6},{6,7},{9,10},{10,11},{13,14},{14,15},{17,18},{18... | collective-permute-start | bytes 1769480 | tf_op jit(solution)/shard_map/ppermute | solution.py:214
  628.3 17.1 %collective-permute-start.56 = (bf16[128,2304]{1,0:T(8,128)(2,1)S(1)}, bf16[128,2304]{1,0:T(8,128)(2,1)S(1)}, u32[]{:S(2)}, u32[]{:S(2)}) collective-permute-start(bf16[128,2304]{1,0:T(8,128)(2,1)S(1)} %collective-permute-done.55), channel_id=1, source_target_pairs={{1,0},{5,4},{9,8},{13,12},{17,16},{21,20},{25,24},{29,28}} | collective-permute-start | bytes 1769480 | tf_op jit(solution)/shard_map/ppermute | solution.py:215
  629.6 18.6 %collective-permute-start.58 = (bf16[128,2304]{1,0:T(8,128)(2,1)S(1)}, bf16[128,2304]{1,0:T(8,128)(2,1)S(1)}, u32[]{:S(2)}, u32[]{:S(2)}) collective-permute-start(bf16[128,2304]{1,0:T(8,128)(2,1)S(1)} %collective-permute-done.57), channel_id=1, source_target_pairs={{2,3},{6,7},{10,11},{14,15},{18,19},{22,23},{26,27},{30,31}} | collective-permute-start | bytes 1769480 | tf_op jit(solution)/shard_map/ppermute | solution.py:214
  630.5 17.9 %collective-permute-start.47 = (bf16[512,512]{1,0:T(8,128)(2,1)S(1)}, bf16[512,512]{1,0:T(8,128)(2,1)S(1)}, u32[]{:S(2)}, u32[]{:S(2)}) collective-permute-start(bf16[512,512]{1,0:T(8,128)(2,1)S(1)} %get-tuple-element.125), channel_id=1, source_target_pairs={{0,4},{4,0},{8,12},{12,8},{16,20},{20,16},{24,28},{28,24},{1,5},{5... | collective-permute-start | bytes 1572872 | tf_op jit(solution)/shard_map/ppermute | solution.py:100
  678.9 34.0 %collective-permute-start.62 = (bf16[576,1536]{1,0:T(8,128)(2,1)}, bf16[576,1536]{1,0:T(8,128)(2,1)S(1)}, u32[]{:S(2)}, u32[]{:S(2)}) collective-permute-start(bf16[576,1536]{1,0:T(8,128)(2,1)} %pad_maximum_fusion.3), channel_id=1, source_target_pairs={{0,16},{4,12},{8,24},{12,4},{16,0},{20,28},{24,8},{28,20},{1,17},{... | collective-permute-start | bytes 5308424 | tf_op jit(solution)/shard_map/ppermute | solution.py:100
  680.1 21.6 %collective-permute-start.66 = (f32[8,288]{1,0:T(8,128)S(1)}, f32[8,288]{1,0:T(8,128)S(1)}, u32[]{:S(2)}, u32[]{:S(2)}) collective-permute-start(f32[8,288]{1,0:T(8,128)S(1)} %pad_maximum_fusion.14), channel_id=1, source_target_pairs={{0,16},{4,12},{8,24},{12,4},{16,0},{20,28},{24,8},{28,20},{1,17},{... | collective-permute-start | bytes 27656 | tf_op jit(solution)/shard_map/ppermute | solution.py:536
  681.1 30.4 %collective-permute-start.63 = (bf16[288,1536]{1,0:T(8,128)(2,1)}, bf16[288,1536]{1,0:T(8,128)(2,1)S(1)}, u32[]{:S(2)}, u32[]{:S(2)}) collective-permute-start(bf16[288,1536]{1,0:T(8,128)(2,1)} %get-tuple-element.140), channel_id=1, source_target_pairs={{0,4},{4,0},{8,12},{12,8},{16,20},{20,16},{24,28},{28,24},{1,5},{5... | collective-permute-start | bytes 2654216 | tf_op jit(solution)/shard_map/ppermute | solution.py:100
  (96 other events, 1015.3 us)
Sparse Core Ops, SparseCore 0:
  10.5 51.6 all-gather.4
  66.0 124.3 all-gather.6
  236.5 63.1 all-gather.8
  312.2 48.0 reduce-scatter.4
  365.1 49.9 all-gather.10
  483.3 46.0 reduce-scatter.6
  556.7 80.6 reduce-scatter.8
  665.8 48.0 reduce-scatter.10

commit v4 on v3

--- a/solution.py
+++ b/solution.py
@@ -382,7 +382,8 @@
 
 GELU = 0.7978845608028654
 CUBIC = 0.044715
-TILE = 256
+TILE = 768
+PAIR_TILE = 256
 
 
 def ffn_in_kernel(x_ref, gate_w_ref, up_w_ref, gate_ref, up_ref, mid_ref):
@@ -459,12 +460,13 @@
 def rows_call(xs, w, name):
     rows, depth = xs[0].shape
     width, terms = w.shape[0], len(xs)
+    tile = TILE if terms == 1 else PAIR_TILE
     return pl.pallas_call(
         functools.partial(rows_kernel, terms),
-        grid=(width // TILE,),
+        grid=(width // tile,),
         in_specs=[pl.BlockSpec((rows, depth), lambda i: (0, 0), pipeline_mode=pl.Buffered(1))] * terms
-        + [pl.BlockSpec((TILE, terms * depth), lambda i: (i, 0))],
-        out_specs=pl.BlockSpec((rows, TILE), lambda i: (0, i)),
+        + [pl.BlockSpec((tile, terms * depth), lambda i: (i, 0))],
+        out_specs=pl.BlockSpec((rows, tile), lambda i: (0, i)),
         out_shape=jax.ShapeDtypeStruct((rows, width), BF16),
         compiler_params=pltpu.CompilerParams(vmem_limit_bytes=VMEM_LIMIT),
         cost_estimate=pl.CostEstimate(
@@ -616,7 +618,7 @@
     hidden = xf + branch * s_branch * gains[1]
     s_hidden = inv_rms(hidden)
     inner = gather_line((hidden * s_hidden * gains[2]).astype(BF16), steps=inner_steps)
-    down_t = gather_weight(tie_all(w_down.T, [pair_w] + inner_steps[0]))
+    down_t = gather_weight(tie_all(w_down.T, [pair_w, branch]))
     gate_pre, up_pre, mid = ffn_in(inner, pair_w)
     feed = scatter_tp(rows_call([mid], down_t, "ffn_out"))
     s_feed = inv_rms(feed)

time: 750 us -> 732 us (0.976)
  waiting for transfers between devices: 330 us -> 314 us
    ppermute x12, waiting for transfers between devices: 11.5 us -> 0.03 us  [gather_line(): up = lax.ppermute(up, 'tp', [(i, i + 1) for i in range(s - 1, size - 1)])]
    all_gather x3, waiting for transfers between devices: 9.96 us -> 0.02 us  [gather_weight(): return lax.all_gather(w, 'ctx', axis=0, tiled=True)]
    unnamed x154 -> x146, local copies, waits for them, and re-layouts: 37.8 us -> 40.3 us
  transfers between devices with their start and end apart: 79 -> 79, of which waited for: 30 -> 28; matrix products, arithmetic and copies ran while one was open for 19% -> 19% of each run, Pallas kernels for 11% -> 11%
where the time goes in v4:
time: 732 us; the launch traced here: 723 us
  waiting for transfers between devices  314 us (43%)
  starting transfers between devices  101 us (14%)
  Pallas kernels  92.3 us (13%)
  other arithmetic  80.6 us (11%)
  local copies, waits for them, and re-layouts  71.1 us (10%)
  matrix products  48.6 us (7%)
  between operations  15.8 us (2%)
    ppermute x12, waiting for transfers between devices, gather_line(): lax.ppermute(down, 'tp', [(i, i - 1) for i in range(1, size - s + 1)])  103 us
    reduce_scatter x3, waiting for transfers between devices, scatter_tp(): lax.psum_scatter(part.astype(BF16), 'tp', scatter_dimension=0, tiled=True)  74.2 us
    all_gather x1, waiting for transfers between devices, gather_tp(): return lax.all_gather(x, 'tp', axis=axis, tiled=True)  49.8 us
    ppermute x32, waiting for transfers between devices, send(): done.append(lax.ppermute(x, 'ctx', pairs))  47.1 us
    unnamed x146, local copies, waits for them, and re-layouts  40.3 us
    ppermute x6, starting transfers between devices, exchange_tp(): lax.ppermute(take((me + r) % size), 'tp', [(i, (i + r) % size) for i in r...  29.4 us
    dot_general x5, matrix products, dot_rows(): lax.dot_general(a, b, (((0,), (0,)), ((), ())), preferred_element_type=F32)  28.8 us
    ppermute x12, starting transfers between devices, gather_line(): up = lax.ppermute(up, 'tp', [(i, i + 1) for i in range(s - 1, size - 1)])  28.2 us
  transfers between devices with their start and end apart: 79, of which 28 were waited for; matrix products, arithmetic and copies ran while one was open for 19% of the time, Pallas kernels for 11%

profile of v4, /device:TPU:0, one launch (start us, length us, event | category | flops | bytes accessed | tf_op | source)
XLA Modules:
  0.0 722.9 jit_solution(2509002258822583645)
XLA Ops:
  9.5 5.8 collective-permute-start
  18.4 3.6 pad_maximum_fusion
  27.8 4.2 collective-permute-done.1
  35.7 12.2 %collective-permute-done.2 = bf16[128,2304]{1,0:T(8,128)(2,1)} collective-permute-done((bf16[128,2304]{1,0:T(8,128)(2,1)S(1)}, bf16[128,2304]{1,0:T(8,128)(2,1)}, u32[]{:S(2)}, u32[]{:S(2)}) %collective-permute-start.2) | collective-permute-done | bytes 589856 | tf_op jit(solution)/shard_map/ppermute | solution.py:215
  54.5 8.7 %collective-permute-done.3 = bf16[128,2304]{1,0:T(8,128)(2,1)} collective-permute-done((bf16[128,2304]{1,0:T(8,128)(2,1)}, bf16[128,2304]{1,0:T(8,128)(2,1)}, u32[]{:S(2)}, u32[]{:S(2)}) %collective-permute-start.3) | collective-permute-done | bytes 589856 | tf_op jit(solution)/shard_map/ppermute | solution.py:215
  70.3 4.6 fusion.1
  79.5 5.6 collective-permute-start.16
  85.0 10.7 %collective-permute-done.17 = bf16[1152,512]{1,0:T(8,128)(2,1)} collective-permute-done((bf16[1152,512]{1,0:T(8,128)(2,1)S(1)}, bf16[1152,512]{1,0:T(8,128)(2,1)}, u32[]{:S(2)}, u32[]{:S(2)}) %collective-permute-start.17) | collective-permute-done | bytes 1179680 | tf_op jit(solution)/shard_map/ppermute | solution.py:215
  106.3 10.5 %collective-permute-done.9 = bf16[512,512]{1,0:T(8,128)(2,1)} collective-permute-done((bf16[512,512]{1,0:T(8,128)(2,1)}, bf16[512,512]{1,0:T(8,128)(2,1)}, u32[]{:S(2)}, u32[]{:S(2)}) %collective-permute-start.9) | collective-permute-done | bytes 524320 | tf_op jit(solution)/shard_map/ppermute | solution.py:100
  131.6 11.4 %shard_map.222 = (f32[512,512]{1,0:T(8,128)}, f32[1024,128]{1,0:T(8,128)}) custom-call(s32[4,36]{1,0:T(4,128)} %pad.4.index_ref, s32[4]{0:T(128)} %get-tuple-element.235.count_ref, bf16[512,512]{1,0:T(8,128)(2,1)} %fusion.28.q_ref, bf16[4096,512]{1,0:T(8,128)(2,1)} %copy-done.2, bf16[4096,512]{1,0:T(8,128)(2,1)} %copy-done.2), custom_call_target="tpu_custom_call" | custom-call | flops 2147483648 | bytes 6291456 | tf_op jit(solution)/shard_map/pallas_call | solution.py:342
  145.1 6.8 collective-permute-done.23
  160.8 24.2 %collective-permute-start.20 = (bf16[128,512]{1,0:T(8,128)(2,1)}, bf16[128,512]{1,0:T(8,128)(2,1)S(1)}, u32[]{:S(2)}, u32[]{:S(2)}) collective-permute-start(bf16[128,512]{1,0:T(8,128)(2,1)} %get-tuple-element.209), channel_id=1, source_target_pairs={{0,3},{1,0},{2,1},{3,2},{4,7},{5,4},{6,5},{7,6},{8,11},{9,8},{10,9... | collective-permute-start | bytes 393224 | tf_op jit(solution)/shard_map/ppermute | solution.py:232
  189.8 7.4 %collective-permute-done.21 = bf16[128,512]{1,0:T(8,128)(2,1)S(1)} collective-permute-done((bf16[128,512]{1,0:T(8,128)(2,1)S(1)}, bf16[128,512]{1,0:T(8,128)(2,1)S(1)}, u32[]{:S(2)}, u32[]{:S(2)}) %collective-permute-start.21) | collective-permute-done | bytes 131104 | tf_op jit(solution)/shard_map/ppermute | solution.py:232
  206.2 3.6 copy-done
  209.9 3.8 multiply_reduce_fusion.7
  218.8 4.6 collective-permute-start.26
  223.4 10.7 %collective-permute-done.27 = bf16[128,2304]{1,0:T(8,128)(2,1)S(1)} collective-permute-done((bf16[128,2304]{1,0:T(8,128)(2,1)S(1)}, bf16[128,2304]{1,0:T(8,128)(2,1)S(1)}, u32[]{:S(2)}, u32[]{:S(2)}) %collective-permute-start.27) | collective-permute-done | bytes 589856 | tf_op jit(solution)/shard_map/ppermute | solution.py:215
  236.1 13.8 %collective-permute-done.28 = bf16[128,2304]{1,0:T(8,128)(2,1)S(1)} collective-permute-done((bf16[128,2304]{1,0:T(8,128)(2,1)S(1)}, bf16[128,2304]{1,0:T(8,128)(2,1)S(1)}, u32[]{:S(2)}, u32[]{:S(2)}) %collective-permute-start.28) | collective-permute-done | bytes 589856 | tf_op jit(solution)/shard_map/ppermute | solution.py:215
  251.9 13.0 %collective-permute-done.29 = bf16[128,2304]{1,0:T(8,128)(2,1)S(1)} collective-permute-done((bf16[128,2304]{1,0:T(8,128)(2,1)S(1)}, bf16[128,2304]{1,0:T(8,128)(2,1)S(1)}, u32[]{:S(2)}, u32[]{:S(2)}) %collective-permute-start.29) | collective-permute-done | bytes 589856 | tf_op jit(solution)/shard_map/ppermute | solution.py:215
  266.8 17.7 %ffn_in.1 = (f32[512,2304]{1,0:T(8,128)}, f32[512,2304]{1,0:T(8,128)}, bf16[512,2304]{1,0:T(8,128)(2,1)}) custom-call(bf16[512,2304]{1,0:T(8,128)(2,1)} %copy-done.12, bf16[2304,4608]{1,0:T(8,128)(2,1)} %all-gather.7.cloned.1.call-done.gate_w_ref.up_w_ref.refs_2_, bf16[2304,4608]{1,0:T(8,128)(2,1)} %all-gather.7.cloned.1.call-done.gate_w_ref.up_w_ref.refs_2_), custom_call_target="tpu_custom_call" | custom-call | flops 10871635968 | bytes 21233664 | tf_op jit(solution)/shard_map/ffn_in/pallas_call | solution.py:404
  284.5 10.0 %ffn_out.1 = bf16[512,2304]{1,0:T(8,128)(2,1)} custom-call(bf16[512,2304]{1,0:T(8,128)(2,1)} %get-tuple-element.90.refs_0_, bf16[2304,2304]{1,0:T(8,128)(2,1)} %all-gather.9.cloned.1.call-done.refs_1_.w_ref), custom_call_target="tpu_custom_call" | custom-call | flops 5435817984 | bytes 10616832 | tf_op jit(solution)/shard_map/ffn_out/pallas_call | solution.py:464
  294.5 50.1 %reduce-scatter.5.cloned.1.call-done = bf16[128,2304]{1,0:T(8,128)(2,1)} async-done(((bf16[512,2304]{1,0:T(8,128)(2,1)}), bf16[128,2304]{1,0:T(8,128)(2,1)}) %reduce-scatter.5.cloned.1.call-update) | async-done | bytes 589840 | tf_op jit(solution)/shard_map/reduce_scatter | solution.py:205
  349.7 49.8 %all-gather.11.cloned.1.call-done.x_ref = bf16[512,2304]{1,0:T(8,128)(2,1)} async-done(((bf16[128,2304]{1,0:T(8,128)(2,1)}), bf16[512,2304]{1,0:T(8,128)(2,1)}) %all-gather.11.cloned.1.call-update) | async-done | bytes 2359312 | tf_op jit(solution)/shard_map/all_gather | solution.py:201
  399.5 8.0 %convolution_convert_fusion.2 = bf16[2304,2304]{1,0:T(8,128)(2,1)S(1)} fusion(bf16[512,2304]{1,0:T(8,128)(2,1)} %all-gather.11.cloned.1.call-done.x_ref, bf16[512,2304]{1,0:T(8,128)(2,1)} %get-tuple-element.90.refs_0_), kind=kOutput, calls=%fused_computation.2 | convolution fusion | flops 5441126400 | bytes 15335424 | tf_op jit(solution)/shard_map/dot_general | solution.py:32
  413.5 14.2 %ffn_back.1 = (bf16[512,2304]{1,0:T(8,128)(2,1)}, bf16[512,2304]{1,0:T(8,128)(2,1)}) custom-call(bf16[512,2304]{1,0:T(8,128)(2,1)} %all-gather.11.cloned.1.call-done.x_ref, f32[512,2304]{1,0:T(8,128)} %get-tuple-element.93.gate_ref, f32[512,2304]{1,0:T(8,128)} %get-tuple-element.94.up_ref, bf16[2304,2304]{1,0:T(8,128)(2,1)} %all-gather.9.cloned.1.call-done.refs_1_.w_ref), custom_call_target="tpu_custom_call" | custom-call | flops 5435817984 | bytes 10616832 | tf_op jit(solution)/shard_map/ffn_back/pallas_call | solution.py:434
  427.7 3.1 add_convert_fusion.5
  434.0 18.1 %ffn_back_in.1 = bf16[512,2304]{1,0:T(8,128)(2,1)} custom-call(bf16[512,2304]{1,0:T(8,128)(2,1)} %get-tuple-element.104.refs_0_, bf16[512,2304]{1,0:T(8,128)(2,1)} %get-tuple-element.129.refs_1_, bf16[2304,4608]{1,0:T(8,128)(2,1)} %all-gather.7.cloned.1.call-done.gate_w_ref.up_w_ref.refs_2_), custom_call_target="tpu_custom_call" | custom-call | flops 10871635968 | bytes 21233664 | tf_op jit(solution)/shard_map/ffn_back_in/pallas_call | solution.py:464
  452.1 8.0 %convolution_convert_fusion.1 = bf16[2304,2304]{1,0:T(8,128)(2,1)S(1)} fusion(bf16[512,2304]{1,0:T(8,128)(2,1)} %copy-done.12, bf16[512,2304]{1,0:T(8,128)(2,1)} %get-tuple-element.104.refs_0_), kind=kOutput, calls=%fused_computation.1 | convolution fusion | flops 5441126400 | bytes 15335424 | tf_op jit(solution)/shard_map/dot_general | solution.py:32
  470.9 3.1 add_convert_fusion.2
  475.7 11.2 %collective-permute-done.36 = bf16[288,2304]{1,0:T(8,128)(2,1)} collective-permute-done((bf16[288,2304]{1,0:T(8,128)(2,1)S(1)}, bf16[288,2304]{1,0:T(8,128)(2,1)}, u32[]{:S(2)}, u32[]{:S(2)}) %collective-permute-start.36) | collective-permute-done | bytes 1327136 | tf_op jit(solution)/shard_map/ppermute | solution.py:100
  488.2 24.2 %reduce-scatter.7.cloned.1.call-done = bf16[128,2304]{1,0:T(8,128)(2,1)} async-done(((bf16[512,2304]{1,0:T(8,128)(2,1)}), bf16[128,2304]{1,0:T(8,128)(2,1)}) %reduce-scatter.7.cloned.1.call-update) | async-done | bytes 589840 | tf_op jit(solution)/shard_map/reduce_scatter | solution.py:205
  513.6 5.7 collective-permute-done.40
  519.3 3.7 add_convert_fusion
  531.1 8.4 %convolution_convert_fusion = bf16[2304,2304]{1,0:T(8,128)(2,1)} fusion(bf16[512,2304]{1,0:T(8,128)(2,1)S(1)} %copy-done.13, bf16[512,2304]{1,0:T(8,128)(2,1)S(1)} %copy-done.53), kind=kOutput, calls=%fused_computation | convolution fusion | flops 5441126400 | bytes 15335424 | tf_op jit(solution)/shard_map/dot_general | solution.py:32
  548.7 5.9 collective-permute-done.42
  563.8 5.4 collective-permute-start.53
  572.4 20.9 %shard_map.223 = (bf16[512,512]{1,0:T(8,128)(2,1)}, f32[4096,512]{1,0:T(8,128)}) custom-call(s32[4,36]{1,0:T(4,128)} %pad.4.index_ref, s32[4]{0:T(128)} %get-tuple-element.235.count_ref, bf16[512,512]{1,0:T(8,128)(2,1)} %fusion.28.q_ref, bf16[512,512]{1,0:T(8,128)(2,1)} %constant_dynamic-slice_fusion.30.dout_ref, f32[512,512]{1,0:T(8,128)} %get-tuple-element.82.out_ref, ...), custom_call_target="tpu_custom_call" | custom-call | flops 5368709120 | bytes 16777216 | tf_op jit(solution)/shard_map/pallas_call | solution.py:364
  595.6 4.2 convert.10
  600.8 8.9 %collective-permute-done.55 = bf16[128,2304]{1,0:T(8,128)(2,1)S(1)} collective-permute-done((bf16[128,2304]{1,0:T(8,128)(2,1)S(1)}, bf16[128,2304]{1,0:T(8,128)(2,1)S(1)}, u32[]{:S(2)}, u32[]{:S(2)}) %collective-permute-start.55) | collective-permute-done | bytes 589856 | tf_op jit(solution)/shard_map/ppermute | solution.py:215
  614.1 11.1 %collective-permute-done.56 = bf16[128,2304]{1,0:T(8,128)(2,1)S(1)} collective-permute-done((bf16[128,2304]{1,0:T(8,128)(2,1)S(1)}, bf16[128,2304]{1,0:T(8,128)(2,1)S(1)}, u32[]{:S(2)}, u32[]{:S(2)}) %collective-permute-start.56) | collective-permute-done | bytes 589856 | tf_op jit(solution)/shard_map/ppermute | solution.py:215
  625.5 3.9 collective-permute-done.50
  631.4 7.5 %collective-permute-done.52 = bf16[512,512]{1,0:T(8,128)(2,1)S(1)} collective-permute-done((bf16[512,512]{1,0:T(8,128)(2,1)S(1)}, bf16[512,512]{1,0:T(8,128)(2,1)S(1)}, u32[]{:S(2)}, u32[]{:S(2)}) %collective-permute-start.52) | collective-permute-done | bytes 524320 | tf_op jit(solution)/shard_map/ppermute | solution.py:100
  639.4 6.2 convolution_convert_fusion.5
  664.0 20.7 %collective-permute-done.66 = f32[8,288]{1,0:T(8,128)S(1)} collective-permute-done((f32[8,288]{1,0:T(8,128)S(1)}, f32[8,288]{1,0:T(8,128)S(1)}, u32[]{:S(2)}, u32[]{:S(2)}) %collective-permute-start.66) | collective-permute-done | bytes 9248 | tf_op jit(solution)/shard_map/ppermute | solution.py:538
  686.3 4.7 add_bitcast_fusion
  691.1 3.3 collective-permute-start.70
  697.0 4.2 convert_add_fusion
  701.8 7.7 %collective-permute-done.64 = bf16[288,1536]{1,0:T(8,128)(2,1)S(1)} collective-permute-done((bf16[288,1536]{1,0:T(8,128)(2,1)S(1)}, bf16[288,1536]{1,0:T(8,128)(2,1)S(1)}, u32[]{:S(2)}, u32[]{:S(2)}) %collective-permute-start.64) | collective-permute-done | bytes 884768 | tf_op jit(solution)/shard_map/ppermute | solution.py:100
  (397 shorter events, 192.2 us)
Async XLA Ops:
  7.2 58.7 %all-gather.5.cloned.1.call-start = ((), (), s32[]{:S(2)}) async-start(), calls=%async_computation.4 | async-start | bytes 7962624 | tf_op jit(solution)/shard_map/all_gather | solution.py:582
  9.5 204.2 %all-gather.7.cloned.1.call-start = ((), (), s32[]{:S(2)}) async-start(), calls=%async_computation.5 | async-start | bytes 23887872 | tf_op jit(solution)/shard_map/all_gather | solution.py:582
  9.5 25.5 %collective-permute-start = (bf16[128,2304]{1,0:T(8,128)(2,1)S(1)}, bf16[128,2304]{1,0:T(8,128)(2,1)}, u32[]{:S(2)}, u32[]{:S(2)}) collective-permute-start(bf16[128,2304]{1,0:T(8,128)(2,1)S(1)} %copy-done.17), channel_id=1, source_target_pairs={{0,1},{1,2},{2,3},{4,5},{5,6},{6,7},{8,9},{9,10},{10,11},{12,13},{... | collective-permute-start | bytes 1769480 | tf_op jit(solution)/shard_map/ppermute | solution.py:214
  15.3 16.7 %collective-permute-start.1 = (bf16[128,2304]{1,0:T(8,128)(2,1)S(1)}, bf16[128,2304]{1,0:T(8,128)(2,1)S(1)}, u32[]{:S(2)}, u32[]{:S(2)}) collective-permute-start(bf16[128,2304]{1,0:T(8,128)(2,1)S(1)} %copy-done.17), channel_id=1, source_target_pairs={{1,0},{2,1},{3,2},{5,4},{6,5},{7,6},{9,8},{10,9},{11,10},{13,12},{... | collective-permute-start | bytes 1769480 | tf_op jit(solution)/shard_map/ppermute | solution.py:215
  32.0 16.0 %collective-permute-start.2 = (bf16[128,2304]{1,0:T(8,128)(2,1)S(1)}, bf16[128,2304]{1,0:T(8,128)(2,1)}, u32[]{:S(2)}, u32[]{:S(2)}) collective-permute-start(bf16[128,2304]{1,0:T(8,128)(2,1)S(1)} %collective-permute-done.1), channel_id=1, source_target_pairs={{1,0},{2,1},{5,4},{6,5},{9,8},{10,9},{13,12},{14,13},{17,16},{18,1... | collective-permute-start | bytes 1769480 | tf_op jit(solution)/shard_map/ppermute | solution.py:215
  35.0 18.8 %collective-permute-start.4 = (bf16[128,2304]{1,0:T(8,128)(2,1)}, bf16[128,2304]{1,0:T(8,128)(2,1)S(1)}, u32[]{:S(2)}, u32[]{:S(2)}) collective-permute-start(bf16[128,2304]{1,0:T(8,128)(2,1)} %collective-permute-done), channel_id=1, source_target_pairs={{1,2},{2,3},{5,6},{6,7},{9,10},{10,11},{13,14},{14,15},{17,18},{18... | collective-permute-start | bytes 1769480 | tf_op jit(solution)/shard_map/ppermute | solution.py:214
  48.0 15.3 %collective-permute-start.3 = (bf16[128,2304]{1,0:T(8,128)(2,1)}, bf16[128,2304]{1,0:T(8,128)(2,1)}, u32[]{:S(2)}, u32[]{:S(2)}) collective-permute-start(bf16[128,2304]{1,0:T(8,128)(2,1)} %collective-permute-done.2), channel_id=1, source_target_pairs={{1,0},{5,4},{9,8},{13,12},{17,16},{21,20},{25,24},{29,28}} | collective-permute-start | bytes 1769480 | tf_op jit(solution)/shard_map/ppermute | solution.py:215
  65.9 218.5 %all-gather.9.cloned.1.call-start = ((), (), s32[]{:S(2)}) async-start(), calls=%async_computation.6 | async-start | bytes 11943936 | tf_op jit(solution)/shard_map/all_gather | solution.py:582
  69.0 26.8 %collective-permute-start.17 = (bf16[1152,512]{1,0:T(8,128)(2,1)S(1)}, bf16[1152,512]{1,0:T(8,128)(2,1)}, u32[]{:S(2)}, u32[]{:S(2)}) collective-permute-start(bf16[1152,512]{1,0:T(8,128)(2,1)S(1)} %dynamic-slice), channel_id=1, source_target_pairs={{1,0},{2,1},{3,2},{5,4},{6,5},{7,6},{9,8},{10,9},{11,10},{13,12},{... | collective-permute-start | bytes 3538952 | tf_op jit(solution)/shard_map/ppermute | solution.py:215
  77.3 24.1 %collective-permute-start.10 = (bf16[512,512]{1,0:T(8,128)(2,1)}, bf16[512,512]{1,0:T(8,128)(2,1)}, u32[]{:S(2)}, u32[]{:S(2)}) collective-permute-start(bf16[512,512]{1,0:T(8,128)(2,1)} %get-tuple-element.162), channel_id=1, source_target_pairs={{0,16},{4,12},{8,24},{12,4},{16,0},{20,28},{24,8},{28,20},{1,17},{... | collective-permute-start | bytes 1572872 | tf_op jit(solution)/shard_map/ppermute | solution.py:100
  78.8 22.6 %collective-permute-start.12 = (bf16[512,512]{1,0:T(8,128)(2,1)}, bf16[512,512]{1,0:T(8,128)(2,1)}, u32[]{:S(2)}, u32[]{:S(2)}) collective-permute-start(bf16[512,512]{1,0:T(8,128)(2,1)} %get-tuple-element.162), channel_id=1, source_target_pairs={{0,4},{4,0},{8,12},{12,8},{16,20},{20,16},{24,28},{28,24},{1,5},{5... | collective-permute-start | bytes 1572872 | tf_op jit(solution)/shard_map/ppermute | solution.py:100
  79.5 38.1 %collective-permute-start.16 = (bf16[1152,512]{1,0:T(8,128)(2,1)S(1)}, bf16[1152,512]{1,0:T(8,128)(2,1)}, u32[]{:S(2)}, u32[]{:S(2)}) collective-permute-start(bf16[1152,512]{1,0:T(8,128)(2,1)S(1)} %dynamic-slice), channel_id=1, source_target_pairs={{0,1},{1,2},{2,3},{4,5},{5,6},{6,7},{8,9},{9,10},{10,11},{12,13},{... | collective-permute-start | bytes 3538952 | tf_op jit(solution)/shard_map/ppermute | solution.py:214
  95.8 26.1 %collective-permute-start.19 = (bf16[1152,512]{1,0:T(8,128)(2,1)}, bf16[1152,512]{1,0:T(8,128)(2,1)}, u32[]{:S(2)}, u32[]{:S(2)}) collective-permute-start(bf16[1152,512]{1,0:T(8,128)(2,1)} %collective-permute-done.17), channel_id=1, source_target_pairs={{1,0},{2,1},{5,4},{6,5},{9,8},{10,9},{13,12},{14,13},{17,16},{18,1... | collective-permute-start | bytes 3538952 | tf_op jit(solution)/shard_map/ppermute | solution.py:215
  99.9 16.9 %collective-permute-start.9 = (bf16[512,512]{1,0:T(8,128)(2,1)}, bf16[512,512]{1,0:T(8,128)(2,1)}, u32[]{:S(2)}, u32[]{:S(2)}) collective-permute-start(bf16[512,512]{1,0:T(8,128)(2,1)} %get-tuple-element.162), channel_id=1, source_target_pairs={{0,8},{4,20},{8,0},{12,28},{16,24},{20,4},{24,16},{28,12},{1,9},{5... | collective-permute-start | bytes 1572872 | tf_op jit(solution)/shard_map/ppermute | solution.py:100
  101.4 15.4 %collective-permute-start.13 = (bf16[512,512]{1,0:T(8,128)(2,1)}, bf16[512,512]{1,0:T(8,128)(2,1)}, u32[]{:S(2)}, u32[]{:S(2)}) collective-permute-start(bf16[512,512]{1,0:T(8,128)(2,1)} %collective-permute-done.10), channel_id=1, source_target_pairs={{0,4},{4,0},{8,12},{12,8},{16,20},{20,16},{24,28},{28,24},{1,5},{5... | collective-permute-start | bytes 1572872 | tf_op jit(solution)/shard_map/ppermute | solution.py:100
  105.7 19.4 %collective-permute-start.11 = (bf16[512,512]{1,0:T(8,128)(2,1)}, bf16[512,512]{1,0:T(8,128)(2,1)S(1)}, u32[]{:S(2)}, u32[]{:S(2)}) collective-permute-start(bf16[512,512]{1,0:T(8,128)(2,1)} %collective-permute-done.10), channel_id=1, source_target_pairs={{0,8},{4,20},{8,0},{12,28},{16,24},{20,4},{24,16},{28,12},{1,9},{5... | collective-permute-start | bytes 1572872 | tf_op jit(solution)/shard_map/ppermute | solution.py:100
  117.6 26.7 %collective-permute-start.18 = (bf16[1152,512]{1,0:T(8,128)(2,1)}, bf16[1152,512]{1,0:T(8,128)(2,1)}, u32[]{:S(2)}, u32[]{:S(2)}) collective-permute-start(bf16[1152,512]{1,0:T(8,128)(2,1)} %collective-permute-done.16), channel_id=1, source_target_pairs={{1,2},{2,3},{5,6},{6,7},{9,10},{10,11},{13,14},{14,15},{17,18},{18... | collective-permute-start | bytes 3538952 | tf_op jit(solution)/shard_map/ppermute | solution.py:214
  121.8 30.1 %collective-permute-start.23 = (bf16[1152,512]{1,0:T(8,128)(2,1)}, bf16[1152,512]{1,0:T(8,128)(2,1)}, u32[]{:S(2)}, u32[]{:S(2)}) collective-permute-start(bf16[1152,512]{1,0:T(8,128)(2,1)} %collective-permute-done.19), channel_id=1, source_target_pairs={{1,0},{5,4},{9,8},{13,12},{17,16},{21,20},{25,24},{29,28}} | collective-permute-start | bytes 3538952 | tf_op jit(solution)/shard_map/ppermute | solution.py:215
  160.0 43.1 %collective-permute-start.25 = (bf16[1152,2048]{1,0:T(8,128)(2,1)}, bf16[1152,2048]{1,0:T(8,128)(2,1)}, u32[]{:S(2)}, u32[]{:S(2)}) collective-permute-start(bf16[1152,2048]{1,0:T(8,128)(2,1)} %select_dynamic-update-slice_fusion), channel_id=1, source_target_pairs={{0,4},{4,0},{8,12},{12,8},{16,20},{20,16},{24,28},{28,24},{1,5},{5... | collective-permute-start | bytes 14155784 | tf_op jit(solution)/shard_map/ppermute | solution.py:100
  160.8 28.4 %collective-permute-start.20 = (bf16[128,512]{1,0:T(8,128)(2,1)}, bf16[128,512]{1,0:T(8,128)(2,1)S(1)}, u32[]{:S(2)}, u32[]{:S(2)}) collective-permute-start(bf16[128,512]{1,0:T(8,128)(2,1)} %get-tuple-element.209), channel_id=1, source_target_pairs={{0,3},{1,0},{2,1},{3,2},{4,7},{5,4},{6,5},{7,6},{8,11},{9,8},{10,9... | collective-permute-start | bytes 393224 | tf_op jit(solution)/shard_map/ppermute | solution.py:232
  213.7 130.8 %reduce-scatter.5.cloned.1.call-start = ((), (), s32[]{:S(2)}) async-start(), calls=%async_computation.7 | async-start | bytes 2949120 | tf_op jit(solution)/shard_map/reduce_scatter | solution.py:205
  217.5 16.6 %collective-permute-start.27 = (bf16[128,2304]{1,0:T(8,128)(2,1)S(1)}, bf16[128,2304]{1,0:T(8,128)(2,1)S(1)}, u32[]{:S(2)}, u32[]{:S(2)}) collective-permute-start(bf16[128,2304]{1,0:T(8,128)(2,1)S(1)} %get-tuple-element.158), channel_id=1, source_target_pairs={{1,0},{2,1},{3,2},{5,4},{6,5},{7,6},{9,8},{10,9},{11,10},{13,12},{... | collective-permute-start | bytes 1769480 | tf_op jit(solution)/shard_map/ppermute | solution.py:215
  218.8 16.6 %collective-permute-start.26 = (bf16[128,2304]{1,0:T(8,128)(2,1)S(1)}, bf16[128,2304]{1,0:T(8,128)(2,1)S(1)}, u32[]{:S(2)}, u32[]{:S(2)}) collective-permute-start(bf16[128,2304]{1,0:T(8,128)(2,1)S(1)} %get-tuple-element.158), channel_id=1, source_target_pairs={{0,1},{1,2},{2,3},{4,5},{5,6},{6,7},{8,9},{9,10},{10,11},{12,13},{... | collective-permute-start | bytes 1769480 | tf_op jit(solution)/shard_map/ppermute | solution.py:214
  234.1 15.8 %collective-permute-start.28 = (bf16[128,2304]{1,0:T(8,128)(2,1)S(1)}, bf16[128,2304]{1,0:T(8,128)(2,1)S(1)}, u32[]{:S(2)}, u32[]{:S(2)}) collective-permute-start(bf16[128,2304]{1,0:T(8,128)(2,1)S(1)} %collective-permute-done.27), channel_id=1, source_target_pairs={{1,0},{2,1},{5,4},{6,5},{9,8},{10,9},{13,12},{14,13},{17,16},{18,1... | collective-permute-start | bytes 1769480 | tf_op jit(solution)/shard_map/ppermute | solution.py:215
  235.4 15.8 %collective-permute-start.30 = (bf16[128,2304]{1,0:T(8,128)(2,1)S(1)}, bf16[128,2304]{1,0:T(8,128)(2,1)S(1)}, u32[]{:S(2)}, u32[]{:S(2)}) collective-permute-start(bf16[128,2304]{1,0:T(8,128)(2,1)S(1)} %collective-permute-done.26), channel_id=1, source_target_pairs={{1,2},{2,3},{5,6},{6,7},{9,10},{10,11},{13,14},{14,15},{17,18},{18... | collective-permute-start | bytes 1769480 | tf_op jit(solution)/shard_map/ppermute | solution.py:214
  294.5 105.0 %all-gather.11.cloned.1.call-start = ((), (), s32[]{:S(2)}) async-start(), calls=%async_computation.8 | async-start | bytes 2949120 | tf_op jit(solution)/shard_map/all_gather | solution.py:201
  349.3 163.0 %reduce-scatter.7.cloned.1.call-start = ((), (), s32[]{:S(2)}) async-start(), calls=%async_computation.9 | async-start | bytes 2949120 | tf_op jit(solution)/shard_map/reduce_scatter | solution.py:205
  413.5 53.0 %collective-permute-start.34 = (bf16[288,2304]{1,0:T(8,128)(2,1)}, bf16[288,2304]{1,0:T(8,128)(2,1)}, u32[]{:S(2)}, u32[]{:S(2)}) collective-permute-start(bf16[288,2304]{1,0:T(8,128)(2,1)} %get-tuple-element.100), channel_id=1, source_target_pairs={{0,4},{4,0},{8,12},{12,8},{16,20},{20,16},{24,28},{28,24},{1,5},{5... | collective-permute-start | bytes 3981320 | tf_op jit(solution)/shard_map/ppermute | solution.py:100
  432.5 33.1 %collective-permute-start.35 = (bf16[576,2304]{1,0:T(8,128)(2,1)}, bf16[576,2304]{1,0:T(8,128)(2,1)}, u32[]{:S(2)}, u32[]{:S(2)}) collective-permute-start(bf16[576,2304]{1,0:T(8,128)(2,1)} %pad_maximum_fusion.1), channel_id=1, source_target_pairs={{0,16},{4,12},{8,24},{12,4},{16,0},{20,28},{24,8},{28,20},{1,17},{... | collective-permute-start | bytes 7962632 | tf_op jit(solution)/shard_map/ppermute | solution.py:100
  466.2 179.5 %reduce-scatter.9.cloned.1.call-start = ((), (), s32[]{:S(2)}) async-start(), calls=%async_computation.10 | async-start | bytes 11943936 | tf_op jit(solution)/shard_map/reduce_scatter | solution.py:647
  469.0 18.0 %collective-permute-start.36 = (bf16[288,2304]{1,0:T(8,128)(2,1)S(1)}, bf16[288,2304]{1,0:T(8,128)(2,1)}, u32[]{:S(2)}, u32[]{:S(2)}) collective-permute-start(bf16[288,2304]{1,0:T(8,128)(2,1)S(1)} %add_convert_fusion.3), channel_id=1, source_target_pairs={{0,8},{4,20},{8,0},{12,28},{16,24},{20,4},{24,16},{28,12},{1,9},{5... | collective-permute-start | bytes 3981320 | tf_op jit(solution)/shard_map/ppermute | solution.py:100
  487.0 32.3 %collective-permute-start.40 = (bf16[576,2304]{1,0:T(8,128)(2,1)}, bf16[576,2304]{1,0:T(8,128)(2,1)}, u32[]{:S(2)}, u32[]{:S(2)}) collective-permute-start(bf16[576,2304]{1,0:T(8,128)(2,1)} %pad_maximum_fusion.2), channel_id=1, source_target_pairs={{0,16},{4,12},{8,24},{12,4},{16,0},{20,28},{24,8},{28,20},{1,17},{... | collective-permute-start | bytes 7962632 | tf_op jit(solution)/shard_map/ppermute | solution.py:100
  488.2 25.4 %collective-permute-start.37 = (bf16[288,2304]{1,0:T(8,128)(2,1)}, bf16[288,2304]{1,0:T(8,128)(2,1)}, u32[]{:S(2)}, u32[]{:S(2)}) collective-permute-start(bf16[288,2304]{1,0:T(8,128)(2,1)} %get-tuple-element.106), channel_id=1, source_target_pairs={{0,4},{4,0},{8,12},{12,8},{16,20},{20,16},{24,28},{28,24},{1,5},{5... | collective-permute-start | bytes 3981320 | tf_op jit(solution)/shard_map/ppermute | solution.py:100
  539.6 172.3 %reduce-scatter.11.cloned.1.call-start = ((), (), s32[]{:S(2)}) async-start(), calls=%async_computation.11 | async-start | bytes 2949120 | tf_op jit(solution)/shard_map/reduce_scatter | solution.py:205
  539.6 30.2 %collective-permute-start.45 = (bf16[288,2304]{1,0:T(8,128)(2,1)}, bf16[288,2304]{1,0:T(8,128)(2,1)}, u32[]{:S(2)}, u32[]{:S(2)}) collective-permute-start(bf16[288,2304]{1,0:T(8,128)(2,1)} %get-tuple-element.121), channel_id=1, source_target_pairs={{0,4},{4,0},{8,12},{12,8},{16,20},{20,16},{24,28},{28,24},{1,5},{5... | collective-permute-start | bytes 3981320 | tf_op jit(solution)/shard_map/ppermute | solution.py:100
  544.6 51.0 %collective-permute-start.44 = (bf16[288,2304]{1,0:T(8,128)(2,1)}, bf16[288,2304]{1,0:T(8,128)(2,1)}, u32[]{:S(2)}, u32[]{:S(2)}) collective-permute-start(bf16[288,2304]{1,0:T(8,128)(2,1)} %add_convert_fusion), channel_id=1, source_target_pairs={{0,8},{4,20},{8,0},{12,28},{16,24},{20,4},{24,16},{28,12},{1,9},{5... | collective-permute-start | bytes 3981320 | tf_op jit(solution)/shard_map/ppermute | solution.py:100
  562.5 30.8 %collective-permute-start.54 = (bf16[128,2304]{1,0:T(8,128)(2,1)S(1)}, bf16[128,2304]{1,0:T(8,128)(2,1)S(1)}, u32[]{:S(2)}, u32[]{:S(2)}) collective-permute-start(bf16[128,2304]{1,0:T(8,128)(2,1)S(1)} %copy-done.20), channel_id=1, source_target_pairs={{1,0},{2,1},{3,2},{5,4},{6,5},{7,6},{9,8},{10,9},{11,10},{13,12},{... | collective-permute-start | bytes 1769480 | tf_op jit(solution)/shard_map/ppermute | solution.py:215
  563.8 30.8 %collective-permute-start.53 = (bf16[128,2304]{1,0:T(8,128)(2,1)S(1)}, bf16[128,2304]{1,0:T(8,128)(2,1)}, u32[]{:S(2)}, u32[]{:S(2)}) collective-permute-start(bf16[128,2304]{1,0:T(8,128)(2,1)S(1)} %copy-done.20), channel_id=1, source_target_pairs={{0,1},{1,2},{2,3},{4,5},{5,6},{6,7},{8,9},{9,10},{10,11},{12,13},{... | collective-permute-start | bytes 1769480 | tf_op jit(solution)/shard_map/ppermute | solution.py:214
  569.8 41.9 %collective-permute-start.46 = (bf16[288,2304]{1,0:T(8,128)(2,1)}, bf16[288,2304]{1,0:T(8,128)(2,1)S(1)}, u32[]{:S(2)}, u32[]{:S(2)}) collective-permute-start(bf16[288,2304]{1,0:T(8,128)(2,1)} %get-tuple-element.122), channel_id=1, source_target_pairs={{0,4},{4,0},{8,12},{12,8},{16,20},{20,16},{24,28},{28,24},{1,5},{5... | collective-permute-start | bytes 3981320 | tf_op jit(solution)/shard_map/ppermute | solution.py:100
  593.3 16.3 %collective-permute-start.55 = (bf16[128,2304]{1,0:T(8,128)(2,1)S(1)}, bf16[128,2304]{1,0:T(8,128)(2,1)S(1)}, u32[]{:S(2)}, u32[]{:S(2)}) collective-permute-start(bf16[128,2304]{1,0:T(8,128)(2,1)S(1)} %collective-permute-done.54), channel_id=1, source_target_pairs={{1,0},{2,1},{5,4},{6,5},{9,8},{10,9},{13,12},{14,13},{17,16},{18,1... | collective-permute-start | bytes 1769480 | tf_op jit(solution)/shard_map/ppermute | solution.py:215
  594.6 16.4 %collective-permute-start.57 = (bf16[128,2304]{1,0:T(8,128)(2,1)}, bf16[128,2304]{1,0:T(8,128)(2,1)S(1)}, u32[]{:S(2)}, u32[]{:S(2)}) collective-permute-start(bf16[128,2304]{1,0:T(8,128)(2,1)} %collective-permute-done.53), channel_id=1, source_target_pairs={{1,2},{2,3},{5,6},{6,7},{9,10},{10,11},{13,14},{14,15},{17,18},{18... | collective-permute-start | bytes 1769480 | tf_op jit(solution)/shard_map/ppermute | solution.py:214
  609.7 15.5 %collective-permute-start.56 = (bf16[128,2304]{1,0:T(8,128)(2,1)S(1)}, bf16[128,2304]{1,0:T(8,128)(2,1)S(1)}, u32[]{:S(2)}, u32[]{:S(2)}) collective-permute-start(bf16[128,2304]{1,0:T(8,128)(2,1)S(1)} %collective-permute-done.55), channel_id=1, source_target_pairs={{1,0},{5,4},{9,8},{13,12},{17,16},{21,20},{25,24},{29,28}} | collective-permute-start | bytes 1769480 | tf_op jit(solution)/shard_map/ppermute | solution.py:215
  611.0 20.2 %collective-permute-start.58 = (bf16[128,2304]{1,0:T(8,128)(2,1)S(1)}, bf16[128,2304]{1,0:T(8,128)(2,1)S(1)}, u32[]{:S(2)}, u32[]{:S(2)}) collective-permute-start(bf16[128,2304]{1,0:T(8,128)(2,1)S(1)} %collective-permute-done.57), channel_id=1, source_target_pairs={{2,3},{6,7},{10,11},{14,15},{18,19},{22,23},{26,27},{30,31}} | collective-permute-start | bytes 1769480 | tf_op jit(solution)/shard_map/ppermute | solution.py:214
  611.8 19.5 %collective-permute-start.47 = (bf16[512,512]{1,0:T(8,128)(2,1)S(1)}, bf16[512,512]{1,0:T(8,128)(2,1)S(1)}, u32[]{:S(2)}, u32[]{:S(2)}) collective-permute-start(bf16[512,512]{1,0:T(8,128)(2,1)S(1)} %get-tuple-element.123), channel_id=1, source_target_pairs={{0,4},{4,0},{8,12},{12,8},{16,20},{20,16},{24,28},{28,24},{1,5},{5... | collective-permute-start | bytes 1572872 | tf_op jit(solution)/shard_map/ppermute | solution.py:100
  612.9 16.5 %collective-permute-start.50 = (bf16[1024,512]{1,0:T(8,128)(2,1)S(1)}, bf16[1024,512]{1,0:T(8,128)(2,1)S(1)}, u32[]{:S(2)}, u32[]{:S(2)}) collective-permute-start(bf16[1024,512]{1,0:T(8,128)(2,1)S(1)} %pad_maximum_fusion.4), channel_id=1, source_target_pairs={{0,16},{4,12},{8,24},{12,4},{16,0},{20,28},{24,8},{28,20},{1,17},{... | collective-permute-start | bytes 3145736 | tf_op jit(solution)/shard_map/ppermute | solution.py:100
  661.8 34.2 %collective-permute-start.62 = (bf16[576,1536]{1,0:T(8,128)(2,1)}, bf16[576,1536]{1,0:T(8,128)(2,1)S(1)}, u32[]{:S(2)}, u32[]{:S(2)}) collective-permute-start(bf16[576,1536]{1,0:T(8,128)(2,1)} %pad_maximum_fusion.3), channel_id=1, source_target_pairs={{0,16},{4,12},{8,24},{12,4},{16,0},{20,28},{24,8},{28,20},{1,17},{... | collective-permute-start | bytes 5308424 | tf_op jit(solution)/shard_map/ppermute | solution.py:100
  662.2 22.5 %collective-permute-start.66 = (f32[8,288]{1,0:T(8,128)S(1)}, f32[8,288]{1,0:T(8,128)S(1)}, u32[]{:S(2)}, u32[]{:S(2)}) collective-permute-start(f32[8,288]{1,0:T(8,128)S(1)} %pad_maximum_fusion.14), channel_id=1, source_target_pairs={{0,16},{4,12},{8,24},{12,4},{16,0},{20,28},{24,8},{28,20},{1,17},{... | collective-permute-start | bytes 27656 | tf_op jit(solution)/shard_map/ppermute | solution.py:538
  664.0 30.4 %collective-permute-start.63 = (bf16[288,1536]{1,0:T(8,128)(2,1)}, bf16[288,1536]{1,0:T(8,128)(2,1)S(1)}, u32[]{:S(2)}, u32[]{:S(2)}) collective-permute-start(bf16[288,1536]{1,0:T(8,128)(2,1)} %get-tuple-element.138), channel_id=1, source_target_pairs={{0,4},{4,0},{8,12},{12,8},{16,20},{20,16},{24,28},{28,24},{1,5},{5... | collective-permute-start | bytes 2654216 | tf_op jit(solution)/shard_map/ppermute | solution.py:100
  (92 other events, 803.1 us)
Sparse Core Ops, SparseCore 0:
  10.5 51.6 all-gather.4
  66.0 123.9 all-gather.6
  213.9 63.5 all-gather.8
  294.6 49.9 reduce-scatter.4
  349.5 49.9 all-gather.10
  466.3 46.0 reduce-scatter.6
  539.7 81.3 reduce-scatter.8
  648.8 48.0 reduce-scatter.10
